TPU v7x, 32 devices: a whole 2x2x4 slice. The times are simulated.
32 devices in a mesh: dp: 8 (over z, y), mp: 4 (over x, core).
Axes of the slice: x: 2, y: 2, z: 4, core: 2. Of those that a mesh axis runs over, the one named last changes fastest.
Arguments:
- embedded_symbols: bfloat16 [4, 8192, 768], P('mp', 'dp'), may hold values from -6 to 6
- stream_opening_marker: int32 [4, 64], P('mp'), may hold values from 0 to 1, as said below
- retained_tile_selector: int32 [2, 4, 64, 15], P(None, 'mp', 'dp'), may hold values 0 or 1
- asker_projection: bfloat16 [2, 768, 768], P(None, ('dp', 'mp')), may hold values from -0.21875 to 0.21875
- lookup_projection: bfloat16 [2, 768, 768], P(None, ('dp', 'mp')), may hold values from -0.21875 to 0.21875
- content_projection: bfloat16 [2, 768, 768], P(None, ('dp', 'mp')), may hold values from -0.21875 to 0.21875
- mixer_result_projection: bfloat16 [2, 768, 768], P(None, ('dp', 'mp')), may hold values from -3.5 to 3.5
- asker_offset: bfloat16 [2, 768], P(None, ('dp', 'mp')), may hold values from -3 to 3
- content_offset: bfloat16 [2, 768], P(None, ('dp', 'mp')), may hold values from -3 to 3
- mixer_result_offset: bfloat16 [2, 768], P(None, ('dp', 'mp')), may hold values from -3 to 3
- mixer_standardise_scaling: bfloat16 [2, 768], P(None, ('dp', 'mp')), may hold values from 0.5 to 1.5
- mixer_standardise_offset: bfloat16 [2, 768], P(None, ('dp', 'mp')), may hold values from -2 to 2
- perceptron_widen_projection: bfloat16 [2, 768, 3072], P(None, ('dp', 'mp')), may hold values from -0.21875 to 0.21875
- perceptron_widen_offset: bfloat16 [2, 3072], P(None, ('dp', 'mp')), may hold values from -3 to 3
- perceptron_narrow_projection: bfloat16 [2, 3072, 768], P(None, ('dp', 'mp')), may hold values from -0.21875 to 0.21875
- perceptron_narrow_offset: bfloat16 [2, 768], P(None, ('dp', 'mp')), may hold values from -3 to 3
- perceptron_standardise_scaling: bfloat16 [2, 768], P(None, ('dp', 'mp')), may hold values from 0.5 to 1.5
- perceptron_standardise_offset: bfloat16 [2, 768], P(None, ('dp', 'mp')), may hold values from -2 to 2
- tile_gate_scores: bfloat16 [2, 768], P(None, ('dp', 'mp')), may hold values from -6 to 6
- tile_gate_jitter: bfloat16 [2, 768], P(None, ('dp', 'mp')), may hold values from -4 to 4
- relaxing_warmth: float32 [2, 12], replicated, may hold values from 0.5 to 2
- upstream_derivative: bfloat16 [4, 8192, 768], P('mp', 'dp'), may hold values from -6 to 6
Outputs:
- result: float32 [4, 8192, 768], P('mp', 'dp')
- tokens_grad: float32 [4, 8192, 768], P('mp', 'dp')
- query_proj_grad: float32 [2, 768, 768], P(None, ('dp', 'mp'))
- key_proj_grad: float32 [2, 768, 768], P(None, ('dp', 'mp'))
- value_proj_grad: float32 [2, 768, 768], P(None, ('dp', 'mp'))
- output_proj_grad: float32 [2, 768, 768], P(None, ('dp', 'mp'))
- query_bias_grad: float32 [2, 768], P(None, ('dp', 'mp'))
- value_bias_grad: float32 [2, 768], P(None, ('dp', 'mp'))
- output_bias_grad: float32 [2, 768], P(None, ('dp', 'mp'))
- first_gain_grad: float32 [2, 768], P(None, ('dp', 'mp'))
- first_shift_grad: float32 [2, 768], P(None, ('dp', 'mp'))
- inner_proj_grad: float32 [2, 768, 3072], P(None, ('dp', 'mp'))
- inner_bias_grad: float32 [2, 3072], P(None, ('dp', 'mp'))
- outer_proj_grad: float32 [2, 3072, 768], P(None, ('dp', 'mp'))
- outer_bias_grad: float32 [2, 768], P(None, ('dp', 'mp'))
- second_gain_grad: float32 [2, 768], P(None, ('dp', 'mp'))
- second_shift_grad: float32 [2, 768], P(None, ('dp', 'mp'))
- mask_logit_grad: float32 [2, 768], P(None, ('dp', 'mp'))
- new_mask: int32 [2, 768], P(None, ('dp', 'mp'))
Inputs may be any that keep to these rules, and one draw needn't show every extreme that they name: `stream_opening_marker`: block 0 of each column begins a sequence; every sequence lies on one device along dp or on two neighbouring ones, with at most 4 blocks on any one device and so at most 8 blocks; every boundary between neighbouring devices along dp falls inside a sequence; in each column one sequence has exactly 8 blocks.
All inputs are finite; a program needn't handle non-finite values. No bound on the sum of `retained_tile_selector` on one device may be relied on, other than what follows from the above.
Results may differ from a plain program's by a relative error of at most 0.025.
Values may be sent and summed in bfloat16 or wider, within the bound.
No kernel may reach another device: no remote copies, remote signals or barrier semaphores. Data moves between devices by JAX's collectives and lax.ppermute only.
A program may use at most 320 MiB of HBM per device.

v0:
```python
import jax
import jax.numpy as jnp
from jax import lax
from jax.sharding import PartitionSpec as P

D = 768
ATTENDER_TOTAL = 12
HD = 64
BLK = 128
MAX_SPAN_TILES = 8
RIM = 4


def extended_2(cells, sides, width):
    for axis, dim in sides:
        count = lax.axis_size(axis)
        ends = count - 1
        head = lax.slice_in_dim(cells, 0, width, axis=dim)
        tail = lax.slice_in_dim(cells, cells.shape[dim] - width, cells.shape[dim], axis=dim)
        cells = jnp.concatenate(
            [
                lax.ppermute(tail, axis, [(i, (i + 1) % count) for i in range(ends)]),
                cells,
                lax.ppermute(head, axis, [((i + 1) % count, i) for i in range(ends)]),
            ],
            axis=dim,
        )
    return cells


def passed_along(block, axis, distance):
    devices = range(lax.axis_size(axis))
    route = [(i - distance, i) for i in devices if i - distance in devices]
    return lax.ppermute(block, axis, route)


def norm_rows(values, gain, shift):
    middle = jnp.mean(values, -1, keepdims=True)
    centred = values - middle
    spread = jnp.mean(centred * centred, -1, keepdims=True)
    return centred * lax.rsqrt(spread + 1e-06) * gain + shift


def gelu_exact(values):
    return jax.nn.gelu(values, approximate=False)


def table_pick(table, index):
    slots = jnp.arange(table.shape[0], dtype=jnp.int32)
    return jnp.sum(jnp.where(index[:, None] == slots[None, :], table[None, :], 0), axis=1)


def one_hot(index, count):
    return (index[:, None] == jnp.arange(count, dtype=jnp.int32)[None, :]).astype(jnp.float32)


def contract_rows(left, right):
    return lax.dot_general(
        left, right, (((0,), (0,)), ((), ())), preferred_element_type=jnp.float32
    )


def contract_cols(left, right):
    return lax.dot_general(
        left, right, (((1,), (1,)), ((), ())), preferred_element_type=jnp.float32
    )


def head_columns(values, head):
    return lax.dynamic_slice_in_dim(values, head * HD, HD, 1)


def block_layouts(start_flags, keep_rows, block_position, blocks, smooth_tile_selector):
    total = start_flags.shape[0]
    order = jnp.arange(total, dtype=jnp.int32)
    seq_of = jnp.cumsum(start_flags) - 1
    start_of = lax.cummax(jnp.where(start_flags == 1, order, 0), axis=0)
    window = keep_rows.shape[1]
    layouts = []
    for group in range(blocks // 4):
        query_ids = block_position * blocks + group * 4 + jnp.arange(4, dtype=jnp.int32)
        key_ids = (
            block_position * blocks - RIM + group * 4 + jnp.arange(4 + 2 * RIM, dtype=jnp.int32)
        )
        valid = (key_ids >= 0) & (key_ids < total)
        seq_query = table_pick(seq_of, query_ids)
        seq_key = jnp.where(valid, table_pick(seq_of, key_ids), -1)
        pick_query = one_hot(query_ids - table_pick(start_of, query_ids), MAX_SPAN_TILES)
        pick_key = one_hot(key_ids - table_pick(start_of, key_ids), MAX_SPAN_TILES)
        offset = key_ids[None, :] - query_ids[:, None]
        rows = keep_rows[group * 4 : group * 4 + 4]
        chosen_elements = jnp.sum(
            jnp.where(
                offset[:, :, None] + MAX_SPAN_TILES - 1 == jnp.arange(window)[None, None, :],
                rows[:, None, :],
                0,
            ),
            axis=2,
        )
        kept = (seq_query[:, None] == seq_key[None, :]) & ((chosen_elements > 0) | (offset == 0))
        factors = jnp.einsum(
            "ia,hab,jb->hij",
            pick_query,
            smooth_tile_selector,
            pick_key,
            precision=lax.Precision.HIGHEST,
        )
        layouts.append((kept, factors, pick_query, pick_key))
    return layouts


def head_scores(query_rows, key_rows, kept, head):
    count_query, count_key = kept.shape
    scores = contract_cols(head_columns(query_rows, head), head_columns(key_rows, head)) * HD ** (
        -0.5
    )
    scores = scores.reshape(count_query, BLK, count_key, BLK)
    return jnp.where(kept[:, None, :, None], scores, -1e30)


def forward_group(query_rows, key_rows, value_rows, kept, factors):
    count_query, count_key = kept.shape
    masked = kept[:, None, :, None]

    def forward_one_head(head):
        scores = head_scores(query_rows, key_rows, kept, head)
        largest = jnp.max(scores, axis=(2, 3), keepdims=True)
        expo = jnp.where(masked, jnp.exp(scores - largest), 0.0)
        total = jnp.sum(expo, axis=(2, 3), keepdims=True)
        factor = lax.dynamic_index_in_dim(factors, head, 0, keepdims=False)[:, None, :, None]
        weights = (
            (expo / total * factor).astype(jnp.bfloat16).reshape(count_query * BLK, count_key * BLK)
        )
        context = jnp.dot(
            weights, head_columns(value_rows, head), preferred_element_type=jnp.float32
        )
        return (context, (largest + jnp.log(total)).reshape(count_query * BLK))

    context, logsum = lax.map(forward_one_head, jnp.arange(ATTENDER_TOTAL))
    return (
        jnp.transpose(context, (1, 0, 2)).reshape(count_query * BLK, ATTENDER_TOTAL * HD),
        logsum,
    )


def backward_group(query_rows, key_rows, value_rows, kept, factors, logsum, dcontext):
    count_query, count_key = kept.shape
    masked = kept[:, None, :, None]

    def backward_one_head(head):
        scores = head_scores(query_rows, key_rows, kept, head)
        level = lax.dynamic_index_in_dim(logsum, head, 0, keepdims=False).reshape(
            count_query, BLK, 1, 1
        )
        probs = jnp.where(masked, jnp.exp(scores - level), 0.0)
        factor = lax.dynamic_index_in_dim(factors, head, 0, keepdims=False)[:, None, :, None]
        weights = (probs * factor).astype(jnp.bfloat16).reshape(count_query * BLK, count_key * BLK)
        dcontext_part = head_columns(dcontext, head)
        dweights = contract_cols(dcontext_part, head_columns(value_rows, head)).reshape(
            count_query, BLK, count_key, BLK
        )
        dvalue = contract_rows(weights, dcontext_part)
        dprobs = dweights * factor
        inner = jnp.sum(probs * dprobs, axis=(2, 3), keepdims=True)
        dscores = (
            (probs * (dprobs - inner))
            .astype(jnp.bfloat16)
            .reshape(count_query * BLK, count_key * BLK)
        )
        dquery = jnp.dot(
            dscores, head_columns(key_rows, head), preferred_element_type=jnp.float32
        ) * HD ** (-0.5)
        dkey = contract_rows(dscores, head_columns(query_rows, head)) * HD ** (-0.5)
        dfactor = jnp.sum(probs * dweights, axis=(1, 3))
        return (dquery, dkey, dvalue, dfactor)

    dquery, dkey, dvalue, dfactor = lax.map(backward_one_head, jnp.arange(ATTENDER_TOTAL))
    rows_query = count_query * BLK
    rows_key = count_key * BLK
    return (
        jnp.transpose(dquery, (1, 0, 2)).reshape(rows_query, ATTENDER_TOTAL * HD),
        jnp.transpose(dkey, (1, 0, 2)).reshape(rows_key, ATTENDER_TOTAL * HD),
        jnp.transpose(dvalue, (1, 0, 2)).reshape(rows_key, ATTENDER_TOTAL * HD),
        dfactor,
    )


def gather_layer(params, score_jitter, tier_evaluate):
    (
        asker_projection,
        lookup_projection,
        content_projection,
        mixer_result_projection,
        asker_offset,
        content_offset,
        mixer_result_offset,
        mixer_standardise_scaling,
        mixer_standardise_offset,
        perceptron_widen_projection,
        perceptron_widen_offset,
        perceptron_narrow_projection,
        perceptron_narrow_offset,
        perceptron_standardise_scaling,
        perceptron_standardise_offset,
        tile_gate_scores,
    ) = params
    return (
        lax.all_gather(asker_projection[tier_evaluate], ("dp", "mp"), axis=0, tiled=True),
        lax.all_gather(lookup_projection[tier_evaluate], ("dp", "mp"), axis=0, tiled=True),
        lax.all_gather(content_projection[tier_evaluate], ("dp", "mp"), axis=0, tiled=True),
        lax.all_gather(mixer_result_projection[tier_evaluate], ("dp", "mp"), axis=0, tiled=True),
        lax.all_gather(asker_offset[tier_evaluate], ("dp", "mp"), axis=0, tiled=True),
        lax.all_gather(content_offset[tier_evaluate], ("dp", "mp"), axis=0, tiled=True),
        lax.all_gather(mixer_result_offset[tier_evaluate], ("dp", "mp"), axis=0, tiled=True),
        lax.all_gather(mixer_standardise_scaling[tier_evaluate], ("dp", "mp"), axis=0, tiled=True),
        lax.all_gather(mixer_standardise_offset[tier_evaluate], ("dp", "mp"), axis=0, tiled=True),
        lax.all_gather(
            perceptron_widen_projection[tier_evaluate], ("dp", "mp"), axis=0, tiled=True
        ),
        lax.all_gather(perceptron_widen_offset[tier_evaluate], ("dp", "mp"), axis=0, tiled=True),
        lax.all_gather(
            perceptron_narrow_projection[tier_evaluate], ("dp", "mp"), axis=0, tiled=True
        ),
        lax.all_gather(perceptron_narrow_offset[tier_evaluate], ("dp", "mp"), axis=0, tiled=True),
        lax.all_gather(
            perceptron_standardise_scaling[tier_evaluate], ("dp", "mp"), axis=0, tiled=True
        ),
        lax.all_gather(
            perceptron_standardise_offset[tier_evaluate], ("dp", "mp"), axis=0, tiled=True
        ),
        lax.all_gather(tile_gate_scores[tier_evaluate], ("dp", "mp"), axis=0, tiled=True),
        lax.all_gather(score_jitter[tier_evaluate], ("dp", "mp"), axis=0, tiled=True),
    )


def gather_again(params, score_jitter, tier_evaluate):
    (
        asker_projection,
        lookup_projection,
        content_projection,
        mixer_result_projection,
        asker_offset,
        content_offset,
        mixer_result_offset,
        mixer_standardise_scaling,
        mixer_standardise_offset,
        perceptron_widen_projection,
        perceptron_widen_offset,
        perceptron_narrow_projection,
        perceptron_narrow_offset,
        perceptron_standardise_scaling,
        perceptron_standardise_offset,
        tile_gate_scores,
    ) = params
    return (
        lax.all_gather(asker_projection[tier_evaluate], ("dp", "mp"), axis=0, tiled=True),
        lax.all_gather(lookup_projection[tier_evaluate], ("dp", "mp"), axis=0, tiled=True),
        lax.all_gather(content_projection[tier_evaluate], ("dp", "mp"), axis=0, tiled=True),
        lax.all_gather(mixer_result_projection[tier_evaluate], ("dp", "mp"), axis=0, tiled=True),
        lax.all_gather(asker_offset[tier_evaluate], ("dp", "mp"), axis=0, tiled=True),
        lax.all_gather(content_offset[tier_evaluate], ("dp", "mp"), axis=0, tiled=True),
        lax.all_gather(mixer_result_offset[tier_evaluate], ("dp", "mp"), axis=0, tiled=True),
        lax.all_gather(mixer_standardise_scaling[tier_evaluate], ("dp", "mp"), axis=0, tiled=True),
        lax.all_gather(mixer_standardise_offset[tier_evaluate], ("dp", "mp"), axis=0, tiled=True),
        lax.all_gather(
            perceptron_widen_projection[tier_evaluate], ("dp", "mp"), axis=0, tiled=True
        ),
        lax.all_gather(perceptron_widen_offset[tier_evaluate], ("dp", "mp"), axis=0, tiled=True),
        lax.all_gather(
            perceptron_narrow_projection[tier_evaluate], ("dp", "mp"), axis=0, tiled=True
        ),
        lax.all_gather(perceptron_narrow_offset[tier_evaluate], ("dp", "mp"), axis=0, tiled=True),
        lax.all_gather(
            perceptron_standardise_scaling[tier_evaluate], ("dp", "mp"), axis=0, tiled=True
        ),
        lax.all_gather(
            perceptron_standardise_offset[tier_evaluate], ("dp", "mp"), axis=0, tiled=True
        ),
        lax.all_gather(tile_gate_scores[tier_evaluate], ("dp", "mp"), axis=0, tiled=True),
        lax.all_gather(score_jitter[tier_evaluate], ("dp", "mp"), axis=0, tiled=True),
    )


def layer_forward(hidden_state, collected_rows, start_flags, keep_rows, temper, block_position):
    (
        query_w,
        key_w,
        value_w,
        output_w,
        query_b,
        value_b,
        output_b,
        gain_one,
        shift_one,
        inner_w,
        inner_b,
        outer_w,
        outer_b,
        gain_two,
        shift_two,
        logits,
        score_jitter,
    ) = collected_rows
    rows = hidden_state.shape[0]
    blocks = rows // BLK
    smooth_tile_selector = jax.nn.sigmoid(
        (logits.astype(jnp.float32) + score_jitter.astype(jnp.float32)).reshape(
            ATTENDER_TOTAL, MAX_SPAN_TILES, MAX_SPAN_TILES
        )
        / temper[:, None, None]
    )
    hidden_low = hidden_state.astype(jnp.bfloat16)
    queries = (
        jnp.dot(hidden_low, query_w, preferred_element_type=jnp.float32)
        + query_b.astype(jnp.float32)
    ).astype(jnp.bfloat16)
    keys = jnp.dot(hidden_low, key_w, preferred_element_type=jnp.float32).astype(jnp.bfloat16)
    values = (
        jnp.dot(hidden_low, value_w, preferred_element_type=jnp.float32)
        + value_b.astype(jnp.float32)
    ).astype(jnp.bfloat16)
    extended = extended_2(jnp.concatenate([keys, values], 1), (("dp", 0),), RIM * BLK)
    layouts = block_layouts(start_flags, keep_rows, block_position, blocks, smooth_tile_selector)
    contexts = []
    logsums = []
    for group in range(blocks // 4):
        kept, factors, pick_query, pick_key = layouts[group]
        query_rows = queries[group * 4 * BLK : (group * 4 + 4) * BLK]
        key_rows = extended[group * 4 * BLK : (group * 4 + 4 + 2 * RIM) * BLK]
        context, logsum = forward_group(query_rows, key_rows[:, :D], key_rows[:, D:], kept, factors)
        contexts.append(context)
        logsums.append(logsum)
    context_low = jnp.concatenate(contexts, 0).astype(jnp.bfloat16)
    attended = jnp.dot(context_low, output_w, preferred_element_type=jnp.float32) + output_b.astype(
        jnp.float32
    )
    first_sum = hidden_state + attended
    normed = norm_rows(first_sum, gain_one.astype(jnp.float32), shift_one.astype(jnp.float32))
    normed_low = normed.astype(jnp.bfloat16)
    inner = jnp.dot(normed_low, inner_w, preferred_element_type=jnp.float32) + inner_b.astype(
        jnp.float32
    )
    active_low = gelu_exact(inner).astype(jnp.bfloat16)
    outer = jnp.dot(active_low, outer_w, preferred_element_type=jnp.float32) + outer_b.astype(
        jnp.float32
    )
    second_sum = normed + outer
    result = norm_rows(second_sum, gain_two.astype(jnp.float32), shift_two.astype(jnp.float32))
    record = (
        hidden_low,
        queries,
        extended,
        context_low,
        logsums,
        first_sum,
        normed_low,
        inner,
        active_low,
        second_sum,
        layouts,
        smooth_tile_selector,
    )
    return (result, record)


def layer_gradient_pass(incoming_gradient, collected_rows, record, temper):
    (
        query_w,
        key_w,
        value_w,
        output_w,
        query_b,
        value_b,
        output_b,
        gain_one,
        shift_one,
        inner_w,
        inner_b,
        outer_w,
        outer_b,
        gain_two,
        shift_two,
        logits,
        score_jitter,
    ) = collected_rows
    (
        hidden_low,
        queries,
        extended,
        context_low,
        logsums,
        first_sum,
        normed_low,
        inner,
        active_low,
        second_sum,
        layouts,
        smooth_tile_selector,
    ) = record
    rows = queries.shape[0]
    rim = RIM * BLK
    unused, pull_two = jax.vjp(
        norm_rows, second_sum, gain_two.astype(jnp.float32), shift_two.astype(jnp.float32)
    )
    dsecond, gain_second, shift_second = pull_two(incoming_gradient)
    douter = dsecond.astype(jnp.bfloat16)
    grad_outer = contract_rows(active_low, douter)
    bias_outer = jnp.sum(douter.astype(jnp.float32), 0)
    dactive = contract_cols(douter, outer_w)
    unused, pull_gelu = jax.vjp(gelu_exact, inner)
    dinner = pull_gelu(dactive)[0].astype(jnp.bfloat16)
    grad_inner = contract_rows(normed_low, dinner)
    bias_inner = jnp.sum(dinner.astype(jnp.float32), 0)
    dnormed = dsecond + contract_cols(dinner, inner_w)
    unused, pull_one = jax.vjp(
        norm_rows, first_sum, gain_one.astype(jnp.float32), shift_one.astype(jnp.float32)
    )
    dfirst, gain_first, shift_first = pull_one(dnormed)
    dattend = dfirst.astype(jnp.bfloat16)
    grad_output = contract_rows(context_low, dattend)
    bias_output = jnp.sum(dattend.astype(jnp.float32), 0)
    dcontext = contract_cols(dattend, output_w).astype(jnp.bfloat16)
    dextended = jnp.zeros((extended.shape[0], 2 * D), jnp.float32)
    dscale = jnp.zeros((ATTENDER_TOTAL, MAX_SPAN_TILES, MAX_SPAN_TILES), jnp.float32)
    dquery_parts = []
    for group in range(len(layouts)):
        kept, factors, pick_query, pick_key = layouts[group]
        lower = group * 4 * BLK
        upper = (group * 4 + 4 + 2 * RIM) * BLK
        query_rows = queries[group * 4 * BLK : (group * 4 + 4) * BLK]
        key_rows = extended[lower:upper]
        dquery, dkey, dvalue, dfactor = backward_group(
            query_rows,
            key_rows[:, :D],
            key_rows[:, D:],
            kept,
            factors,
            logsums[group],
            dcontext[group * 4 * BLK : (group * 4 + 4) * BLK],
        )
        dquery_parts.append(dquery)
        dextended = dextended.at[lower:upper].add(jnp.concatenate([dkey, dvalue], 1))
        dscale = dscale + jnp.einsum(
            "ia,hij,jb->hab", pick_query, dfactor, pick_key, precision=lax.Precision.HIGHEST
        )
    from_upper = passed_along(dextended[:rim].astype(jnp.bfloat16), "dp", -1).astype(jnp.float32)
    from_lower = passed_along(dextended[rows + rim :].astype(jnp.bfloat16), "dp", 1).astype(
        jnp.float32
    )
    downed = dextended[rim : rim + rows]
    downed = downed.at[:rim].add(from_lower)
    downed = downed.at[rows - rim :].add(from_upper)
    dquery_low = jnp.concatenate(dquery_parts, 0).astype(jnp.bfloat16)
    dkeys_low = downed[:, :D].astype(jnp.bfloat16)
    dvalues_low = downed[:, D:].astype(jnp.bfloat16)
    grad_query = contract_rows(hidden_low, dquery_low)
    bias_query = jnp.sum(dquery_low.astype(jnp.float32), 0)
    grad_key = contract_rows(hidden_low, dkeys_low)
    grad_value = contract_rows(hidden_low, dvalues_low)
    bias_value = jnp.sum(dvalues_low.astype(jnp.float32), 0)
    dhidden = (
        dfirst
        + contract_cols(dquery_low, query_w)
        + contract_cols(dkeys_low, key_w)
        + contract_cols(dvalues_low, value_w)
    )
    grad_logit = (
        dscale * smooth_tile_selector * (1.0 - smooth_tile_selector) / temper[:, None, None]
    ).reshape(ATTENDER_TOTAL * MAX_SPAN_TILES * MAX_SPAN_TILES)
    layer_quantities = (
        grad_query,
        grad_key,
        grad_value,
        grad_output,
        bias_query,
        bias_value,
        bias_output,
        gain_first,
        shift_first,
        grad_inner,
        bias_inner,
        grad_outer,
        bias_outer,
        gain_second,
        shift_second,
        grad_logit,
    )
    return (dhidden, layer_quantities)


def scatter_each(layer_quantities):
    (
        grad_query,
        grad_key,
        grad_value,
        grad_output,
        bias_query,
        bias_value,
        bias_output,
        gain_first,
        shift_first,
        grad_inner,
        bias_inner,
        grad_outer,
        bias_outer,
        gain_second,
        shift_second,
        grad_logit,
    ) = layer_quantities
    return (
        lax.psum_scatter(grad_query, ("dp", "mp"), scatter_dimension=0, tiled=True),
        lax.psum_scatter(grad_key, ("dp", "mp"), scatter_dimension=0, tiled=True),
        lax.psum_scatter(grad_value, ("dp", "mp"), scatter_dimension=0, tiled=True),
        lax.psum_scatter(grad_output, ("dp", "mp"), scatter_dimension=0, tiled=True),
        lax.psum_scatter(bias_query, ("dp", "mp"), scatter_dimension=0, tiled=True),
        lax.psum_scatter(bias_value, ("dp", "mp"), scatter_dimension=0, tiled=True),
        lax.psum_scatter(bias_output, ("dp", "mp"), scatter_dimension=0, tiled=True),
        lax.psum_scatter(gain_first, ("dp", "mp"), scatter_dimension=0, tiled=True),
        lax.psum_scatter(shift_first, ("dp", "mp"), scatter_dimension=0, tiled=True),
        lax.psum_scatter(grad_inner, ("dp", "mp"), scatter_dimension=0, tiled=True),
        lax.psum_scatter(bias_inner, ("dp", "mp"), scatter_dimension=0, tiled=True),
        lax.psum_scatter(grad_outer, ("dp", "mp"), scatter_dimension=0, tiled=True),
        lax.psum_scatter(bias_outer, ("dp", "mp"), scatter_dimension=0, tiled=True),
        lax.psum_scatter(gain_second, ("dp", "mp"), scatter_dimension=0, tiled=True),
        lax.psum_scatter(shift_second, ("dp", "mp"), scatter_dimension=0, tiled=True),
        lax.psum_scatter(grad_logit, ("dp", "mp"), scatter_dimension=0, tiled=True),
    )


def per_device(
    embedded_symbols,
    stream_opening_marker,
    retained_tile_selector,
    asker_projection,
    lookup_projection,
    content_projection,
    mixer_result_projection,
    asker_offset,
    content_offset,
    mixer_result_offset,
    mixer_standardise_scaling,
    mixer_standardise_offset,
    perceptron_widen_projection,
    perceptron_widen_offset,
    perceptron_narrow_projection,
    perceptron_narrow_offset,
    perceptron_standardise_scaling,
    perceptron_standardise_offset,
    tile_gate_scores,
    tile_gate_jitter,
    relaxing_warmth,
    upstream_derivative,
):
    params = (
        asker_projection,
        lookup_projection,
        content_projection,
        mixer_result_projection,
        asker_offset,
        content_offset,
        mixer_result_offset,
        mixer_standardise_scaling,
        mixer_standardise_offset,
        perceptron_widen_projection,
        perceptron_widen_offset,
        perceptron_narrow_projection,
        perceptron_narrow_offset,
        perceptron_standardise_scaling,
        perceptron_standardise_offset,
        tile_gate_scores,
    )
    start_flags = stream_opening_marker[0]
    block_position = lax.axis_index("dp")
    hidden_state = embedded_symbols[0].astype(jnp.float32)
    saved_residuals = []
    held = []
    for tier_evaluate in range(2):
        collected_rows = gather_layer(params, tile_gate_jitter, tier_evaluate)
        hidden_state, record = layer_forward(
            hidden_state,
            collected_rows,
            start_flags,
            retained_tile_selector[tier_evaluate, 0],
            relaxing_warmth[tier_evaluate],
            block_position,
        )
        saved_residuals.append(record)
        held.append(collected_rows)
    incoming_gradient = upstream_derivative[0].astype(jnp.float32)
    layer_terms = [None, None]
    for tier_evaluate in (1, 0):
        collected_rows = gather_again(params, tile_gate_jitter, tier_evaluate)
        incoming_gradient, layer_quantities = layer_gradient_pass(
            incoming_gradient,
            collected_rows,
            saved_residuals[tier_evaluate],
            relaxing_warmth[tier_evaluate],
        )
        layer_terms[tier_evaluate] = scatter_each(layer_quantities)
    stacked = tuple(
        (jnp.stack([layer_terms[0][index], layer_terms[1][index]]) for index in range(16))
    )
    new_mask = (
        tile_gate_scores.astype(jnp.float32) + tile_gate_jitter.astype(jnp.float32) > 0
    ).astype(jnp.int32)
    return (hidden_state[None], incoming_gradient[None]) + tuple(stacked) + (new_mask,)


def solution(mesh):
    return jax.shard_map(
        per_device,
        mesh=mesh,
        in_specs=(
            P("mp", "dp", None),
            P("mp", None),
            P(None, "mp", "dp", None),
            P(None, ("dp", "mp"), None),
            P(None, ("dp", "mp"), None),
            P(None, ("dp", "mp"), None),
            P(None, ("dp", "mp"), None),
            P(None, ("dp", "mp")),
            P(None, ("dp", "mp")),
            P(None, ("dp", "mp")),
            P(None, ("dp", "mp")),
            P(None, ("dp", "mp")),
            P(None, ("dp", "mp"), None),
            P(None, ("dp", "mp")),
            P(None, ("dp", "mp"), None),
            P(None, ("dp", "mp")),
            P(None, ("dp", "mp")),
            P(None, ("dp", "mp")),
            P(None, ("dp", "mp")),
            P(None, ("dp", "mp")),
            P(),
            P("mp", "dp", None),
        ),
        out_specs=(
            P("mp", "dp", None),
            P("mp", "dp", None),
            P(None, ("dp", "mp"), None),
            P(None, ("dp", "mp"), None),
            P(None, ("dp", "mp"), None),
            P(None, ("dp", "mp"), None),
            P(None, ("dp", "mp")),
            P(None, ("dp", "mp")),
            P(None, ("dp", "mp")),
            P(None, ("dp", "mp")),
            P(None, ("dp", "mp")),
            P(None, ("dp", "mp"), None),
            P(None, ("dp", "mp")),
            P(None, ("dp", "mp"), None),
            P(None, ("dp", "mp")),
            P(None, ("dp", "mp")),
            P(None, ("dp", "mp")),
            P(None, ("dp", "mp")),
            P(None, ("dp", "mp")),
        ),
        check_vma=False,
    )
```

profile of v0, /device:TPU:0, one launch (start us, length us, event | category | flops | bytes accessed | tf_op | source)
XLA Modules:
  0.0 5709.2 jit_solution(17861450761621060978)
XLA Ops:
  143.0 57.3 %all-gather.47.cloned.1.call-done = bf16[1,768,768]{2,1,0:T(8,128)(2,1)} async-done(((bf16[1,24,768]{2,1,0:T(8,128)(2,1)}), bf16[1,768,768]{2,1,0:T(8,128)(2,1)}) %all-gather.47.cloned.1.call-update) | async-done | bytes 1179664 | tf_op jit(solution)/shard_map/all_gather | solution.py:208
  230.8 250.3 %while.120 = (s32[]{:T(128)}, bf16[12,512,64]{1,2,0:T(8,128)(2,1)}, f32[12,512]{1,0:T(8,128)S(1)}, pred[4,1,12,1]{2,0,3,1:T(4,128)(4,1)S(1)}, pred[4,12]{0,1:T(8...) while((s32[]{:T(128)}, bf16[12,512,64]{1,2,0:T(8,128)(2,1)}, ...), condition=%wide.region_10.11_spmd, body=%wide.region_7.10_spmd.sunk | while | flops 209976832 | bytes 42752912 | solution.py:139
  489.1 250.0 %while.121 = (s32[]{:T(128)}, bf16[12,512,64]{1,2,0:T(8,128)(2,1)}, f32[12,512]{1,0:T(8,128)S(1)}, pred[4,1,12,1]{2,0,3,1:T(4,128)(4,1)S(1)}, pred[4,12]{0,1:T(8...) while((s32[]{:T(128)}, bf16[12,512,64]{1,2,0:T(8,128)(2,1)}, ...), condition=%wide.region_19.20_spmd, body=%wide.region_16.19_spmd.sunk | while | flops 209976832 | bytes 42752912 | solution.py:139
  821.3 52.4 collective-permute-done.2
  899.3 250.3 %while.122 = (s32[]{:T(128)}, bf16[12,512,64]{1,2,0:T(8,128)(2,1)}, f32[12,512]{1,0:T(8,128)S(1)}, pred[4,1,12,1]{2,0,3,1:T(4,128)(4,1)S(1)}, pred[4,12]{0,1:T(8...) while((s32[]{:T(128)}, bf16[12,512,64]{1,2,0:T(8,128)(2,1)}, ...), condition=%wide.region_28.29_spmd, body=%wide.region_25.28_spmd.sunk | while | flops 209976832 | bytes 42752912 | solution.py:139
  1161.5 251.4 %while.123 = (s32[]{:T(128)}, bf16[12,512,64]{1,2,0:T(8,128)(2,1)}, f32[12,512]{1,0:T(8,128)S(1)}, pred[4,1,12,1]{2,0,3,1:T(4,128)(4,1)S(1)}, pred[4,12]{0,1:T(8...) while((s32[]{:T(128)}, bf16[12,512,64]{1,2,0:T(8,128)(2,1)}, ...), condition=%wide.region_33.34_spmd, body=%wide.region_30.33_spmd.sunk | while | flops 209976832 | bytes 42752912 | solution.py:139
  1514.1 605.9 %while.125 = (s32[]{:T(128)}, bf16[12,512,64]{1,2,0:T(8,128)(2,1)}, f32[12,1536,64]{1,2,0:T(8,128)}, f32[12,1536,64]{1,2,0:T(8,128)}, f32[12,4,12]{2,0,1:T(8,128...) while((s32[]{:T(128)}, bf16[12,512,64]{1,2,0:T(8,128)(2,1)}, ...), condition=%wide.region_49.50_spmd, body=%wide.region_46.49_spmd.sunk | while | flops 521534912 | bytes 152066256 | solution.py:177
  2126.4 605.5 %while.124 = (s32[]{:T(128)}, bf16[12,512,64]{1,2,0:T(8,128)(2,1)}, f32[12,1536,64]{1,2,0:T(8,128)}, f32[12,1536,64]{1,2,0:T(8,128)}, f32[12,4,12]{2,0,1:T(8,128...) while((s32[]{:T(128)}, bf16[12,512,64]{1,2,0:T(8,128)(2,1)}, ...), condition=%wide.region_45.46_spmd, body=%wide.region_42.45_spmd.sunk | while | flops 521534912 | bytes 145774736 | solution.py:177
  2779.9 51.9 collective-permute-done.4
  2896.6 607.1 %while.127 = (s32[]{:T(128)}, bf16[12,512,64]{1,2,0:T(8,128)(2,1)}, f32[12,1536,64]{1,2,0:T(8,128)}, f32[12,1536,64]{1,2,0:T(8,128)}, f32[12,4,12]{2,0,1:T(8,128...) while((s32[]{:T(128)}, bf16[12,512,64]{1,2,0:T(8,128)(2,1)}, ...), condition=%wide.region_61.62_spmd, body=%wide.region_58.61_spmd.sunk | while | flops 521534912 | bytes 152066256 | solution.py:177
  3510.3 606.3 %while.126 = (s32[]{:T(128)}, bf16[12,512,64]{1,2,0:T(8,128)(2,1)}, f32[12,1536,64]{1,2,0:T(8,128)}, f32[12,1536,64]{1,2,0:T(8,128)}, f32[12,4,12]{2,0,1:T(8,128...) while((s32[]{:T(128)}, bf16[12,512,64]{1,2,0:T(8,128)(2,1)}, ...), condition=%wide.region_57.58_spmd, body=%wide.region_54.57_spmd.sunk | while | flops 521534912 | bytes 145774736 | solution.py:177
  4164.1 48.9 collective-permute-done.6
  4336.7 71.2 %all-reduce.50.cloned.1.call-done = (f32[768]{0:T(1024)}, f32[768]{0:T(1024)}, f32[768]{0:T(1024)}, f32[768]{0:T(1024)}, f32[768]{0:T(1024)}, /*index=5*/f32[768...) async-done(((f32[768]{0:T(1024)}, f32[768]{0:T(1024)}, ...) | async-done | bytes 79888
  4428.7 85.9 %reduce-scatter.47.cloned.1.call-done = f32[24,768]{1,0:T(8,128)} async-done(((f32[768,768]{1,0:T(8,128)}), f32[24,768]{1,0:T(8,128)}) %reduce-scatter.47.cloned.1.call-update) | async-done | bytes 73744
  4515.7 102.1 %reduce-scatter.43.cloned.1.call-done = f32[24,768]{1,0:T(8,128)} async-done(((f32[768,768]{1,0:T(8,128)}), f32[24,768]{1,0:T(8,128)}) %reduce-scatter.43.cloned.1.call-update) | async-done | bytes 73744
  4619.0 102.8 %reduce-scatter.37.cloned.1.call-done = f32[24,768]{1,0:T(8,128)} async-done(((f32[768,768]{1,0:T(8,128)}), f32[24,768]{1,0:T(8,128)}) %reduce-scatter.37.cloned.1.call-update) | async-done | bytes 73744
  4723.0 102.1 %reduce-scatter.27.cloned.1.call-done = f32[24,768]{1,0:T(8,128)} async-done(((f32[768,768]{1,0:T(8,128)}), f32[24,768]{1,0:T(8,128)}) %reduce-scatter.27.cloned.1.call-update) | async-done | bytes 73744 | tf_op jit(solution)/shard_map/reduce_scatter | solution.py:514
  4825.0 104.2 %reduce-scatter.25.cloned.1.call-done = f32[24,768]{1,0:T(8,128)} async-done(((f32[768,768]{1,0:T(8,128)}), f32[24,768]{1,0:T(8,128)}) %reduce-scatter.25.cloned.1.call-update) | async-done | bytes 73744 | tf_op jit(solution)/shard_map/reduce_scatter | solution.py:514
  4931.5 101.0 %reduce-scatter.45.cloned.1.call-done = f32[24,768]{1,0:T(8,128)} async-done(((f32[768,768]{1,0:T(8,128)}), f32[24,768]{1,0:T(8,128)}) %reduce-scatter.45.cloned.1.call-update) | async-done | bytes 73744
  5033.7 103.0 %reduce-scatter.41.cloned.1.call-done = f32[24,768]{1,0:T(8,128)} async-done(((f32[768,768]{1,0:T(8,128)}), f32[24,768]{1,0:T(8,128)}) %reduce-scatter.41.cloned.1.call-update) | async-done | bytes 73744
  5139.2 138.0 %reduce-scatter.35.cloned.1.call-done = f32[96,768]{1,0:T(8,128)} async-done(((f32[3072,768]{1,0:T(8,128)}), f32[96,768]{1,0:T(8,128)}) %reduce-scatter.35.cloned.1.call-update) | async-done | bytes 294928 | tf_op jit(solution)/shard_map/reduce_scatter | solution.py:522
  5277.3 141.5 %reduce-scatter.33.cloned.1.call-done = f32[96,768]{1,0:T(8,128)} async-done(((f32[3072,768]{1,0:T(8,128)}), f32[96,768]{1,0:T(8,128)}) %reduce-scatter.33.cloned.1.call-update) | async-done | bytes 294928 | tf_op jit(solution)/shard_map/reduce_scatter | solution.py:522
  5420.7 138.5 %reduce-scatter.31.cloned.1.call-done = f32[24,3072]{1,0:T(8,128)} async-done(((f32[768,3072]{1,0:T(8,128)}), f32[24,3072]{1,0:T(8,128)}) %reduce-scatter.31.cloned.1.call-update) | async-done | bytes 294928 | tf_op jit(solution)/shard_map/reduce_scatter | solution.py:520
  5559.1 141.2 %reduce-scatter.29.cloned.1.call-done = f32[24,3072]{1,0:T(8,128)} async-done(((f32[768,3072]{1,0:T(8,128)}), f32[24,3072]{1,0:T(8,128)}) %reduce-scatter.29.cloned.1.call-update) | async-done | bytes 294928 | tf_op jit(solution)/shard_map/reduce_scatter | solution.py:520
  (3744 shorter events, 3887.1 us)
Async XLA Ops:
  8.8 116.0 %all-gather.51.cloned.1.call-start = ((), (), s32[]{:S(2)}) async-start(), calls=%async_computation.20 | async-start | bytes 1216512 | tf_op jit(solution)/shard_map/all_gather | solution.py:210
  10.3 189.9 %all-gather.47.cloned.1.call-start = ((), (), s32[]{:S(2)}) async-start(), calls=%async_computation.18 | async-start | bytes 1216512 | tf_op jit(solution)/shard_map/all_gather | solution.py:208
  11.8 727.3 %all-gather.53.cloned.1.call-start = ((), (), s32[]{:S(2)}) async-start(), calls=%async_computation.21 | async-start | bytes 1216512 | tf_op jit(solution)/shard_map/all_gather | solution.py:211
  13.3 730.7 %all-gather.55.cloned.1.call-start = ((), (), s32[]{:S(2)}) async-start(), calls=%async_computation.22 | async-start | bytes 4866048 | tf_op jit(solution)/shard_map/all_gather | solution.py:217
  15.1 766.8 %all-gather.57.cloned.1.call-start = ((), (), s32[]{:S(2)}) async-start(), calls=%async_computation.23 | async-start | bytes 4866048 | tf_op jit(solution)/shard_map/all_gather | solution.py:221
  16.9 777.2 %all-gather.61.cloned.1.call-start = ((), (), s32[]{:S(2)}) async-start(), calls=%async_computation.25 | async-start | bytes 1216512 | tf_op jit(solution)/shard_map/all_gather | solution.py:209
  17.6 779.7 %all-gather.63.cloned.1.call-start = ((), (), s32[]{:S(2)}) async-start(), calls=%async_computation.26 | async-start | bytes 1216512 | tf_op jit(solution)/shard_map/all_gather | solution.py:210
  18.4 798.4 %all-gather.59.cloned.1.call-start = ((), (), s32[]{:S(2)}) async-start(), calls=%async_computation.24 | async-start | bytes 1216512 | tf_op jit(solution)/shard_map/all_gather | solution.py:208
  19.1 1393.8 %all-gather.65.cloned.1.call-start = ((), (), s32[]{:S(2)}) async-start(), calls=%async_computation.27 | async-start | bytes 1216512 | tf_op jit(solution)/shard_map/all_gather | solution.py:211
  19.7 1398.4 %all-gather.67.cloned.1.call-start = ((), (), s32[]{:S(2)}) async-start(), calls=%async_computation.28 | async-start | bytes 4866048 | tf_op jit(solution)/shard_map/all_gather | solution.py:217
  20.4 1435.8 %all-gather.69.cloned.1.call-start = ((), (), s32[]{:S(2)}) async-start(), calls=%async_computation.29 | async-start | bytes 4866048 | tf_op jit(solution)/shard_map/all_gather | solution.py:221
  21.0 4303.7 %reduce-scatter.39.cloned.1.call-start = ((), (), s32[]{:S(2)}) async-start(), calls=%async_computation.31 | async-start | bytes 2433024
  4145.7 262.2 %all-reduce.50.cloned.1.call-start = ((), (), s32[]{:S(2)}) async-start(), calls=%async_computation.36 | async-start | bytes 196608
  4226.6 287.9 %reduce-scatter.47.cloned.1.call-start = ((), (), s32[]{:S(2)}) async-start(), calls=%async_computation.35 | async-start | bytes 2433024
  4231.5 386.3 %reduce-scatter.43.cloned.1.call-start = ((), (), s32[]{:S(2)}) async-start(), calls=%async_computation.33 | async-start | bytes 2433024
  4236.2 485.6 %reduce-scatter.37.cloned.1.call-start = ((), (), s32[]{:S(2)}) async-start(), calls=%async_computation.30 | async-start | bytes 2433024
  4244.1 581.0 %reduce-scatter.27.cloned.1.call-start = ((), (), s32[]{:S(2)}) async-start(), calls=%async_computation.13 | async-start | bytes 2433024 | tf_op jit(solution)/shard_map/reduce_scatter | solution.py:514
  4248.9 680.3 %reduce-scatter.25.cloned.1.call-start = ((), (), s32[]{:S(2)}) async-start(), calls=%async_computation.12 | async-start | bytes 2433024 | tf_op jit(solution)/shard_map/reduce_scatter | solution.py:514
  4253.9 778.5 %reduce-scatter.45.cloned.1.call-start = ((), (), s32[]{:S(2)}) async-start(), calls=%async_computation.34 | async-start | bytes 2433024
  4261.3 875.4 %reduce-scatter.41.cloned.1.call-start = ((), (), s32[]{:S(2)}) async-start(), calls=%async_computation.32 | async-start | bytes 2433024
  4268.8 1008.4 %reduce-scatter.35.cloned.1.call-start = ((), (), s32[]{:S(2)}) async-start(), calls=%async_computation.17 | async-start | bytes 9732096 | tf_op jit(solution)/shard_map/reduce_scatter | solution.py:522
  4279.1 1139.7 %reduce-scatter.33.cloned.1.call-start = ((), (), s32[]{:S(2)}) async-start(), calls=%async_computation.16 | async-start | bytes 9732096 | tf_op jit(solution)/shard_map/reduce_scatter | solution.py:522
  4290.7 1268.4 %reduce-scatter.31.cloned.1.call-start = ((), (), s32[]{:S(2)}) async-start(), calls=%async_computation.15 | async-start | bytes 9732096 | tf_op jit(solution)/shard_map/reduce_scatter | solution.py:520
  4303.1 1397.3 %reduce-scatter.29.cloned.1.call-start = ((), (), s32[]{:S(2)}) async-start(), calls=%async_computation.14 | async-start | bytes 9732096 | tf_op jit(solution)/shard_map/reduce_scatter | solution.py:520
  (595 other events, 6056.0 us)
Sparse Core Ops, SparseCore 0:
  11.5 56.7 all-gather.48
  71.8 52.9 all-gather.50
  127.7 72.4 all-gather.46
  203.6 53.0 all-gather.52
  260.0 62.4 all-gather.54
  325.9 62.4 all-gather.56
  447.1 53.0 all-gather.62
  503.1 52.9 all-gather.58
  559.4 53.0 all-gather.64
  616.0 62.5 all-gather.66
  681.8 62.3 all-gather.68
  4145.8 103.0 reduce-scatter.38
  4257.5 150.3 all-reduce.49
  4413.9 100.5 reduce-scatter.46
  4519.7 98.0 reduce-scatter.42
  4623.8 98.0 reduce-scatter.36
  4726.9 98.0 reduce-scatter.26
  4831.2 98.0 reduce-scatter.24
  4934.4 98.0 reduce-scatter.44
  5038.6 98.0 reduce-scatter.40
  5142.6 134.6 reduce-scatter.34
  5284.2 134.5 reduce-scatter.32
  5424.5 134.5 reduce-scatter.30
  5566.0 134.2 reduce-scatter.28
  (1 shorter events, 52.8 us)
where the time goes:
time: 5740 us; the launch traced here: 5710 us
  local copies, waits for them, and re-layouts  1900 us (33%)
  waiting for transfers between devices  1580 us (28%)
  matrix products  1390 us (24%)
  other arithmetic  481 us (8%)
  loops' own time  264 us (5%)
    unnamed x32, waiting for transfers between devices  570 us
    dot_general x156, matrix products, contract_cols(): lax.dot_general(left, right, (((1,), (1,)), ((), ())), preferred_element_...  553 us
    dot_general x105, matrix products, contract_rows(): lax.dot_general(left, right, (((0,), (0,)), ((), ())), preferred_element_...  388 us
    reduce_scatter x2, waiting for transfers between devices, scatter_each(): lax.psum_scatter(grad_inner, ('dp', 'mp'), scatter_dimension=0, tiled=True)  280 us
    reduce_scatter x2, waiting for transfers between devices, scatter_each(): lax.psum_scatter(grad_outer, ('dp', 'mp'), scatter_dimension=0, tiled=True)  280 us
    reshape x48, local copies, waits for them, and re-layouts, head_scores(): scores = scores.reshape(count_query, BLK, count_key, BLK)  235 us
    reshape x48, local copies, waits for them, and re-layouts, backward_one_head(): contract_cols(dcontext_part, head_columns(value_rows, head))  234 us
    while x1152, local copies, waits for them, and re-layouts  231 us
  transfers between devices with their start and end apart: 33, of which 17 were waited for; matrix products, arithmetic and copies ran while one was open for 22% of the time, Pallas kernels for 0%

commit v1 on v0

v1 whole, which is shorter than its diff:
```python
import functools
import math

import jax
import jax.numpy as jnp
from jax import lax
from jax.experimental import pallas as pl
from jax.experimental.pallas import tpu as pltpu
from jax.sharding import PartitionSpec as P

D = 768
HEADS = 12
HD = 64
FF = 3072
BLK = 128
SPAN = 8
RIM = 4
PAIRS = HEADS // 2
AXES = ("dp", "mp")
SCALE = HD**-0.5
SCALE2 = SCALE * math.log2(math.e)
F32 = jnp.float32
BF16 = jnp.bfloat16


def cost(us):
    return pl.CostEstimate(flops=int(us * 1e9), bytes_accessed=1_000_000, transcendentals=0)


def once(shape, column=0):
    return pl.BlockSpec(shape, lambda i: (0,) * (len(shape) - 1) + (column,), pipeline_mode=pl.Buffered(1))


def dot(a, b):
    return jnp.dot(a, b, preferred_element_type=F32)


def dot_rows(a, b):
    return lax.dot_general(a, b, (((0,), (0,)), ((), ())), preferred_element_type=F32)


def dot_cols(a, b):
    return lax.dot_general(a, b, (((1,), (1,)), ((), ())), preferred_element_type=F32)


def dot_tt(a, b):
    return lax.dot_general(a, b, (((0,), (1,)), ((), ())), preferred_element_type=F32)


def scan_blocks(flags, pos, first_s, last_s, own):
    ext = own + 2 * RIM
    total = flags.shape[0]
    base = pos * own - RIM

    def opens(e):
        gid = base + e
        inside = jnp.logical_and(gid >= 0, gid < total)
        return jnp.where(inside, flags[jnp.clip(gid, 0, total - 1)], 1)

    def up(e, start):
        start = jnp.where(opens(e) == 1, e, start)
        first_s[e] = start
        return start

    lax.fori_loop(0, ext, up, jnp.int32(0))

    def down(n, stop):
        e = ext - 1 - n
        last_s[e] = stop
        return jnp.where(opens(e) == 1, e, stop)

    lax.fori_loop(0, ext, down, jnp.int32(ext))


def forward_kernel(
    flags, keep, pos, factor, q_t, k, v_t, ctx_t, lse, qbd, acc, top, total, first_s, last_s
):
    own = q_t.shape[1] // BLK
    scan_blocks(flags, pos[0], first_s, last_s, own)
    qbd[...] = jnp.zeros_like(qbd)

    @pl.loop(0, own)
    def _(i):
        cols = pl.ds(pl.multiple_of(i * BLK, BLK), BLK)
        for hp in range(PAIRS):
            qbd[hp, :HD, :BLK] = q_t[pl.ds(hp * BLK, HD), cols]
            qbd[hp, HD:, BLK:] = q_t[pl.ds(hp * BLK + HD, HD), cols]
        acc[...] = jnp.zeros_like(acc)
        top[...] = jnp.full_like(top, -1e30)
        total[...] = jnp.zeros_like(total)
        me = i + RIM
        start = first_s[me]

        @pl.loop(start, last_s[me])
        def _(e):
            wanted = jnp.logical_or(e == me, keep[i, jnp.clip(e - me + SPAN - 1, 0, 2 * SPAN - 2)] > 0)

            @pl.when(wanted)
            def _():
                rows = pl.ds(pl.multiple_of(e * BLK, BLK), BLK)
                ab = (me - start) * SPAN + (e - start)
                for hp in range(PAIRS):
                    lanes = slice(hp * BLK, (hp + 1) * BLK)
                    s = dot(k[rows, lanes], qbd[hp])
                    m_old = top[hp : hp + 1, :]
                    m_new = jnp.maximum(m_old, jnp.max(s, axis=0, keepdims=True))
                    p = jnp.exp2((s - m_new) * SCALE2)
                    alpha = jnp.exp2((m_old - m_new) * SCALE2)
                    total[hp : hp + 1, :] = total[hp : hp + 1, :] * alpha + jnp.sum(
                        p, axis=0, keepdims=True
                    )
                    top[hp : hp + 1, :] = m_new
                    c = dot(v_t[lanes, rows], p.astype(BF16))
                    f = factor[ab, hp : hp + 1, :]
                    upper = slice(hp * BLK, hp * BLK + HD)
                    lower = slice(hp * BLK + HD, (hp + 1) * BLK)
                    acc[upper, :] = acc[upper, :] * alpha[:, :BLK] + c[:HD, :BLK] * f[:, :BLK]
                    acc[lower, :] = acc[lower, :] * alpha[:, BLK:] + c[HD:, BLK:] * f[:, BLK:]

        for hp in range(PAIRS):
            t = total[hp : hp + 1, :]
            r = 1.0 / t
            upper = slice(hp * BLK, hp * BLK + HD)
            lower = slice(hp * BLK + HD, (hp + 1) * BLK)
            ctx_t[upper, cols] = acc[upper, :] * r[:, :BLK]
            ctx_t[lower, cols] = acc[lower, :] * r[:, BLK:]
            lse[i, hp : hp + 1, :] = top[hp : hp + 1, :] * SCALE2 + jnp.log2(t)


def smem():
    return pl.BlockSpec(memory_space=pltpu.SMEM)


def vmem():
    return pl.BlockSpec(memory_space=pltpu.VMEM)


def attend(flags, keep, pos, factor, q_t, k, v_t):
    own = q_t.shape[1] // BLK
    ext = own + 2 * RIM
    return pl.pallas_call(
        forward_kernel,
        out_shape=(
            jax.ShapeDtypeStruct(q_t.shape, F32),
            jax.ShapeDtypeStruct((own, 8, 2 * BLK), F32),
        ),
        in_specs=[smem(), smem(), smem(), vmem(), vmem(), vmem(), vmem()],
        out_specs=(vmem(), vmem()),
        scratch_shapes=[
            pltpu.VMEM((PAIRS, BLK, 2 * BLK), BF16),
            pltpu.VMEM((D, BLK), F32),
            pltpu.VMEM((8, 2 * BLK), F32),
            pltpu.VMEM((8, 2 * BLK), F32),
            pltpu.SMEM((ext,), jnp.int32),
            pltpu.SMEM((ext,), jnp.int32),
        ],
        compiler_params=pltpu.CompilerParams(vmem_limit_bytes=40 * 2**20),
        cost_estimate=cost(13),
        name="attend",
    )(flags, keep, pos, factor, q_t, k, v_t)


def backward_kernel(
    flags,
    keep,
    pos,
    log_factor,
    inv_factor,
    q_t,
    q,
    dc_t,
    dc,
    ctx_t,
    lse,
    k,
    k_t,
    v,
    dq_t,
    dk,
    dv,
    dr,
    qbd,
    cbd,
    q2,
    c2,
    dq_acc,
    dk_acc,
    dv_acc,
    delta,
    first_s,
    last_s,
):
    own = q_t.shape[1] // BLK
    scan_blocks(flags, pos[0], first_s, last_s, own)
    qbd[...] = jnp.zeros_like(qbd)
    cbd[...] = jnp.zeros_like(cbd)
    dk_acc[...] = jnp.zeros_like(dk_acc)
    dv_acc[...] = jnp.zeros_like(dv_acc)
    dr[...] = jnp.zeros_like(dr)
    left = lax.broadcasted_iota(jnp.int32, (BLK, BLK), 1) < HD

    @pl.loop(0, own)
    def _(i):
        cols = pl.ds(pl.multiple_of(i * BLK, BLK), BLK)
        for hp in range(PAIRS):
            lanes = slice(hp * BLK, (hp + 1) * BLK)
            upper = pl.ds(hp * BLK, HD)
            lower = pl.ds(hp * BLK + HD, HD)
            qbd[hp, :HD, :BLK] = q_t[upper, cols]
            qbd[hp, HD:, BLK:] = q_t[lower, cols]
            cu = dc_t[upper, cols]
            cl = dc_t[lower, cols]
            cbd[hp, :HD, :BLK] = cu
            cbd[hp, HD:, BLK:] = cl
            delta[hp : hp + 1, :BLK] = jnp.sum(
                cu.astype(F32) * ctx_t[upper, cols], axis=0, keepdims=True
            )
            delta[hp : hp + 1, BLK:] = jnp.sum(
                cl.astype(F32) * ctx_t[lower, cols], axis=0, keepdims=True
            )
            qn = q[cols, lanes].astype(F32)
            cn = dc[cols, lanes].astype(F32)
            q2[hp, :BLK, :] = jnp.where(left, qn, 0.0).astype(BF16)
            q2[hp, BLK:, :] = jnp.where(left, 0.0, qn).astype(BF16)
            c2[hp, :BLK, :] = jnp.where(left, cn, 0.0).astype(BF16)
            c2[hp, BLK:, :] = jnp.where(left, 0.0, cn).astype(BF16)
        dq_acc[...] = jnp.zeros_like(dq_acc)
        me = i + RIM
        start = first_s[me]

        @pl.loop(start, last_s[me])
        def _(e):
            wanted = jnp.logical_or(e == me, keep[i, jnp.clip(e - me + SPAN - 1, 0, 2 * SPAN - 2)] > 0)

            @pl.when(wanted)
            def _():
                rows = pl.ds(pl.multiple_of(e * BLK, BLK), BLK)
                ab = (me - start) * SPAN + (e - start)
                for hp in range(PAIRS):
                    lanes = slice(hp * BLK, (hp + 1) * BLK)
                    vb = v[rows, lanes]
                    s = dot(k[rows, lanes], qbd[hp])
                    dw = dot(vb, cbd[hp])
                    bias = log_factor[ab, hp : hp + 1, :] - lse[i, hp : hp + 1, :]
                    w = jnp.exp2(s * SCALE2 + bias)
                    ds = w * (dw - delta[hp : hp + 1, :] * inv_factor[ab, hp : hp + 1, :])
                    wb = w.astype(BF16)
                    dsb = ds.astype(BF16)
                    dvc = dot(wb, c2[hp])
                    dkc = dot(dsb, q2[hp])
                    dqc = dot(k_t[lanes, rows], dsb)
                    dv_acc[rows, lanes] += dvc
                    dk_acc[rows, lanes] += dkc
                    upper = slice(hp * BLK, hp * BLK + HD)
                    lower = slice(hp * BLK + HD, (hp + 1) * BLK)
                    dq_acc[upper, :] += dqc[:HD, :BLK]
                    dq_acc[lower, :] += dqc[HD:, BLK:]
                    dr[ab, hp : hp + 1, :] += jnp.sum(
                        dvc * vb.astype(F32), axis=0, keepdims=True
                    )

        dq_t[:, cols] = (dq_acc[...] * SCALE).astype(BF16)

    ext = dk.shape[0] // BLK

    @pl.loop(0, ext)
    def _(e):
        rows = pl.ds(pl.multiple_of(e * BLK, BLK), BLK)
        dk[rows, :] = (dk_acc[rows, :] * SCALE).astype(BF16)
        dv[rows, :] = dv_acc[rows, :].astype(BF16)


def attend_back(flags, keep, pos, log_factor, inv_factor, q_t, q, dc_t, dc, ctx_t, lse, k, k_t, v):
    own = q_t.shape[1] // BLK
    ext = own + 2 * RIM
    return pl.pallas_call(
        backward_kernel,
        out_shape=(
            jax.ShapeDtypeStruct(q_t.shape, BF16),
            jax.ShapeDtypeStruct(k.shape, BF16),
            jax.ShapeDtypeStruct(v.shape, BF16),
            jax.ShapeDtypeStruct((SPAN * SPAN, 8, BLK), F32),
        ),
        in_specs=[smem()] * 3 + [vmem()] * 11,
        out_specs=(vmem(),) * 4,
        scratch_shapes=[
            pltpu.VMEM((PAIRS, BLK, 2 * BLK), BF16),
            pltpu.VMEM((PAIRS, BLK, 2 * BLK), BF16),
            pltpu.VMEM((PAIRS, 2 * BLK, BLK), BF16),
            pltpu.VMEM((PAIRS, 2 * BLK, BLK), BF16),
            pltpu.VMEM((D, BLK), F32),
            pltpu.VMEM((ext * BLK, D), F32),
            pltpu.VMEM((ext * BLK, D), F32),
            pltpu.VMEM((8, 2 * BLK), F32),
            pltpu.SMEM((ext,), jnp.int32),
            pltpu.SMEM((ext,), jnp.int32),
        ],
        compiler_params=pltpu.CompilerParams(vmem_limit_bytes=56 * 2**20),
        cost_estimate=cost(5),
        name="attend_back",
    )(flags, keep, pos, log_factor, inv_factor, q_t, q, dc_t, dc, ctx_t, lse, k, k_t, v)


def centred_rows(x):
    middle = jnp.mean(x, -1, keepdims=True)
    c = x - middle
    spread = jnp.mean(c * c, -1, keepdims=True)
    r = lax.rsqrt(spread + 1e-06)
    return c * r, r

def gelu_and_slope(v):
    e = jnp.exp2(v * v * (-0.5 * math.log2(math.e)))
    t = 1.0 / (1.0 + jnp.abs(v) * (0.3275911 * math.sqrt(0.5)))
    q = t * (0.127414796 + t * (-0.142248368 + t * (0.7107068705 + t * (-0.7265760135 + t * 0.5307027145)))) * e
    phi = jnp.where(v >= 0, 1.0 - q, q)
    return v * phi, phi + v * (e * (1.0 / math.sqrt(2.0 * math.pi)))

ROWS = 256

def ffn_kernel(ctx_t, hidden, wo, w1, w2, vec, b1, first, normed_low, active, slope, second, result, result_low):
    x = hidden[...].astype(F32) + dot_rows(ctx_t[...].astype(BF16), wo[...]) + vec[0:1, :]
    first[...] = x
    hat, _ = centred_rows(x)
    normed = hat * vec[1:2, :] + vec[2:3, :]
    low = normed.astype(BF16)
    normed_low[...] = low
    total = normed + vec[3:4, :]
    for j in range(FF // D):
        cols = slice(j * D, (j + 1) * D)
        inner = dot(low, w1[:, cols]) + b1[:, cols]
        a, s = gelu_and_slope(inner)
        a = a.astype(BF16)
        active[:, cols] = a
        slope[:, cols] = s.astype(BF16)
        total = total + dot(a, w2[:, cols])
    second[...] = total
    hat, _ = centred_rows(total)
    x = hat * vec[4:5, :] + vec[5:6, :]
    result[...] = x
    result_low[...] = x.astype(BF16)

def ffn(ctx_t, hidden, wo, wo_at, w12, vec, b1):
    n = hidden.shape[0]
    row = lambda w: pl.BlockSpec((ROWS, w), lambda i: (i, 0))
    return pl.pallas_call(
        ffn_kernel,
        grid=(n // ROWS,),
        in_specs=[pl.BlockSpec((D, ROWS), lambda i: (0, i)), row(D), once((D, D), wo_at), once((D, FF)), once((D, FF), 1), once((8, D)), once((1, FF))],
        out_specs=[row(D), row(D), row(FF), row(FF), row(D), row(D), row(D)],
        out_shape=[jax.ShapeDtypeStruct((n, D), F32), jax.ShapeDtypeStruct((n, D), BF16), jax.ShapeDtypeStruct((n, FF), BF16),
                   jax.ShapeDtypeStruct((n, FF), BF16), jax.ShapeDtypeStruct((n, D), F32), jax.ShapeDtypeStruct((n, D), F32), jax.ShapeDtypeStruct((n, D), BF16)],
        compiler_params=pltpu.CompilerParams(vmem_limit_bytes=56 * 2**20),
        cost_estimate=cost(28),
        name="ffn",
    )(ctx_t, hidden, wo, w12, w12, vec, b1)

def ffn_back_kernel(grad, second, first, slope, w1, w2, wo, gains, douter, dinner, dfirst, dattend, dc, dc_t, sums, b1_sum):
    @pl.when(pl.program_id(0) == 0)
    def _():
        sums[...] = jnp.zeros_like(sums)
        b1_sum[...] = jnp.zeros_like(b1_sum)
    def back(g, x, gain):
        hat, r = centred_rows(x)
        e = g * gain
        return (e - jnp.mean(e, -1, keepdims=True) - hat * jnp.mean(e * hat, -1, keepdims=True)) * r, hat
    def column(v):
        return jnp.sum(v, 0, keepdims=True)
    g = grad[...].astype(F32)
    dsecond, hat = back(g, second[...], gains[4:5, :])
    sums[0:1, :] += column(g * hat)
    sums[1:2, :] += column(g)
    low = dsecond.astype(BF16)
    douter[...] = low
    sums[2:3, :] += column(low.astype(F32))
    dnormed = dsecond
    for j in range(FF // D):
        cols = slice(j * D, (j + 1) * D)
        d = (dot_cols(low, w2[:, cols]) * slope[:, cols].astype(F32)).astype(BF16)
        dinner[:, cols] = d
        b1_sum[:, cols] += column(d.astype(F32))
        dnormed = dnormed + dot_cols(d, w1[:, cols])
    dx, hat = back(dnormed, first[...], gains[1:2, :])
    sums[3:4, :] += column(dnormed * hat)
    sums[4:5, :] += column(dnormed)
    dfirst[...] = dx
    low = dx.astype(BF16)
    dattend[...] = low
    sums[5:6, :] += column(low.astype(F32))
    dc[...] = dot_cols(low, wo[...]).astype(BF16)
    dc_t[...] = dot_cols(wo[...], low).astype(BF16)

def ffn_back(grad, second, first, slope, w12, wo, wo_at, gains):
    n = grad.shape[0]
    row = lambda w: pl.BlockSpec((ROWS, w), lambda i: (i, 0))
    return pl.pallas_call(
        ffn_back_kernel,
        grid=(n // ROWS,),
        in_specs=[row(D), row(D), row(D), row(FF), once((D, FF)), once((D, FF), 1), once((D, D), wo_at), once((8, D))],
        out_specs=[row(D), row(FF), row(D), row(D), row(D), pl.BlockSpec((D, ROWS), lambda i: (0, i)), pl.BlockSpec((8, D), lambda i: (0, 0)), pl.BlockSpec((1, FF), lambda i: (0, 0))],
        out_shape=[jax.ShapeDtypeStruct((n, D), BF16), jax.ShapeDtypeStruct((n, FF), BF16), jax.ShapeDtypeStruct((n, D), F32),
                   jax.ShapeDtypeStruct((n, D), BF16), jax.ShapeDtypeStruct((n, D), BF16), jax.ShapeDtypeStruct((D, n), BF16),
                   jax.ShapeDtypeStruct((8, D), F32), jax.ShapeDtypeStruct((1, FF), F32)],
        compiler_params=pltpu.CompilerParams(vmem_limit_bytes=56 * 2**20),
        cost_estimate=cost(23),
        name="ffn_back",
    )(grad, second, first, slope, w12, w12, wo, gains)

def ffn_grads_kernel(normed, dinner, active, douter, ctx_t, dattend, sums, b1_sum, out, turned):
    n = pl.program_id(0)
    blocks = FF // D
    @pl.when(n == 0)
    def _():
        turned[...] = normed[...].T
    @pl.when(n < blocks)
    def _():
        out[...] = dot(turned[...], dinner[...]).astype(BF16)
    @pl.when(jnp.logical_and(n >= blocks, n < 2 * blocks))
    def _():
        out[...] = dot_rows(active[...], douter[...]).astype(BF16)
    @pl.when(n == 2 * blocks)
    def _():
        out[...] = dot(ctx_t[...].astype(BF16), dattend[...]).astype(BF16)
    @pl.when(n == 2 * blocks + 1)
    def _():
        rows = jnp.concatenate([sums[...]] + [b1_sum[:, j * D:(j + 1) * D] for j in range(blocks)] + [jnp.zeros((128 - 8 - blocks, D), F32)], 0)
        out[:, :128] = rows.T.astype(BF16)

def ffn_grads(normed, dinner, active, douter, ctx_t, dattend, sums, b1_sum):
    n = normed.shape[0]
    blocks = FF // D
    return pl.pallas_call(
        ffn_grads_kernel,
        grid=(2 * blocks + 2,),
        in_specs=[once((n, D)), pl.BlockSpec((n, D), lambda i: (0, jnp.minimum(i, blocks - 1))),
                  pl.BlockSpec((n, D), lambda i: (0, jnp.clip(i - blocks, 0, blocks - 1))),
                  once((n, D)), once((D, n)), once((n, D)), once((8, D)), once((1, FF))],
        out_specs=pl.BlockSpec((D, D), lambda i: (0, i)),
        out_shape=jax.ShapeDtypeStruct((D, 2 * FF + D + 128), BF16),
        scratch_shapes=[pltpu.VMEM((D, n), BF16)],
        compiler_params=pltpu.CompilerParams(vmem_limit_bytes=56 * 2**20),
        cost_estimate=cost(20),
        name="ffn_grads",
    )(normed, dinner, active, douter, ctx_t, dattend, sums, b1_sum)


def project_kernel(low, w, qb, vb, q, q_t, k, k_t, v, v_t):
    i = pl.program_id(0)
    n = pl.num_programs(0)
    x = low[...]
    kk = dot(x, w[:, D : 2 * D]).astype(BF16)
    k[...] = kk
    k_t[...] = kk.T
    vv = (dot(x, w[:, 2 * D : 3 * D]) + vb[...]).astype(BF16)
    v[...] = vv
    v_t[...] = vv.T
    skip = RIM * BLK // ROWS

    @pl.when(jnp.logical_and(i >= skip, i < n - skip))
    def _():
        qq = (dot(x, w[:, :D]) + qb[...]).astype(BF16)
        q[...] = qq
        q_t[...] = qq.T

def project(low_ext, w, qb, vb):
    n = low_ext.shape[0]
    rim = RIM * BLK
    skip = rim // ROWS
    own = n - 2 * rim
    last = own // ROWS - 1
    row = pl.BlockSpec((ROWS, D), lambda i: (i, 0))
    col = pl.BlockSpec((D, ROWS), lambda i: (0, i))
    qrow = pl.BlockSpec((ROWS, D), lambda i: (jnp.clip(i - skip, 0, last), 0))
    qcol = pl.BlockSpec((D, ROWS), lambda i: (0, jnp.clip(i - skip, 0, last)))
    tall = jax.ShapeDtypeStruct((n, D), BF16)
    wide = jax.ShapeDtypeStruct((D, n), BF16)
    return pl.pallas_call(
        project_kernel,
        grid=(n // ROWS,),
        in_specs=[row, once((D, 3 * D)), once((1, D)), once((1, D))],
        out_specs=[qrow, qcol, row, col, row, col],
        out_shape=[jax.ShapeDtypeStruct((own, D), BF16), jax.ShapeDtypeStruct((D, own), BF16), tall, wide, tall, wide],
        compiler_params=pltpu.CompilerParams(vmem_limit_bytes=40 * 2**20),
        cost_estimate=cost(14),
        name="project",
    )(low_ext, w, qb, vb)

def att_grads_kernel(low, dq_t, dk, dv, logit, out, turned):
    n = pl.program_id(0)
    own = dq_t.shape[1]
    rim = (low.shape[0] - own) // 2

    @pl.when(n == 0)
    def _():
        turned[...] = low[...].T
        out[...] = dot_cols(turned[:, rim : rim + own], dq_t[...]).astype(BF16)

    @pl.when(n == 1)
    def _():
        out[...] = dot(turned[...], dk[...]).astype(BF16)

    @pl.when(n == 2)
    def _():
        out[...] = dot(turned[...], dv[...]).astype(BF16)

    @pl.when(n == 3)
    def _():
        qb = jnp.sum(dq_t[...].astype(F32), 1, keepdims=True)
        vb = jnp.sum(dv[...].astype(F32), 0, keepdims=True)
        rows = jnp.concatenate([vb, logit[...], jnp.zeros((126, D), F32)], 0).T
        lane = lax.broadcasted_iota(jnp.int32, (D, 128), 1)
        out[:, :128] = jnp.where(lane == 2, qb, rows).astype(BF16)

def att_grads(low_ext, dq_t, dk, dv, logit):
    n = low_ext.shape[0]
    own = dq_t.shape[1]
    return pl.pallas_call(
        att_grads_kernel,
        grid=(4,),
        in_specs=[once((n, D)), once((D, own)), once((n, D)), once((n, D)), once((1, D))],
        out_specs=pl.BlockSpec((D, D), lambda i: (0, i)),
        out_shape=jax.ShapeDtypeStruct((D, 3 * D + 128), BF16),
        scratch_shapes=[pltpu.VMEM((D, n), BF16)],
        compiler_params=pltpu.CompilerParams(vmem_limit_bytes=48 * 2**20),
        cost_estimate=cost(12),
        name="att_grads",
    )(low_ext, dq_t, dk, dv, logit)

def input_back_kernel(dk, dv, dq_t, dfirst, w, own, rims):
    i = pl.program_id(0)
    n = pl.num_programs(0)
    skip = RIM * BLK // ROWS
    total = dot_cols(dk[...], w[:, D : 2 * D]) + dot_cols(dv[...], w[:, 2 * D : 3 * D])
    inside = jnp.logical_and(i >= skip, i < n - skip)

    @pl.when(inside)
    def _():
        own[...] = total + dot_tt(dq_t[...], w[:, :D]) + dfirst[...]

    @pl.when(jnp.logical_not(inside))
    def _():
        rims[...] = total.astype(BF16)

def input_back(dk, dv, dq_t, dfirst, w):
    n = dk.shape[0]
    own = dfirst.shape[0]
    skip = (n - own) // 2 // ROWS
    last = own // ROWS - 1
    row = pl.BlockSpec((ROWS, D), lambda i: (i, 0))
    orow = pl.BlockSpec((ROWS, D), lambda i: (jnp.clip(i - skip, 0, last), 0))
    ocol = pl.BlockSpec((D, ROWS), lambda i: (0, jnp.clip(i - skip, 0, last)))
    rrow = pl.BlockSpec((ROWS, D), lambda i: (jnp.where(i < skip, i, jnp.maximum(i - last - 1, skip)), 0))
    return pl.pallas_call(
        input_back_kernel,
        grid=(n // ROWS,),
        in_specs=[row, row, ocol, orow, once((D, 3 * D))],
        out_specs=[orow, rrow],
        out_shape=[jax.ShapeDtypeStruct((own, D), F32), jax.ShapeDtypeStruct((n - own, D), BF16)],
        compiler_params=pltpu.CompilerParams(vmem_limit_bytes=40 * 2**20),
        cost_estimate=cost(12),
        name="input_back",
    )(dk, dv, dq_t, dfirst, w)


def neighbours(tail, head):
    count = lax.axis_size("dp")
    return (
        lax.ppermute(tail, "dp", [(i, i + 1) for i in range(count - 1)]),
        lax.ppermute(head, "dp", [(i + 1, i) for i in range(count - 1)]),
    )


def gathered(part):
    return lax.all_gather(part, AXES, axis=0, tiled=True)


def place():
    dp = lax.axis_index("dp")
    mp = lax.axis_index("mp")
    return dp // 2, (dp % 2) * (lax.axis_size("mp") // 2) + mp // 2, mp % 2


def sizes():
    return lax.axis_size("dp") // 2, lax.axis_size("mp")


def swap(block, mask):
    count = lax.axis_size("dp") * lax.axis_size("mp")
    return lax.ppermute(block, AXES, [(i, i ^ mask) for i in range(count)])


def gathered_in_steps(part):
    far, middle = sizes()
    z, m, c = place()
    plane = jnp.zeros((far,) + part.shape, part.dtype)
    for d in range(far):
        piece = part if d == 0 else swap(part, d * 2 * middle)
        plane = lax.dynamic_update_slice(plane, piece[None], (z ^ d, 0, 0))
    half = jnp.zeros((middle,) + plane.shape, part.dtype)
    for d in range(middle):
        piece = plane if d == 0 else swap(plane, d * 2)
        half = lax.dynamic_update_slice(half, piece[None], (m ^ d, 0, 0, 0))
    other = swap(half, 1)
    whole = jnp.zeros((2,) + half.shape, part.dtype)
    whole = lax.dynamic_update_slice(whole, half[None], (c, 0, 0, 0, 0))
    whole = lax.dynamic_update_slice(whole, other[None], (1 - c, 0, 0, 0, 0))
    return whole.transpose(2, 1, 0, 3, 4).reshape(-1, part.shape[1])


def scattered(part):
    return lax.psum_scatter(part, AXES, scatter_dimension=0, tiled=True).astype(F32)


def pick(array, index, axis):
    return lax.dynamic_index_in_dim(array, index, axis, keepdims=False)


class SteppedSum:
    def __init__(self, part):
        far, middle = sizes()
        self.parts = part.reshape(far, middle, 2, -1, part.shape[1])
        self.step = 0

    def middle_sum(self, index):
        kept, got = self.halves
        return pick(kept, index, 1).astype(F32) + pick(got, index, 1).astype(F32)

    def far_sum(self, index):
        z, m, c = place()
        total = self.middle_own(index)
        for piece in self.arrived:
            total = total + pick(piece, index, 0).astype(F32)
        return total

    def middle_own(self, index):
        z, m, c = place()
        kept, got = self.halves
        return pick(pick(kept, m, 1), index, 0).astype(F32) + pick(
            pick(got, m, 1), index, 0
        ).astype(F32)

    def advance(self, tied):
        far, middle = sizes()
        z, m, c = place()
        self.step += 1
        if self.step == 1:
            out = pick(self.parts, 1 - c, 2)
            tied, out = lax.optimization_barrier((tied, out))
            self.halves = (pick(self.parts, c, 2), swap(out, 1))
        elif self.step == 2:
            out = [self.middle_sum(m ^ d).astype(BF16) for d in range(1, middle)]
            tied, out = lax.optimization_barrier((tied, out))
            self.arrived = [swap(item, d * 2) for d, item in zip(range(1, middle), out)]
        else:
            out = [self.far_sum(z ^ d).astype(BF16) for d in range(1, far)]
            tied, out = lax.optimization_barrier((tied, out))
            self.last = [swap(item, d * 2 * middle) for d, item in zip(range(1, far), out)]
        return tied

    def result(self):
        z, m, c = place()
        total = self.far_sum(z)
        for piece in self.last:
            total = total + piece.astype(F32)
        return total


def table_rows(table):
    rows = table.reshape(PAIRS, 2, SPAN * SPAN).transpose(2, 0, 1)
    return jnp.repeat(rows, BLK, axis=2)


def layer_forward(hidden, low_ext, head, vec, flags, keep, temper, pos, between):
    z = (vec["logits"] + vec["jitter"]).reshape(HEADS, SPAN, SPAN) / temper[:, None, None]
    relaxed = jax.nn.sigmoid(z)
    factor = table_rows(relaxed)
    q, q_t, k, k_t, v, v_t = project(low_ext, head, vec["qb"][None], vec["vb"][None])
    ctx_t, lse = attend(flags, keep, pos, factor, q_t, k, v_t)
    ctx_t, wo, wo_at, w12 = between(ctx_t)
    names = ("ob", "g1", "s1", "b2", "g2", "s2", "s2", "s2")
    vectors = jnp.stack([vec[name] for name in names])
    first, normed_low, active, slope, second, result, result_low = ffn(
        ctx_t, hidden, wo, wo_at, w12, vectors, vec["b1"][None]
    )
    record = (low_ext, q, q_t, k, k_t, v, ctx_t, lse, first, normed_low, active, slope, second)
    return result, result_low, record + (relaxed, factor, vectors, head, wo, wo_at, w12)


def layer_backward(grad, record, flags, keep, temper, pos, before=None, done=None):
    low_ext, q, q_t, k, k_t, v, ctx_t, lse, first, normed_low, active, slope, second = record[:13]
    relaxed, factor, vectors, head, wo, wo_at, w12 = record[13:]
    rows = first.shape[0]
    rim = RIM * BLK
    if before is not None:
        grad = before.advance(grad)
    douter, dinner, dfirst, dattend, dc, dc_t, row_sums, b1_sum = ffn_back(
        grad, second, first, slope, w12, wo, wo_at, vectors
    )
    ffn_part = ffn_grads(normed_low, dinner, active, douter, ctx_t, dattend, row_sums, b1_sum)
    if before is None:
        dc, ffn_part = lax.optimization_barrier((dc, ffn_part))
        ffn_sum = scattered(ffn_part)
    else:
        dc, done = lax.optimization_barrier((dc, done))
        dc = before.advance(dc)
        ffn_sum = SteppedSum(ffn_part)
        dc = ffn_sum.advance(dc)
        dc = before.advance(dc)
        dc = ffn_sum.advance(dc)
    dq_t, dk, dv, dr = attend_back(
        flags, keep, pos, jnp.log2(factor), 1.0 / factor, q_t, q, dc_t, dc, ctx_t, lse, k, k_t, v
    )
    drelaxed = dr[:, :PAIRS].reshape(SPAN * SPAN, HEADS, HD).sum(-1).T.reshape(HEADS, SPAN, SPAN)
    logit_grad = (drelaxed * (1.0 - relaxed) / temper[:, None, None]).reshape(1, -1)
    if before is None:
        own, rims = input_back(dk, dv, dq_t, dfirst, head)
        from_lower, from_upper = neighbours(rims[rim:], rims[:rim])
        dq_t, rims = lax.optimization_barrier((dq_t, rims))
        att_sum = SteppedSum(att_grads(low_ext, dq_t, dk, dv, logit_grad))
    else:
        att_sum = SteppedSum(att_grads(low_ext, dq_t, dk, dv, logit_grad))
        dk = att_sum.advance(dk)
        dk = ffn_sum.advance(dk)
        own, rims = input_back(dk, dv, dq_t, dfirst, head)
        own = att_sum.advance(own)
        from_lower, from_upper = neighbours(rims[rim:], rims[:rim])
        own = att_sum.advance(own)
    dhidden = own.at[:rim].add(from_lower.astype(F32))
    dhidden = dhidden.at[rows - rim :].add(from_upper.astype(F32))
    return dhidden, ffn_sum, att_sum, done


def per_device(
    embedded,
    opening,
    selector,
    wq,
    wk,
    wv,
    wo,
    qb,
    vb,
    ob,
    g1,
    s1,
    w1,
    b1,
    w2,
    b2,
    g2,
    s2,
    scores,
    jitter,
    warmth,
    upstream,
):
    share = wq.shape[1]
    devices = D // share
    flags = opening[0]
    pos = lax.axis_index("dp").reshape(1).astype(jnp.int32)
    rim = RIM * BLK

    def widened(part):
        lead = part.shape[:-1]
        return jnp.swapaxes(part.reshape(lead + (devices, 4, share)), -3, -2).reshape(lead + (FF,))

    def unwidened(part):
        lead = part.shape[:-1]
        return jnp.swapaxes(part.reshape(lead + (4, devices, share)), -3, -2).reshape(lead + (FF,))

    def own_parts(tier):
        narrow = w2[tier].reshape(4, share, D)
        vectors = jnp.stack(
            [item[tier] for item in (qb, vb, ob, g1, s1, b2, g2, s2, scores, jitter)]
            + [b1[tier].reshape(4, share)[j] for j in range(4)],
            1,
        )
        vectors = jnp.pad(vectors, ((0, 0), (0, 128 - vectors.shape[1])))
        first = [wq[tier], wk[tier], wv[tier]]
        wide = [widened(w1[tier])] + [narrow[j] for j in range(4)]
        return first, wide, [wo[tier]], [vectors]

    def unpacked(columns):
        columns = jnp.transpose(columns.astype(F32))
        names = ("qb", "vb", "ob", "g1", "s1", "b2", "g2", "s2", "logits", "jitter")
        vec = {name: columns[n] for n, name in enumerate(names)}
        vec["b1"] = columns[len(names) : len(names) + 4].reshape(FF)
        return vec

    symbols = embedded[0]
    lower, upper = neighbours(symbols[symbols.shape[0] - rim :], symbols[:rim])
    low_ext = jnp.concatenate([lower, symbols, upper], 0)
    first, wide, out, vectors = own_parts(0)
    head_zero = gathered_in_steps(jnp.concatenate(first + vectors, 1))
    head_zero, *rest = lax.optimization_barrier((head_zero, *wide, *out))
    tail_zero = gathered(jnp.concatenate(rest, 1))
    later = {}

    def between_zero(ctx_t):
        first, wide, out, vectors = own_parts(1)
        ctx_t, tail, *parts = lax.optimization_barrier(
            (ctx_t, tail_zero, *first, *out, *vectors, *wide)
        )
        later["head"] = gathered_in_steps(jnp.concatenate(parts[:5], 1))
        later["tail"] = gathered(jnp.concatenate(parts[5:], 1))
        return ctx_t, tail, 2 * FF // D, tail

    def between_one(ctx_t):
        return ctx_t, later["head"], 3, later["tail"]

    hidden, low, record = layer_forward(
        symbols,
        low_ext,
        head_zero,
        unpacked(head_zero[:, 3 * D :]),
        flags,
        selector[0, 0],
        warmth[0],
        pos,
        between_zero,
    )
    records = [record]
    lower, upper = neighbours(low[low.shape[0] - rim :], low[:rim])
    low_ext = jnp.concatenate([lower, low, upper], 0)
    hidden, _, record = layer_forward(
        hidden,
        low_ext,
        later["head"],
        unpacked(later["head"][:, 4 * D :]),
        flags,
        selector[1, 0],
        warmth[1],
        pos,
        between_one,
    )
    records.append(record)
    grad = upstream[0]
    grad, ffn_one, att_one, _ = layer_backward(
        grad, records[1], flags, selector[1, 0], warmth[1], pos
    )
    grad, ffn_zero, att_zero, ffn_one = layer_backward(
        grad, records[0], flags, selector[0, 0], warmth[0], pos, att_one, ffn_one
    )
    sums = jnp.stack(
        [
            jnp.concatenate([ffn_zero.result(), att_zero.result()], 1),
            jnp.concatenate([ffn_one, att_one.result()], 1),
        ]
    )
    w1_grad = unwidened(sums[:, :, :FF])
    w2_grad = jnp.concatenate([sums[:, :, FF + j * D : FF + (j + 1) * D] for j in range(4)], 1)
    wo_grad = sums[:, :, 2 * FF : 2 * FF + D]
    fv = sums[:, :, 2 * FF + D : 2 * FF + D + 128]
    att = sums[:, :, 2 * FF + D + 128 :]
    av = att[:, :, 3 * D :]
    b1_grad = jnp.concatenate([fv[:, :, 8 + j] for j in range(4)], 1)
    new_mask = (scores.astype(F32) + jitter.astype(F32) > 0).astype(jnp.int32)
    return (
        hidden[None],
        grad[None],
        att[:, :, :D],
        att[:, :, D : 2 * D],
        att[:, :, 2 * D : 3 * D],
        wo_grad,
        av[:, :, 2],
        av[:, :, 0],
        fv[:, :, 5],
        fv[:, :, 3],
        fv[:, :, 4],
        w1_grad,
        b1_grad,
        w2_grad,
        fv[:, :, 2],
        fv[:, :, 0],
        fv[:, :, 1],
        av[:, :, 1],
        new_mask,
    )


def solution(mesh):
    rows = P("mp", "dp", None)
    matrix = P(None, AXES, None)
    vector = P(None, AXES)
    return jax.shard_map(
        per_device,
        mesh=mesh,
        in_specs=(rows, P("mp", None), P(None, "mp", "dp", None))
        + (matrix,) * 4
        + (vector,) * 5
        + (matrix, vector, matrix)
        + (vector,) * 5
        + (P(), rows),
        out_specs=(rows, rows)
        + (matrix,) * 4
        + (vector,) * 5
        + (matrix, vector, matrix)
        + (vector,) * 5,
        check_vma=False,
    )
```

time: 5740 us -> 863 us (0.15)
  local copies, waits for them, and re-layouts: 1900 us -> 106 us
  matrix products: 1390 us -> 0 us
  waiting for transfers between devices: 1580 us -> 258 us
  other arithmetic: 481 us -> 42.8 us
  Pallas kernels: 0 us -> 294 us
  loops' own time: 264 us -> 0 us
  starting transfers between devices: 27.9 us -> 139 us
    dot_general x385 -> x0, matrix products: 1380 us -> none  [the longest x156 553 us: contract_cols(): lax.dot_general(left, right, (((1,), (1,)), ((), ())), preferred_element_...]
    reduce_scatter x6 -> x0, waiting for transfers between devices: 765 us -> none  [the longest x2 280 us: scatter_each(): lax.psum_scatter(grad_inner, ('dp', 'mp'), scatter_dimension=0, tiled=True)]
    unnamed x32 -> x4, waiting for transfers between devices: 570 us -> 6.85 us
    mul x432 -> x0, local copies, waits for them, and re-layouts: 485 us -> none  [the longest x192 199 us: forward_one_head(): expo / total * factor]
    reshape x102 -> x8, local copies, waits for them, and re-layouts: 471 us -> 15.3 us  [the longest x1 5.78 us: unwidened(): jnp.swapaxes(part.reshape(lead + (4, devices, share)), -3, -2)]
    pallas_call x0 -> x16, Pallas kernels: none -> 294 us  [the longest x2 59.6 us: attend_back(): pl.pallas_call(backward_kernel, out_shape=(jax.ShapeDtypeStruct(q_t.shape...]
    reduce_sum x116 -> x2, other arithmetic: 286 us -> 2.08 us  [layer_backward(): dr[:, :PAIRS].reshape(SPAN * SPAN, HEADS, HD).sum(-1)]
    broadcast_in_dim x481 -> x8, local copies, waits for them, and re-layouts: 276 us -> 3.72 us  [the longest x2 2.4 us: gathered_in_steps(): whole = jnp.zeros((2,) + half.shape, part.dtype)]
  transfers between devices with their start and end apart: 33 -> 46, of which waited for: 17 -> 21; matrix products, arithmetic and copies ran while one was open for 22% -> 9% of each run, Pallas kernels for 0% -> 26%
where the time goes in v1:
time: 863 us; the launch traced here: 855 us
  Pallas kernels  294 us (34%)
  waiting for transfers between devices  258 us (30%)
  starting transfers between devices  139 us (16%)
  local copies, waits for them, and re-layouts  106 us (12%)
  other arithmetic  42.8 us (5%)
  between operations  15.6 us (2%)
    ppermute x35, waiting for transfers between devices, swap(): return lax.ppermute(block, AXES, [(i, i ^ mask) for i in range(count)])  143 us
    ppermute x35, starting transfers between devices, swap(): return lax.ppermute(block, AXES, [(i, i ^ mask) for i in range(count)])  104 us
    ppermute x4, waiting for transfers between devices, neighbours(): lax.ppermute(tail, 'dp', [(i, i + 1) for i in range(count - 1)])  63.5 us
    pallas_call x2, Pallas kernels, attend_back(): pl.pallas_call(backward_kernel, out_shape=(jax.ShapeDtypeStruct(q_t.shape...  59.6 us
    pallas_call x2, Pallas kernels, ffn(): pl.pallas_call(ffn_kernel, grid=(n // ROWS,), in_specs=[pl.BlockSpec((D,...  56.3 us
    pallas_call x2, Pallas kernels, ffn_back(): pl.pallas_call(ffn_back_kernel, grid=(n // ROWS,), in_specs=[row(D), row(...  46.3 us
    pallas_call x2, Pallas kernels, ffn_grads(): pl.pallas_call(ffn_grads_kernel, grid=(2 * blocks + 2,), in_specs=[once((...  41.3 us
    unnamed x165, local copies, waits for them, and re-layouts  34.9 us
  transfers between devices with their start and end apart: 46, of which 21 were waited for; matrix products, arithmetic and copies ran while one was open for 9% of the time, Pallas kernels for 26%

profile of v1, /device:TPU:0, one launch (start us, length us, event | category | flops | bytes accessed | tf_op | source)
XLA Modules:
  0.0 854.9 jit_solution(12163108581390272681)
XLA Ops:
  78.8 31.2 %collective-permute-done.7 = bf16[512,768]{1,0:T(8,128)(2,1)} collective-permute-done((bf16[512,768]{1,0:T(8,128)(2,1)}, bf16[512,768]{1,0:T(8,128)(2,1)}, u32[]{:S(2)}, u32[]{:S(2)}) %collective-permute-start.7) | collective-permute-done | bytes 786464 | tf_op jit(solution)/shard_map/ppermute | solution.py:567
  117.0 13.2 %project.2 = (bf16[1024,768]{1,0:T(8,128)(2,1)S(1)}, bf16[768,1024]{1,0:T(8,128)(2,1)S(1)}, bf16[2048,768]{1,0:T(8,128)(2,1)S(1)}, bf16[768,2048]{1,0:T(8,128)(2...) custom-call(bf16[2048,768]{1,0:T(8,128)(2,1)} %pad_maximum_fusion.low, bf16[768,2432]{1,0:T(8,128)(2,1)} %bitcast.36.w, ...), custom_call_target="tpu_custom_call" | custom-call | flops 14000000000 | bytes 1000000 | tf_op jit(solution)/shard_map/project/pallas_call | solution.py:476
  149.9 24.2 %all-gather.3.cloned.1.call-done.wo.w1.w2 = bf16[768,6912]{1,0:T(8,128)(2,1)} async-done(((bf16[24,6912]{1,0:T(8,128)(2,1)}), bf16[768,6912]{1,0:T(8,128)(2,1)}) %all-gather.3.cloned.1.call-update) | async-done | bytes 10616848 | tf_op jit(solution)/shard_map/all_gather | solution.py:573
  200.3 17.6 %collective-permute-done.12 = bf16[4,24,3200]{2,1,0:T(8,128)(2,1)S(1)} collective-permute-done((bf16[4,24,3200]{2,1,0:T(8,128)(2,1)S(1)}, bf16[4,24,3200]{2,1,0:T(8,128)(2,1)S(1)}, u32[]{:S(2)}, u32[]{:S(2)}) %collective-permute-start.12) | collective-permute-done | bytes 614432 | tf_op jit(solution)/shard_map/ppermute | solution.py:588
  218.7 13.1 %collective-permute-done.14 = bf16[4,24,3200]{2,1,0:T(8,128)(2,1)S(1)} collective-permute-done((bf16[4,24,3200]{2,1,0:T(8,128)(2,1)S(1)}, bf16[4,24,3200]{2,1,0:T(8,128)(2,1)S(1)}, u32[]{:S(2)}, u32[]{:S(2)}) %collective-permute-start.14) | collective-permute-done | bytes 614432 | tf_op jit(solution)/shard_map/ppermute | solution.py:588
  232.0 28.1 %ffn.2 = (f32[1024,768]{1,0:T(8,128)}, bf16[1024,768]{1,0:T(8,128)(2,1)}, bf16[1024,3072]{1,0:T(8,128)(2,1)}, bf16[1024,3072]{1,0:T(8,128)(2,1)}, f32[1024,768]{...) custom-call(f32[768,1024]{1,0:T(8,128)} %copy-done.5, bf16[1024,768]{1,0:T(8,128)(2,1)} %bitcast.478, ...), custom_call_target="tpu_custom_call" | custom-call | flops 28000000000 | bytes 1000000 | tf_op jit(solution)/shard_map/ffn/pallas_call | solution.py:345
  266.1 32.2 %collective-permute-done.16 = bf16[512,768]{1,0:T(8,128)(2,1)S(1)} collective-permute-done((bf16[512,768]{1,0:T(8,128)(2,1)S(1)}, bf16[512,768]{1,0:T(8,128)(2,1)S(1)}, u32[]{:S(2)}, u32[]{:S(2)}) %collective-permute-start.16) | collective-permute-done | bytes 786464 | tf_op jit(solution)/shard_map/ppermute | solution.py:567
  308.2 13.3 %project.3 = (bf16[1024,768]{1,0:T(8,128)(2,1)S(1)}, bf16[768,1024]{1,0:T(8,128)(2,1)S(1)}, bf16[2048,768]{1,0:T(8,128)(2,1)S(1)}, bf16[768,2048]{1,0:T(8,128)(2...) custom-call(bf16[2048,768]{1,0:T(8,128)(2,1)} %constant_dynamic-update-slice_fusion.11.low, ...), custom_call_target="tpu_custom_call" | custom-call | flops 14000000000 | bytes 1000000 | tf_op jit(solution)/shard_map/project/pallas_call | solution.py:476
  341.1 28.2 %ffn.3 = (f32[1024,768]{1,0:T(8,128)}, bf16[1024,768]{1,0:T(8,128)(2,1)}, bf16[1024,3072]{1,0:T(8,128)(2,1)}, bf16[1024,3072]{1,0:T(8,128)(2,1)}, f32[1024,768]{...) custom-call(f32[768,1024]{1,0:T(8,128)} %copy-done.9, f32[1024,768]{1,0:T(8,128)} %get-tuple-element.201.hidden, ...), custom_call_target="tpu_custom_call" | custom-call | flops 28000000000 | bytes 1000000 | tf_op jit(solution)/shard_map/ffn/pallas_call | solution.py:345
  369.3 23.2 %ffn_back.2 = (bf16[1024,768]{1,0:T(8,128)(2,1)}, bf16[1024,3072]{1,0:T(8,128)(2,1)}, f32[1024,768]{1,0:T(8,128)}, bf16[1024,768]{1,0:T(8,128)(2,1)}, bf16[1024,...) custom-call(bf16[1024,768]{1,0:T(8,128)(2,1)} %bitcast.505, ...), custom_call_target="tpu_custom_call" | custom-call | flops 23000000512 | bytes 1000000 | tf_op jit(solution)/shard_map/ffn_back/pallas_call | solution.py:395
  392.5 20.6 %ffn_grads.2 = bf16[768,7040]{1,0:T(8,128)(2,1)} custom-call(bf16[1024,768]{1,0:T(8,128)(2,1)} %get-tuple-element.215.normed, bf16[1024,3072]{1,0:T(8,128)(2,1)} %get-tuple-element.216.dinner, bf16[1024,3072]{1,0:T(8,128)(2,1)} %get-tuple-element.217.active, bf16[1024,768]{1,0:T(8,128)(2,1)} %get-tuple-element.218.douter, f32[768,1024]{1,0:T(8,128)} %copy-done.9, ...), custom_call_target="tpu_custom_call" | custom-call | flops 20000000000 | bytes 1000000 | tf_op jit(solution)/shard_map/ffn_grads/pallas_call | solution.py:431
  415.8 30.5 %attend_back.2 = (bf16[768,1024]{1,0:T(8,128)(2,1)}, bf16[2048,768]{1,0:T(8,128)(2,1)}, bf16[2048,768]{1,0:T(8,128)(2,1)}, f32[64,8,128]{2,1,0:T(8,128)}) custom-call(s32[64]{0:T(128)} %bitcast.469, s32[8,15]{1,0:T(8,128)} %copy-done.17, s32[1]{0:T(128)} %bitcast.2.pos, f32[64,6,256]{2,1,0:T(8,128)} %copy_multiply_fusion.log_factor, ...), custom_call_target="tpu_custom_call" | custom-call | flops 5000000000 | bytes 1000000 | tf_op jit(solution)/shard_map/attend_back/pallas_call | solution.py:276
  457.4 11.6 %input_back.2 = (f32[1024,768]{1,0:T(8,128)S(1)}, bf16[1024,768]{1,0:T(8,128)(2,1)S(1)}) custom-call(bf16[2048,768]{1,0:T(8,128)(2,1)S(1)} %copy-done.21, bf16[2048,768]{1,0:T(8,128)(2,1)S(1)} %copy-done.22, bf16[768,1024]{1,0:T(8,128)(2,1)S(1)} %copy-done.25, f32[1024,768]{1,0:T(8,128)} %get-tuple-element.229.dfirst, bf16[768,3200]{1,0:T(8,128)(2,1)} %bitcast.484), custom_call_target="tpu_custom_call" | custom-call | flops 12000000000 | bytes 1000000 | tf_op jit(solution)/shard_map/input_back/pallas_call | solution.py:552
  469.1 21.3 %collective-permute-start.18 = (bf16[512,768]{1,0:T(8,128)(2,1)S(1)}, bf16[512,768]{1,0:T(8,128)(2,1)S(1)}, u32[]{:S(2)}, u32[]{:S(2)}) collective-permute-start(bf16[512,768]{1,0:T(8,128)(2,1)S(1)} %get-tuple-element.333), channel_id=1, source_target_pairs={{0,4},{4,8},{8,12},{12,16},{16,20},{20,24},{24,28},{1,5},{5,9},{9,... | collective-permute-start | bytes 2359304 | tf_op jit(solution)/shard_map/ppermute | solution.py:567
  491.8 12.6 %att_grads.2 = bf16[768,2432]{1,0:T(8,128)(2,1)} custom-call(bf16[2048,768]{1,0:T(8,128)(2,1)} %constant_dynamic-update-slice_fusion.11.low, bf16[768,1024]{1,0:T(8,128)(2,1)S(1)} %copy-done.26, bf16[2048,768]{1,0:T(8,128)(2,1)} %get-tuple-element.226.dk, bf16[2048,768]{1,0:T(8,128)(2,1)} %get-tuple-element.227.dv, f32[1,768]{1,0:T(1,128)S(1)} %copy.215.logit), custom_call_target="tpu_custom_call" | custom-call | flops 12000000000 | bytes 1000000 | tf_op jit(solution)/shard_map/att_grads/pallas_call | solution.py:516
  507.6 20.3 %collective-permute-done.19 = bf16[512,768]{1,0:T(8,128)(2,1)S(1)} collective-permute-done((bf16[512,768]{1,0:T(8,128)(2,1)S(1)}, bf16[512,768]{1,0:T(8,128)(2,1)S(1)}, u32[]{:S(2)}, u32[]{:S(2)}) %collective-permute-start.19) | collective-permute-done | bytes 786464 | tf_op jit(solution)/shard_map/ppermute | solution.py:568
  528.2 13.5 %collective-permute-start.20 = (bf16[4,4,24,2432]{3,2,1,0:T(8,128)(2,1)}, bf16[4,4,24,2432]{3,2,1,0:T(8,128)(2,1)S(1)}, u32[]{:S(2)}, u32[]{:S(2)}) collective-permute-start(bf16[4,4,24,2432]{3,2,1,0:T(8,128)(2,1)} %dynamic-slice_bitcast_fusion.2), channel_id=1, source_target_pairs={{0,1},{1,0},{2,3},{3,2},{4,5},{5,4},{6,7},{7,6},{8,9},{9,8},{10,11... | collective-permute-start | bytes 5603336 | tf_op jit(solution)/shard_map/ppermute | solution.py:588
  541.7 23.1 %ffn_back.3 = (bf16[1024,768]{1,0:T(8,128)(2,1)}, bf16[1024,3072]{1,0:T(8,128)(2,1)}, f32[1024,768]{1,0:T(8,128)}, bf16[1024,768]{1,0:T(8,128)(2,1)}, bf16[1024,...) custom-call(f32[1024,768]{1,0:T(8,128)} %copy-done.1, ...), custom_call_target="tpu_custom_call" | custom-call | flops 23000000512 | bytes 1000000 | tf_op jit(solution)/shard_map/ffn_back/pallas_call | solution.py:395
  564.8 20.8 %ffn_grads.3 = bf16[768,7040]{1,0:T(8,128)(2,1)} custom-call(bf16[1024,768]{1,0:T(8,128)(2,1)} %get-tuple-element.244.normed, bf16[1024,3072]{1,0:T(8,128)(2,1)} %get-tuple-element.245.dinner, bf16[1024,3072]{1,0:T(8,128)(2,1)} %get-tuple-element.246.active, bf16[1024,768]{1,0:T(8,128)(2,1)} %get-tuple-element.247.douter, f32[768,1024]{1,0:T(8,128)} %copy-done.5, ...), custom_call_target="tpu_custom_call" | custom-call | flops 20000000000 | bytes 1000000 | tf_op jit(solution)/shard_map/ffn_grads/pallas_call | solution.py:431
  655.1 29.2 %attend_back.3 = (bf16[768,1024]{1,0:T(8,128)(2,1)}, bf16[2048,768]{1,0:T(8,128)(2,1)}, bf16[2048,768]{1,0:T(8,128)(2,1)}, f32[64,8,128]{2,1,0:T(8,128)}) custom-call(s32[64]{0:T(128)} %bitcast.470, s32[8,15]{1,0:T(8,128)} %copy-done.16, s32[1]{0:T(128)} %bitcast.2.pos, f32[64,6,256]{2,1,0:T(8,128)} %copy_multiply_fusion.1.log_factor, ...), custom_call_target="tpu_custom_call" | custom-call | flops 5000000000 | bytes 1000000 | tf_op jit(solution)/shard_map/attend_back/pallas_call | solution.py:276
  706.3 17.8 %collective-permute-start.28 = (bf16[4,4,24,2432]{3,2,1,0:T(8,128)(2,1)S(1)}, bf16[4,4,24,2432]{3,2,1,0:T(8,128)(2,1)S(1)}, u32[]{:S(2)}, u32[]{:S(2)}) collective-permute-start(bf16[4,4,24,2432]{3,2,1,0:T(8,128)(2,1)S(1)} %dynamic-slice_bitcast_fusion.1), channel_id=1, source_target_pairs={{0,1},{1,0},{2,3},{3,2},{4,5},{5,4},{6,7},{7,6},{8,9},{9,8},{10,11... | collective-permute-start | bytes 5603336 | tf_op jit(solution)/shard_map/ppermute | solution.py:588
  727.7 17.2 %collective-permute-start.35 = (bf16[24,7040]{1,0:T(8,128)(2,1)S(1)}, bf16[24,7040]{1,0:T(8,128)(2,1)S(1)}, u32[]{:S(2)}, u32[]{:S(2)}) collective-permute-start(bf16[24,7040]{1,0:T(8,128)(2,1)S(1)} %get-tuple-element.280), channel_id=1, source_target_pairs={{0,16},{1,17},{2,18},{3,19},{4,20},{5,21},{6,22},{7,23},{8,24},{9,... | collective-permute-start | bytes 1013768 | tf_op jit(solution)/shard_map/ppermute | solution.py:588
  746.2 11.5 %input_back.3 = (f32[1024,768]{1,0:T(8,128)S(1)}, bf16[1024,768]{1,0:T(8,128)(2,1)S(1)}) custom-call(bf16[2048,768]{1,0:T(8,128)(2,1)S(1)} %copy-done.19, bf16[2048,768]{1,0:T(8,128)(2,1)S(1)} %copy-done.20, bf16[768,1024]{1,0:T(8,128)(2,1)S(1)} %copy-done.24, f32[1024,768]{1,0:T(8,128)} %get-tuple-element.270.dfirst, bf16[768,2432]{1,0:T(8,128)(2,1)} %bitcast.36.w), custom_call_target="tpu_custom_call" | custom-call | flops 12000000000 | bytes 1000000 | tf_op jit(solution)/shard_map/input_back/pallas_call | solution.py:552
  776.7 36.3 %collective-permute-done.30 = bf16[4,24,2432]{2,1,0:T(8,128)(2,1)S(1)} collective-permute-done((bf16[4,24,2432]{2,1,0:T(8,128)(2,1)S(1)}, bf16[4,24,2432]{2,1,0:T(8,128)(2,1)S(1)}, u32[]{:S(2)}, u32[]{:S(2)}) %collective-permute-start.30) | collective-permute-done | bytes 466976 | tf_op jit(solution)/shard_map/ppermute | solution.py:588
  (391 shorter events, 328.9 us)
Async XLA Ops:
  7.2 166.8 %all-gather.3.cloned.1.call-start = ((), (), s32[]{:S(2)}) async-start(), calls=%async_computation.1 | async-start | bytes 10948608 | tf_op jit(solution)/shard_map/all_gather | solution.py:573
  68.2 272.9 %all-gather.5.cloned.1.call-start = ((), (), s32[]{:S(2)}) async-start(), calls=%async_computation.2 | async-start | bytes 9732096 | tf_op jit(solution)/shard_map/all_gather | solution.py:573
  69.5 40.5 %collective-permute-start.7 = (bf16[512,768]{1,0:T(8,128)(2,1)}, bf16[512,768]{1,0:T(8,128)(2,1)}, u32[]{:S(2)}, u32[]{:S(2)}) collective-permute-start(bf16[512,768]{1,0:T(8,128)(2,1)} %get-tuple-element.336), channel_id=1, source_target_pairs={{0,4},{4,8},{8,12},{12,16},{16,20},{20,24},{24,28},{1,5},{5,9},{9,... | collective-permute-start | bytes 2359304 | tf_op jit(solution)/shard_map/ppermute | solution.py:567
  73.9 36.1 %collective-permute-start.8 = (bf16[512,768]{1,0:T(8,128)(2,1)}, bf16[512,768]{1,0:T(8,128)(2,1)}, u32[]{:S(2)}, u32[]{:S(2)}) collective-permute-start(bf16[512,768]{1,0:T(8,128)(2,1)} %get-tuple-element.337), channel_id=1, source_target_pairs={{4,0},{8,4},{12,8},{16,12},{20,16},{24,20},{28,24},{5,1},{9,5},{13... | collective-permute-start | bytes 2359304 | tf_op jit(solution)/shard_map/ppermute | solution.py:568
  174.9 425.5 %reduce-scatter.4.cloned.1.call-start = ((), (), s32[]{:S(2)}) async-start(), calls=%async_computation.3 | async-start | bytes 11151360
  198.6 33.2 %collective-permute-start.14 = (bf16[4,24,3200]{2,1,0:T(8,128)(2,1)S(1)}, bf16[4,24,3200]{2,1,0:T(8,128)(2,1)S(1)}, u32[]{:S(2)}, u32[]{:S(2)}) collective-permute-start(bf16[4,24,3200]{2,1,0:T(8,128)(2,1)S(1)} %bitcast_dynamic-update-slice_fusion.12), channel_id=1, source_target_pairs={{0,6},{1,7},{2,4},{3,5},{4,2},{5,3},{6,0},{7,1},{8,14},{9,15},{10,... | collective-permute-start | bytes 1843208 | tf_op jit(solution)/shard_map/ppermute | solution.py:588
  231.9 69.6 %collective-permute-start.15 = (bf16[4,4,24,3200]{3,2,0,1:T(8,128)(2,1)S(1)}, bf16[4,4,24,3200]{3,2,0,1:T(8,128)(2,1)S(1)}, u32[]{:S(2)}, u32[]{:S(2)}) collective-permute-start(bf16[4,4,24,3200]{3,2,0,1:T(8,128)(2,1)S(1)} %bitcast_dynamic-update-slice_fusion.7), channel_id=1, source_target_pairs={{0,1},{1,0},{2,3},{3,2},{4,5},{5,4},{6,7},{7,6},{8,9},{9,8},{10,11... | collective-permute-start | bytes 7372808 | tf_op jit(solution)/shard_map/ppermute | solution.py:588
  261.6 36.7 %collective-permute-start.16 = (bf16[512,768]{1,0:T(8,128)(2,1)S(1)}, bf16[512,768]{1,0:T(8,128)(2,1)S(1)}, u32[]{:S(2)}, u32[]{:S(2)}) collective-permute-start(bf16[512,768]{1,0:T(8,128)(2,1)S(1)} %get-tuple-element.335), channel_id=1, source_target_pairs={{0,4},{4,8},{8,12},{12,16},{16,20},{20,24},{24,28},{1,5},{5,9},{9,... | collective-permute-start | bytes 2359304 | tf_op jit(solution)/shard_map/ppermute | solution.py:567
  264.1 36.4 %collective-permute-start.17 = (bf16[512,768]{1,0:T(8,128)(2,1)S(1)}, bf16[512,768]{1,0:T(8,128)(2,1)S(1)}, u32[]{:S(2)}, u32[]{:S(2)}) collective-permute-start(bf16[512,768]{1,0:T(8,128)(2,1)S(1)} %get-tuple-element.334), channel_id=1, source_target_pairs={{4,0},{8,4},{12,8},{16,12},{20,16},{24,20},{28,24},{5,1},{9,5},{13... | collective-permute-start | bytes 2359304 | tf_op jit(solution)/shard_map/ppermute | solution.py:568
  469.1 38.1 %collective-permute-start.18 = (bf16[512,768]{1,0:T(8,128)(2,1)S(1)}, bf16[512,768]{1,0:T(8,128)(2,1)S(1)}, u32[]{:S(2)}, u32[]{:S(2)}) collective-permute-start(bf16[512,768]{1,0:T(8,128)(2,1)S(1)} %get-tuple-element.333), channel_id=1, source_target_pairs={{0,4},{4,8},{8,12},{12,16},{16,20},{20,24},{24,28},{1,5},{5,9},{9,... | collective-permute-start | bytes 2359304 | tf_op jit(solution)/shard_map/ppermute | solution.py:567
  490.5 37.4 %collective-permute-start.19 = (bf16[512,768]{1,0:T(8,128)(2,1)S(1)}, bf16[512,768]{1,0:T(8,128)(2,1)S(1)}, u32[]{:S(2)}, u32[]{:S(2)}) collective-permute-start(bf16[512,768]{1,0:T(8,128)(2,1)S(1)} %get-tuple-element.332), channel_id=1, source_target_pairs={{4,0},{8,4},{12,8},{16,12},{20,16},{24,20},{28,24},{5,1},{9,5},{13... | collective-permute-start | bytes 2359304 | tf_op jit(solution)/shard_map/ppermute | solution.py:568
  528.2 62.6 %collective-permute-start.20 = (bf16[4,4,24,2432]{3,2,1,0:T(8,128)(2,1)}, bf16[4,4,24,2432]{3,2,1,0:T(8,128)(2,1)S(1)}, u32[]{:S(2)}, u32[]{:S(2)}) collective-permute-start(bf16[4,4,24,2432]{3,2,1,0:T(8,128)(2,1)} %dynamic-slice_bitcast_fusion.2), channel_id=1, source_target_pairs={{0,1},{1,0},{2,3},{3,2},{4,5},{5,4},{6,7},{7,6},{8,9},{9,8},{10,11... | collective-permute-start | bytes 5603336 | tf_op jit(solution)/shard_map/ppermute | solution.py:588
  601.4 44.4 %collective-permute-start.24 = (bf16[4,4,24,7040]{3,2,1,0:T(8,128)(2,1)}, bf16[4,4,24,7040]{3,2,1,0:T(8,128)(2,1)}, u32[]{:S(2)}, u32[]{:S(2)}) collective-permute-start(bf16[4,4,24,7040]{3,2,1,0:T(8,128)(2,1)} %dynamic-slice_bitcast_fusion), channel_id=1, source_target_pairs={{0,1},{1,0},{2,3},{3,2},{4,5},{5,4},{6,7},{7,6},{8,9},{9,8},{10,11... | collective-permute-start | bytes 16220168 | tf_op jit(solution)/shard_map/ppermute | solution.py:588
  651.6 72.5 %collective-permute-start.25 = (bf16[4,24,7040]{2,1,0:T(8,128)(2,1)}, bf16[4,24,7040]{2,1,0:T(8,128)(2,1)}, u32[]{:S(2)}, u32[]{:S(2)}) collective-permute-start(bf16[4,24,7040]{2,1,0:T(8,128)(2,1)} %get-tuple-element.266), channel_id=1, source_target_pairs={{0,2},{1,3},{2,0},{3,1},{4,6},{5,7},{6,4},{7,5},{8,10},{9,11},{10,... | collective-permute-start | bytes 4055048 | tf_op jit(solution)/shard_map/ppermute | solution.py:588
  652.3 71.8 %collective-permute-start.26 = (bf16[4,24,7040]{2,1,0:T(8,128)(2,1)}, bf16[4,24,7040]{2,1,0:T(8,128)(2,1)}, u32[]{:S(2)}, u32[]{:S(2)}) collective-permute-start(bf16[4,24,7040]{2,1,0:T(8,128)(2,1)} %get-tuple-element.267), channel_id=1, source_target_pairs={{0,4},{1,5},{2,6},{3,7},{4,0},{5,1},{6,2},{7,3},{8,12},{9,13},{10,... | collective-permute-start | bytes 4055048 | tf_op jit(solution)/shard_map/ppermute | solution.py:588
  653.6 70.5 %collective-permute-start.27 = (bf16[4,24,7040]{2,1,0:T(8,128)(2,1)}, bf16[4,24,7040]{2,1,0:T(8,128)(2,1)}, u32[]{:S(2)}, u32[]{:S(2)}) collective-permute-start(bf16[4,24,7040]{2,1,0:T(8,128)(2,1)} %get-tuple-element.268), channel_id=1, source_target_pairs={{0,6},{1,7},{2,4},{3,5},{4,2},{5,3},{6,0},{7,1},{8,14},{9,15},{10,... | collective-permute-start | bytes 4055048 | tf_op jit(solution)/shard_map/ppermute | solution.py:588
  706.3 52.8 %collective-permute-start.28 = (bf16[4,4,24,2432]{3,2,1,0:T(8,128)(2,1)S(1)}, bf16[4,4,24,2432]{3,2,1,0:T(8,128)(2,1)S(1)}, u32[]{:S(2)}, u32[]{:S(2)}) collective-permute-start(bf16[4,4,24,2432]{3,2,1,0:T(8,128)(2,1)S(1)} %dynamic-slice_bitcast_fusion.1), channel_id=1, source_target_pairs={{0,1},{1,0},{2,3},{3,2},{4,5},{5,4},{6,7},{7,6},{8,9},{9,8},{10,11... | collective-permute-start | bytes 5603336 | tf_op jit(solution)/shard_map/ppermute | solution.py:588
  727.2 33.7 %collective-permute-start.34 = (bf16[24,7040]{1,0:T(8,128)(2,1)S(1)}, bf16[24,7040]{1,0:T(8,128)(2,1)S(1)}, u32[]{:S(2)}, u32[]{:S(2)}) collective-permute-start(bf16[24,7040]{1,0:T(8,128)(2,1)S(1)} %get-tuple-element.279), channel_id=1, source_target_pairs={{0,8},{1,9},{2,10},{3,11},{4,12},{5,13},{6,14},{7,15},{8,0},{9,1},... | collective-permute-start | bytes 1013768 | tf_op jit(solution)/shard_map/ppermute | solution.py:588
  727.7 36.8 %collective-permute-start.35 = (bf16[24,7040]{1,0:T(8,128)(2,1)S(1)}, bf16[24,7040]{1,0:T(8,128)(2,1)S(1)}, u32[]{:S(2)}, u32[]{:S(2)}) collective-permute-start(bf16[24,7040]{1,0:T(8,128)(2,1)S(1)} %get-tuple-element.280), channel_id=1, source_target_pairs={{0,16},{1,17},{2,18},{3,19},{4,20},{5,21},{6,22},{7,23},{8,24},{9,... | collective-permute-start | bytes 1013768 | tf_op jit(solution)/shard_map/ppermute | solution.py:588
  744.8 24.7 %collective-permute-start.36 = (bf16[24,7040]{1,0:T(8,128)(2,1)S(1)}, bf16[24,7040]{1,0:T(8,128)(2,1)S(1)}, u32[]{:S(2)}, u32[]{:S(2)}) collective-permute-start(bf16[24,7040]{1,0:T(8,128)(2,1)S(1)} %get-tuple-element.281), channel_id=1, source_target_pairs={{0,24},{1,25},{2,26},{3,27},{4,28},{5,29},{6,30},{7,31},{8,16},{9,... | collective-permute-start | bytes 1013768 | tf_op jit(solution)/shard_map/ppermute | solution.py:588
  757.8 64.2 %collective-permute-start.32 = (bf16[512,768]{1,0:T(8,128)(2,1)S(1)}, bf16[512,768]{1,0:T(8,128)(2,1)S(1)}, u32[]{:S(2)}, u32[]{:S(2)}) collective-permute-start(bf16[512,768]{1,0:T(8,128)(2,1)S(1)} %get-tuple-element.331), channel_id=1, source_target_pairs={{0,4},{4,8},{8,12},{12,16},{16,20},{20,24},{24,28},{1,5},{5,9},{9,... | collective-permute-start | bytes 2359304 | tf_op jit(solution)/shard_map/ppermute | solution.py:567
  759.2 63.4 %collective-permute-start.33 = (bf16[512,768]{1,0:T(8,128)(2,1)S(1)}, bf16[512,768]{1,0:T(8,128)(2,1)S(1)}, u32[]{:S(2)}, u32[]{:S(2)}) collective-permute-start(bf16[512,768]{1,0:T(8,128)(2,1)S(1)} %get-tuple-element.330), channel_id=1, source_target_pairs={{4,0},{8,4},{12,8},{16,12},{20,16},{24,20},{28,24},{5,1},{9,5},{13... | collective-permute-start | bytes 2359304 | tf_op jit(solution)/shard_map/ppermute | solution.py:568
  764.5 48.5 %collective-permute-start.30 = (bf16[4,24,2432]{2,1,0:T(8,128)(2,1)S(1)}, bf16[4,24,2432]{2,1,0:T(8,128)(2,1)S(1)}, u32[]{:S(2)}, u32[]{:S(2)}) collective-permute-start(bf16[4,24,2432]{2,1,0:T(8,128)(2,1)S(1)} %get-tuple-element.275), channel_id=1, source_target_pairs={{0,4},{1,5},{2,6},{3,7},{4,0},{5,1},{6,2},{7,3},{8,12},{9,13},{10,... | collective-permute-start | bytes 1400840 | tf_op jit(solution)/shard_map/ppermute | solution.py:588
  769.5 43.5 %collective-permute-start.31 = (bf16[4,24,2432]{2,1,0:T(8,128)(2,1)S(1)}, bf16[4,24,2432]{2,1,0:T(8,128)(2,1)S(1)}, u32[]{:S(2)}, u32[]{:S(2)}) collective-permute-start(bf16[4,24,2432]{2,1,0:T(8,128)(2,1)S(1)} %get-tuple-element.276), channel_id=1, source_target_pairs={{0,6},{1,7},{2,4},{3,5},{4,2},{5,3},{6,0},{7,1},{8,14},{9,15},{10,... | collective-permute-start | bytes 1400840 | tf_op jit(solution)/shard_map/ppermute | solution.py:588
  (95 other events, 1376.1 us)
Sparse Core Ops, SparseCore 0:
  68.3 105.6 all-gather.2
  176.9 93.5 all-gather.4
  413.2 187.1 reduce-scatter.3

commit v2 on v1

--- a/solution.py
+++ b/solution.py
@@ -70,6 +70,30 @@
         return jnp.where(opens(e) == 1, e, stop)
 
     lax.fori_loop(0, ext, down, jnp.int32(ext))
+
+
+def list_kept(keep, i, first_s, last_s, kept_s):
+    me = i + RIM
+
+    def one(e, count):
+        wanted = jnp.logical_or(e == me, keep[i, jnp.clip(e - me + SPAN - 1, 0, 2 * SPAN - 2)] > 0)
+
+        @pl.when(wanted)
+        def _():
+            kept_s[count] = e
+
+        return count + wanted.astype(jnp.int32)
+
+    return lax.fori_loop(first_s[me], last_s[me], one, jnp.int32(0))
+
+
+def two_kept(n, count, kept_s, start, me):
+    out = []
+    for e in (kept_s[2 * n], kept_s[jnp.minimum(2 * n + 1, count - 1)]):
+        rows = pl.ds(pl.multiple_of(e * BLK, BLK), BLK)
+        out.append((rows, (me - start) * SPAN + (e - start)))
+    void = jnp.where(2 * n + 1 < count, 0.0, -1e30).astype(F32)
+    return out, void
 
 
 def forward_kernel(
@@ -189,6 +213,7 @@
     delta,
     first_s,
     last_s,
+    kept_s,
 ):
     own = q_t.shape[1] // BLK
     scan_blocks(flags, pos[0], first_s, last_s, own)
@@ -226,38 +251,38 @@
             c2[hp, BLK:, :] = jnp.where(left, 0.0, cn).astype(BF16)
         dq_acc[...] = jnp.zeros_like(dq_acc)
         me = i + RIM
-        start = first_s[me]
-
-        @pl.loop(start, last_s[me])
-        def _(e):
-            wanted = jnp.logical_or(e == me, keep[i, jnp.clip(e - me + SPAN - 1, 0, 2 * SPAN - 2)] > 0)
-
-            @pl.when(wanted)
-            def _():
-                rows = pl.ds(pl.multiple_of(e * BLK, BLK), BLK)
-                ab = (me - start) * SPAN + (e - start)
-                for hp in range(PAIRS):
-                    lanes = slice(hp * BLK, (hp + 1) * BLK)
-                    vb = v[rows, lanes]
-                    s = dot(k[rows, lanes], qbd[hp])
-                    dw = dot(vb, cbd[hp])
-                    bias = log_factor[ab, hp : hp + 1, :] - lse[i, hp : hp + 1, :]
-                    w = jnp.exp2(s * SCALE2 + bias)
-                    ds = w * (dw - delta[hp : hp + 1, :] * inv_factor[ab, hp : hp + 1, :])
-                    wb = w.astype(BF16)
-                    dsb = ds.astype(BF16)
-                    dvc = dot(wb, c2[hp])
-                    dkc = dot(dsb, q2[hp])
-                    dqc = dot(k_t[lanes, rows], dsb)
-                    dv_acc[rows, lanes] += dvc
-                    dk_acc[rows, lanes] += dkc
-                    upper = slice(hp * BLK, hp * BLK + HD)
-                    lower = slice(hp * BLK + HD, (hp + 1) * BLK)
-                    dq_acc[upper, :] += dqc[:HD, :BLK]
-                    dq_acc[lower, :] += dqc[HD:, BLK:]
-                    dr[ab, hp : hp + 1, :] += jnp.sum(
-                        dvc * vb.astype(F32), axis=0, keepdims=True
-                    )
+        count = list_kept(keep, i, first_s, last_s, kept_s)
+
+        @pl.loop(0, (count + 1) // 2)
+        def _(n):
+            ((rows_a, ab_a), (rows_b, ab_b)), void = two_kept(n, count, kept_s, first_s[me], me)
+            for hp in range(PAIRS):
+                lanes = slice(hp * BLK, (hp + 1) * BLK)
+                one = slice(hp, hp + 1)
+                vb = jnp.concatenate([v[rows_a, lanes], v[rows_b, lanes]], 0)
+                s = dot(jnp.concatenate([k[rows_a, lanes], k[rows_b, lanes]], 0), qbd[hp])
+                dw = dot(vb, cbd[hp])
+                level = lse[i, one, :]
+                w_a = jnp.exp2(s[:BLK] * SCALE2 + (log_factor[ab_a, one, :] - level))
+                w_b = jnp.exp2(s[BLK:] * SCALE2 + (log_factor[ab_b, one, :] - level + void))
+                ds_a = w_a * (dw[:BLK] - delta[one, :] * inv_factor[ab_a, one, :])
+                ds_b = w_b * (dw[BLK:] - delta[one, :] * inv_factor[ab_b, one, :])
+                wb = jnp.concatenate([w_a.astype(BF16), w_b.astype(BF16)], 0)
+                dsb = jnp.concatenate([ds_a.astype(BF16), ds_b.astype(BF16)], 0)
+                dvc = dot(wb, c2[hp])
+                dkc = dot(dsb, q2[hp])
+                dqc = dot(jnp.concatenate([k_t[lanes, rows_a], k_t[lanes, rows_b]], 1), dsb)
+                dv_acc[rows_a, lanes] += dvc[:BLK]
+                dv_acc[rows_b, lanes] += dvc[BLK:]
+                dk_acc[rows_a, lanes] += dkc[:BLK]
+                dk_acc[rows_b, lanes] += dkc[BLK:]
+                upper = slice(hp * BLK, hp * BLK + HD)
+                lower = slice(hp * BLK + HD, (hp + 1) * BLK)
+                dq_acc[upper, :] += dqc[:HD, :BLK]
+                dq_acc[lower, :] += dqc[HD:, BLK:]
+                dots = dvc * vb.astype(F32)
+                dr[ab_a, one, :] += jnp.sum(dots[:BLK], axis=0, keepdims=True)
+                dr[ab_b, one, :] += jnp.sum(dots[BLK:], axis=0, keepdims=True)
 
         dq_t[:, cols] = (dq_acc[...] * SCALE).astype(BF16)
 
@@ -292,6 +317,7 @@
             pltpu.VMEM((ext * BLK, D), F32),
             pltpu.VMEM((ext * BLK, D), F32),
             pltpu.VMEM((8, 2 * BLK), F32),
+            pltpu.SMEM((ext,), jnp.int32),
             pltpu.SMEM((ext,), jnp.int32),
             pltpu.SMEM((ext,), jnp.int32),
         ],
@@ -401,46 +427,78 @@
                    jax.ShapeDtypeStruct((n, D), BF16), jax.ShapeDtypeStruct((n, D), BF16), jax.ShapeDtypeStruct((D, n), BF16),
                    jax.ShapeDtypeStruct((8, D), F32), jax.ShapeDtypeStruct((1, FF), F32)],
         compiler_params=pltpu.CompilerParams(vmem_limit_bytes=56 * 2**20),
-        cost_estimate=cost(23),
+        cost_estimate=cost(3),
         name="ffn_back",
     )(grad, second, first, slope, w12, w12, wo, gains)
 
-def ffn_grads_kernel(normed, dinner, active, douter, ctx_t, dattend, sums, b1_sum, out, turned):
+def ffn_grads_kernel(extra, normed, dinner, active, douter, ctx_t, dattend, sums, b1_sum, *rest):
+    (other, other_vec, out, turned) = rest if extra else (None, None) + rest
     n = pl.program_id(0)
     blocks = FF // D
+    last = 2 * blocks + 1 + extra
+
     @pl.when(n == 0)
     def _():
         turned[...] = normed[...].T
+
     @pl.when(n < blocks)
     def _():
         out[...] = dot(turned[...], dinner[...]).astype(BF16)
+
     @pl.when(jnp.logical_and(n >= blocks, n < 2 * blocks))
     def _():
         out[...] = dot_rows(active[...], douter[...]).astype(BF16)
+
     @pl.when(n == 2 * blocks)
     def _():
         out[...] = dot(ctx_t[...].astype(BF16), dattend[...]).astype(BF16)
-    @pl.when(n == 2 * blocks + 1)
-    def _():
-        rows = jnp.concatenate([sums[...]] + [b1_sum[:, j * D:(j + 1) * D] for j in range(blocks)] + [jnp.zeros((128 - 8 - blocks, D), F32)], 0)
-        out[:, :128] = rows.T.astype(BF16)
-
-def ffn_grads(normed, dinner, active, douter, ctx_t, dattend, sums, b1_sum):
+
+    @pl.when(n == last)
+    def _():
+        rows = [sums[...]] + [b1_sum[:, j * D : (j + 1) * D] for j in range(blocks)]
+        rows = jnp.concatenate(rows + [jnp.zeros((BLK - 8 - blocks, D), F32)], 0)
+        out[:, :BLK] = rows.T.astype(BF16)
+        if extra:
+            out[:, BLK : 2 * BLK] = other_vec[...]
+
+    if extra:
+
+        @pl.when(jnp.logical_and(n > 2 * blocks, n < last))
+        def _():
+            out[...] = other[...]
+
+
+def ffn_grads(normed, dinner, active, douter, ctx_t, dattend, sums, b1_sum, other=None):
     n = normed.shape[0]
     blocks = FF // D
+    extra = 0 if other is None else 3
+    width = (2 * blocks + 1 + extra) * D + (2 if extra else 1) * BLK
+    part = lambda first, count: (lambda i: (0, jnp.clip(i - first, 0, count - 1)))
+    specs = [
+        once((n, D)),
+        pl.BlockSpec((n, D), part(0, blocks)),
+        pl.BlockSpec((n, D), part(blocks, blocks)),
+        once((n, D)),
+        once((D, n)),
+        once((n, D)),
+        once((8, D)),
+        once((1, FF)),
+    ]
+    args = [normed, dinner, active, douter, ctx_t, dattend, sums, b1_sum]
+    if extra:
+        specs += [pl.BlockSpec((D, D), part(2 * blocks + 1, extra)), once((D, BLK), extra * D // BLK)]
+        args += [other, other]
     return pl.pallas_call(
-        ffn_grads_kernel,
-        grid=(2 * blocks + 2,),
-        in_specs=[once((n, D)), pl.BlockSpec((n, D), lambda i: (0, jnp.minimum(i, blocks - 1))),
-                  pl.BlockSpec((n, D), lambda i: (0, jnp.clip(i - blocks, 0, blocks - 1))),
-                  once((n, D)), once((D, n)), once((n, D)), once((8, D)), once((1, FF))],
+        functools.partial(ffn_grads_kernel, extra),
+        grid=(2 * blocks + 2 + extra,),
+        in_specs=specs,
         out_specs=pl.BlockSpec((D, D), lambda i: (0, i)),
-        out_shape=jax.ShapeDtypeStruct((D, 2 * FF + D + 128), BF16),
+        out_shape=jax.ShapeDtypeStruct((D, width), BF16),
         scratch_shapes=[pltpu.VMEM((D, n), BF16)],
         compiler_params=pltpu.CompilerParams(vmem_limit_bytes=56 * 2**20),
-        cost_estimate=cost(20),
+        cost_estimate=cost(3),
         name="ffn_grads",
-    )(normed, dinner, active, douter, ctx_t, dattend, sums, b1_sum)
+    )(*args)
 
 
 def project_kernel(low, w, qb, vb, q, q_t, k, k_t, v, v_t):
@@ -484,7 +542,7 @@
         name="project",
     )(low_ext, w, qb, vb)
 
-def att_grads_kernel(low, dq_t, dk, dv, logit, out, turned):
+def att_grads_kernel(low, dq_t, dk, dv, dr, rate, out, turned):
     n = pl.program_id(0)
     own = dq_t.shape[1]
     rim = (low.shape[0] - own) // 2
@@ -506,24 +564,31 @@
     def _():
         qb = jnp.sum(dq_t[...].astype(F32), 1, keepdims=True)
         vb = jnp.sum(dv[...].astype(F32), 0, keepdims=True)
-        rows = jnp.concatenate([vb, logit[...], jnp.zeros((126, D), F32)], 0).T
+        left = lax.broadcasted_iota(jnp.int32, (SPAN * SPAN, BLK), 1) < HD
+        columns = []
+        for hp in range(PAIRS):
+            both = dr[:, hp, :]
+            columns.append(jnp.sum(jnp.where(left, both, 0.0), 1, keepdims=True))
+            columns.append(jnp.sum(jnp.where(left, 0.0, both), 1, keepdims=True))
+        logit = jnp.concatenate(columns, 0) * rate[...]
+        rows = jnp.concatenate([vb, jnp.zeros((127, D), F32)], 0).T
         lane = lax.broadcasted_iota(jnp.int32, (D, 128), 1)
-        out[:, :128] = jnp.where(lane == 2, qb, rows).astype(BF16)
-
-def att_grads(low_ext, dq_t, dk, dv, logit):
+        out[:, :128] = jnp.where(lane == 2, qb, jnp.where(lane == 1, logit, rows)).astype(BF16)
+
+def att_grads(low_ext, dq_t, dk, dv, dr, rate):
     n = low_ext.shape[0]
     own = dq_t.shape[1]
     return pl.pallas_call(
         att_grads_kernel,
         grid=(4,),
-        in_specs=[once((n, D)), once((D, own)), once((n, D)), once((n, D)), once((1, D))],
+        in_specs=[once((n, D)), once((D, own)), once((n, D)), once((n, D)), once(dr.shape), once((D, 1))],
         out_specs=pl.BlockSpec((D, D), lambda i: (0, i)),
         out_shape=jax.ShapeDtypeStruct((D, 3 * D + 128), BF16),
         scratch_shapes=[pltpu.VMEM((D, n), BF16)],
         compiler_params=pltpu.CompilerParams(vmem_limit_bytes=48 * 2**20),
-        cost_estimate=cost(12),
+        cost_estimate=cost(3),
         name="att_grads",
-    )(low_ext, dq_t, dk, dv, logit)
+    )(low_ext, dq_t, dk, dv, dr, rate)
 
 def input_back_kernel(dk, dv, dq_t, dfirst, w, own, rims):
     i = pl.program_id(0)
@@ -556,7 +621,7 @@
         out_specs=[orow, rrow],
         out_shape=[jax.ShapeDtypeStruct((own, D), F32), jax.ShapeDtypeStruct((n - own, D), BF16)],
         compiler_params=pltpu.CompilerParams(vmem_limit_bytes=40 * 2**20),
-        cost_estimate=cost(12),
+        cost_estimate=cost(3),
         name="input_back",
     )(dk, dv, dq_t, dfirst, w)
 
@@ -588,22 +653,39 @@
     return lax.ppermute(block, AXES, [(i, i ^ mask) for i in range(count)])
 
 
-def gathered_in_steps(part):
-    far, middle = sizes()
-    z, m, c = place()
-    plane = jnp.zeros((far,) + part.shape, part.dtype)
-    for d in range(far):
-        piece = part if d == 0 else swap(part, d * 2 * middle)
-        plane = lax.dynamic_update_slice(plane, piece[None], (z ^ d, 0, 0))
-    half = jnp.zeros((middle,) + plane.shape, part.dtype)
-    for d in range(middle):
-        piece = plane if d == 0 else swap(plane, d * 2)
-        half = lax.dynamic_update_slice(half, piece[None], (m ^ d, 0, 0, 0))
-    other = swap(half, 1)
-    whole = jnp.zeros((2,) + half.shape, part.dtype)
-    whole = lax.dynamic_update_slice(whole, half[None], (c, 0, 0, 0, 0))
-    whole = lax.dynamic_update_slice(whole, other[None], (1 - c, 0, 0, 0, 0))
-    return whole.transpose(2, 1, 0, 3, 4).reshape(-1, part.shape[1])
+def put(buffer, piece, index):
+    return lax.dynamic_update_slice(buffer, piece[None], (index,) + (0,) * piece.ndim)
+
+
+class SteppedGather:
+    def __init__(self, part):
+        self.part = part
+        self.block = part
+        self.step = 0
+
+    def settle(self, tied):
+        if self.step > 0:
+            own = place()[self.step - 1]
+            out = jnp.zeros((len(self.arriving) + 1,) + self.block.shape, self.block.dtype)
+            tied, out = lax.optimization_barrier((tied, out))
+            out = put(out, self.block, own)
+            for d, piece in self.arriving:
+                out = put(out, piece, own ^ d)
+            self.block = out
+        return tied
+
+    def advance(self, tied):
+        far, middle = sizes()
+        tied = self.settle(tied)
+        tied, self.block = lax.optimization_barrier((tied, self.block))
+        self.step += 1
+        count, scale = ((far, 2 * middle), (middle, 2), (2, 1))[self.step - 1]
+        self.arriving = [(d, swap(self.block, d * scale)) for d in range(1, count)]
+        return tied
+
+    def result(self, tied):
+        self.settle(tied)
+        return self.block.transpose(2, 1, 0, 3, 4).reshape(-1, self.part.shape[1])
 
 
 def scattered(part):
@@ -619,6 +701,10 @@
         far, middle = sizes()
         self.parts = part.reshape(far, middle, 2, -1, part.shape[1])
         self.step = 0
+
+    def anchored(self, tied):
+        tied, kept = lax.optimization_barrier((tied, self.halves[0]))
+        return tied, (kept, self.halves[1])
 
     def middle_sum(self, index):
         kept, got = self.halves
@@ -647,10 +733,12 @@
             tied, out = lax.optimization_barrier((tied, out))
             self.halves = (pick(self.parts, c, 2), swap(out, 1))
         elif self.step == 2:
+            tied, self.halves = self.anchored(tied)
             out = [self.middle_sum(m ^ d).astype(BF16) for d in range(1, middle)]
             tied, out = lax.optimization_barrier((tied, out))
             self.arrived = [swap(item, d * 2) for d, item in zip(range(1, middle), out)]
         else:
+            tied, self.halves = self.anchored(tied)
             out = [self.far_sum(z ^ d).astype(BF16) for d in range(1, far)]
             tied, out = lax.optimization_barrier((tied, out))
             self.last = [swap(item, d * 2 * middle) for d, item in zip(range(1, far), out)]
@@ -674,6 +762,7 @@
     relaxed = jax.nn.sigmoid(z)
     factor = table_rows(relaxed)
     q, q_t, k, k_t, v, v_t = project(low_ext, head, vec["qb"][None], vec["vb"][None])
+    log_factor, inv_factor = jnp.log2(factor), 1.0 / factor
     ctx_t, lse = attend(flags, keep, pos, factor, q_t, k, v_t)
     ctx_t, wo, wo_at, w12 = between(ctx_t)
     names = ("ob", "g1", "s1", "b2", "g2", "s2", "s2", "s2")
@@ -682,43 +771,38 @@
         ctx_t, hidden, wo, wo_at, w12, vectors, vec["b1"][None]
     )
     record = (low_ext, q, q_t, k, k_t, v, ctx_t, lse, first, normed_low, active, slope, second)
-    return result, result_low, record + (relaxed, factor, vectors, head, wo, wo_at, w12)
+    return result, result_low, record + (relaxed, log_factor, inv_factor, vectors, head, wo, wo_at, w12)
 
 
 def layer_backward(grad, record, flags, keep, temper, pos, before=None, done=None):
     low_ext, q, q_t, k, k_t, v, ctx_t, lse, first, normed_low, active, slope, second = record[:13]
-    relaxed, factor, vectors, head, wo, wo_at, w12 = record[13:]
+    relaxed, log_factor, inv_factor, vectors, head, wo, wo_at, w12 = record[13:]
     rows = first.shape[0]
     rim = RIM * BLK
-    if before is not None:
-        grad = before.advance(grad)
     douter, dinner, dfirst, dattend, dc, dc_t, row_sums, b1_sum = ffn_back(
         grad, second, first, slope, w12, wo, wo_at, vectors
     )
-    ffn_part = ffn_grads(normed_low, dinner, active, douter, ctx_t, dattend, row_sums, b1_sum)
+    part = ffn_grads(normed_low, dinner, active, douter, ctx_t, dattend, row_sums, b1_sum, before)
     if before is None:
-        dc, ffn_part = lax.optimization_barrier((dc, ffn_part))
-        ffn_sum = scattered(ffn_part)
+        dc, part = lax.optimization_barrier((dc, part))
+        ffn_sum = scattered(part)
     else:
-        dc, done = lax.optimization_barrier((dc, done))
-        dc = before.advance(dc)
-        ffn_sum = SteppedSum(ffn_part)
+        ffn_sum = SteppedSum(part)
         dc = ffn_sum.advance(dc)
-        dc = before.advance(dc)
         dc = ffn_sum.advance(dc)
     dq_t, dk, dv, dr = attend_back(
-        flags, keep, pos, jnp.log2(factor), 1.0 / factor, q_t, q, dc_t, dc, ctx_t, lse, k, k_t, v
+        flags, keep, pos, log_factor, inv_factor, q_t, q, dc_t, dc, ctx_t, lse, k, k_t, v
     )
-    drelaxed = dr[:, :PAIRS].reshape(SPAN * SPAN, HEADS, HD).sum(-1).T.reshape(HEADS, SPAN, SPAN)
-    logit_grad = (drelaxed * (1.0 - relaxed) / temper[:, None, None]).reshape(1, -1)
+    rate = ((1.0 - relaxed) / temper[:, None, None]).reshape(-1, 1)
     if before is None:
         own, rims = input_back(dk, dv, dq_t, dfirst, head)
         from_lower, from_upper = neighbours(rims[rim:], rims[:rim])
         dq_t, rims = lax.optimization_barrier((dq_t, rims))
-        att_sum = SteppedSum(att_grads(low_ext, dq_t, dk, dv, logit_grad))
+        att_sum = att_grads(low_ext, dq_t, dk, dv, dr, rate)
     else:
-        att_sum = SteppedSum(att_grads(low_ext, dq_t, dk, dv, logit_grad))
+        att_sum = SteppedSum(att_grads(low_ext, dq_t, dk, dv, dr, rate))
         dk = att_sum.advance(dk)
+        dk, done = lax.optimization_barrier((dk, done))
         dk = ffn_sum.advance(dk)
         own, rims = input_back(dk, dv, dq_t, dfirst, head)
         own = att_sum.advance(own)
@@ -787,25 +871,28 @@
         return vec
 
     symbols = embedded[0]
+    first, wide, out, vectors = own_parts(0)
+    gather = SteppedGather(jnp.concatenate(first + vectors, 1))
+    for _ in range(3):
+        symbols = gather.advance(symbols)
     lower, upper = neighbours(symbols[symbols.shape[0] - rim :], symbols[:rim])
     low_ext = jnp.concatenate([lower, symbols, upper], 0)
-    first, wide, out, vectors = own_parts(0)
-    head_zero = gathered_in_steps(jnp.concatenate(first + vectors, 1))
+    head_zero = gather.result(symbols)
     head_zero, *rest = lax.optimization_barrier((head_zero, *wide, *out))
     tail_zero = gathered(jnp.concatenate(rest, 1))
-    later = {}
+    first, wide, out, vectors = own_parts(1)
+    later = SteppedGather(jnp.concatenate(first + out + vectors, 1))
+    tails = []
 
     def between_zero(ctx_t):
-        first, wide, out, vectors = own_parts(1)
-        ctx_t, tail, *parts = lax.optimization_barrier(
-            (ctx_t, tail_zero, *first, *out, *vectors, *wide)
-        )
-        later["head"] = gathered_in_steps(jnp.concatenate(parts[:5], 1))
-        later["tail"] = gathered(jnp.concatenate(parts[5:], 1))
-        return ctx_t, tail, 2 * FF // D, tail
+        ctx_t = later.advance(ctx_t)
+        ctx_t = later.advance(ctx_t)
+        _, _, *rest = lax.optimization_barrier((ctx_t, tail_zero, *wide))
+        tails.append(gathered(jnp.concatenate(rest, 1)))
+        return ctx_t, tail_zero, 2 * FF // D, tail_zero
 
     def between_one(ctx_t):
-        return ctx_t, later["head"], 3, later["tail"]
+        return ctx_t, head_one, 3, tails[0]
 
     hidden, low, record = layer_forward(
         symbols,
@@ -819,13 +906,15 @@
         between_zero,
     )
     records = [record]
+    low = later.advance(low)
     lower, upper = neighbours(low[low.shape[0] - rim :], low[:rim])
     low_ext = jnp.concatenate([lower, low, upper], 0)
+    head_one = later.result(low)
     hidden, _, record = layer_forward(
         hidden,
         low_ext,
-        later["head"],
-        unpacked(later["head"][:, 4 * D :]),
+        head_one,
+        unpacked(head_one[:, 4 * D :]),
         flags,
         selector[1, 0],
         warmth[1],
@@ -840,18 +929,16 @@
     grad, ffn_zero, att_zero, ffn_one = layer_backward(
         grad, records[0], flags, selector[0, 0], warmth[0], pos, att_one, ffn_one
     )
-    sums = jnp.stack(
-        [
-            jnp.concatenate([ffn_zero.result(), att_zero.result()], 1),
-            jnp.concatenate([ffn_one, att_one.result()], 1),
-        ]
-    )
-    w1_grad = unwidened(sums[:, :, :FF])
-    w2_grad = jnp.concatenate([sums[:, :, FF + j * D : FF + (j + 1) * D] for j in range(4)], 1)
-    wo_grad = sums[:, :, 2 * FF : 2 * FF + D]
-    fv = sums[:, :, 2 * FF + D : 2 * FF + D + 128]
-    att = sums[:, :, 2 * FF + D + 128 :]
-    av = att[:, :, 3 * D :]
+    both = ffn_zero.result()
+    last = att_zero.result()
+    ends = [2 * FF + D, 2 * FF + 4 * D]
+    fv = jnp.stack([both[:, ends[1] : ends[1] + BLK], ffn_one[:, ends[0] :]])
+    av = jnp.stack([last[:, 3 * D :], both[:, ends[1] + BLK :]])
+    ffn_sums = jnp.stack([both[:, : ends[0]], ffn_one[:, : ends[0]]])
+    att = jnp.stack([last[:, : 3 * D], both[:, ends[0] : ends[1]]])
+    w1_grad = unwidened(ffn_sums[:, :, :FF])
+    w2_grad = jnp.concatenate([ffn_sums[:, :, FF + j * D : FF + (j + 1) * D] for j in range(4)], 1)
+    wo_grad = ffn_sums[:, :, 2 * FF :]
     b1_grad = jnp.concatenate([fv[:, :, 8 + j] for j in range(4)], 1)
     new_mask = (scores.astype(F32) + jitter.astype(F32) > 0).astype(jnp.int32)
     return (

time: 863 us -> 765 us (0.89)
  waiting for transfers between devices: 258 us -> 196 us
  starting transfers between devices: 139 us -> 92.6 us
  Pallas kernels: 294 us -> 306 us
    ppermute x35 -> x28, waiting for transfers between devices: 143 us -> 93 us  [swap(): return lax.ppermute(block, AXES, [(i, i ^ mask) for i in range(count)])]
    ppermute x35 -> x28, starting transfers between devices: 104 us -> 73.7 us  [swap(): return lax.ppermute(block, AXES, [(i, i ^ mask) for i in range(count)])]
    all_gather x2, waiting for transfers between devices: 24.2 us -> 0.02 us  [gathered(): return lax.all_gather(part, AXES, axis=0, tiled=True)]
    ppermute x4, waiting for transfers between devices: 63.5 us -> 81.1 us  [neighbours(): lax.ppermute(tail, 'dp', [(i, i + 1) for i in range(count - 1)])]
    ppermute x4, starting transfers between devices: 29.6 us -> 12.8 us  [neighbours(): lax.ppermute(tail, 'dp', [(i, i + 1) for i in range(count - 1)])]
    unnamed x165 -> x176, local copies, waits for them, and re-layouts: 34.9 us -> 43.3 us
  transfers between devices with their start and end apart: 46 -> 39, of which waited for: 21 -> 14; matrix products, arithmetic and copies ran while one was open for 9% -> 13% of each run, Pallas kernels for 26% -> 31%
where the time goes in v2:
time: 765 us; the launch traced here: 763 us
  Pallas kernels  306 us (40%)
  waiting for transfers between devices  196 us (26%)
  local copies, waits for them, and re-layouts  113 us (15%)
  starting transfers between devices  92.6 us (12%)
  other arithmetic  40.6 us (5%)
  between operations  15.7 us (2%)
    ppermute x28, waiting for transfers between devices, swap(): return lax.ppermute(block, AXES, [(i, i ^ mask) for i in range(count)])  93 us
    ppermute x4, waiting for transfers between devices, neighbours(): lax.ppermute(tail, 'dp', [(i, i + 1) for i in range(count - 1)])  81.1 us
    ppermute x28, starting transfers between devices, swap(): return lax.ppermute(block, AXES, [(i, i ^ mask) for i in range(count)])  73.7 us
    pallas_call x2, Pallas kernels, attend_back(): pl.pallas_call(backward_kernel, out_shape=(jax.ShapeDtypeStruct(q_t.shape...  62.1 us
    pallas_call x2, Pallas kernels, ffn(): pl.pallas_call(ffn_kernel, grid=(n // ROWS,), in_specs=[pl.BlockSpec((D,...  56.4 us
    pallas_call x2, Pallas kernels, ffn_back(): pl.pallas_call(ffn_back_kernel, grid=(n // ROWS,), in_specs=[row(D), row(...  46.3 us
    pallas_call x2, Pallas kernels, ffn_grads(): pl.pallas_call(functools.partial(ffn_grads_kernel, extra), grid=(2 * bloc...  45 us
    unnamed x176, local copies, waits for them, and re-layouts  43.3 us
  transfers between devices with their start and end apart: 39, of which 14 were waited for; matrix products, arithmetic and copies ran while one was open for 13% of the time, Pallas kernels for 31%

profile of v2, /device:TPU:0, one launch (start us, length us, event | category | flops | bytes accessed | tf_op | source)
XLA Modules:
  0.0 763.3 jit_solution(12597408285745714022)
XLA Ops:
  33.5 10.0 %collective-permute-done.3 = bf16[4,24,2432]{2,1,0:T(8,128)(2,1)S(1)} collective-permute-done((bf16[4,24,2432]{2,1,0:T(8,128)(2,1)S(1)}, bf16[4,24,2432]{2,1,0:T(8,128)(2,1)S(1)}, u32[]{:S(2)}, u32[]{:S(2)}) %collective-permute-start.3) | collective-permute-done | bytes 466976 | tf_op jit(solution)/shard_map/ppermute | solution.py:653
  74.6 39.5 %collective-permute-done.7 = bf16[512,768]{1,0:T(8,128)(2,1)S(1)} collective-permute-done((bf16[512,768]{1,0:T(8,128)(2,1)S(1)}, bf16[512,768]{1,0:T(8,128)(2,1)S(1)}, u32[]{:S(2)}, u32[]{:S(2)}) %collective-permute-start.7) | collective-permute-done | bytes 786464 | tf_op jit(solution)/shard_map/ppermute | solution.py:632
  124.6 14.4 %project.2 = (bf16[1024,768]{1,0:T(8,128)(2,1)S(1)}, bf16[768,1024]{1,0:T(8,128)(2,1)S(1)}, bf16[2048,768]{1,0:T(8,128)(2,1)S(1)}, bf16[768,2048]{1,0:T(8,128)(2...) custom-call(bf16[2048,768]{1,0:T(8,128)(2,1)} %copy-done.13, bf16[768,2432]{1,0:T(8,128)(2,1)} %bitcast.37.w, ...), custom_call_target="tpu_custom_call" | custom-call | flops 14000000000 | bytes 1000000 | tf_op jit(solution)/shard_map/project/pallas_call | solution.py:534
  147.1 10.2 %attend.2 = (f32[768,1024]{1,0:T(8,128)S(1)}, f32[8,8,256]{2,1,0:T(8,128)S(1)}) custom-call(s32[64]{0:T(128)S(1)} %bitcast.346, s32[8,15]{1,0:T(8,128)S(1)} %get-tuple-element.384.keep, s32[1]{0:T(128)} %bitcast.2.pos, f32[64,6,256]{2,1,0:T(8,128)S(1)} %get-tuple-element.365.factor, bf16[768,1024]{1,0:T(8,128)(2,1)S(1)} %get-tuple-element.203.q_t, ...), custom_call_target="tpu_custom_call" | custom-call | flops 12999999488 | bytes 1000000 | tf_op jit(solution)/shard_map/attend/pallas_call | solution.py:165
  190.6 28.2 %ffn.2 = (f32[1024,768]{1,0:T(8,128)}, bf16[1024,768]{1,0:T(8,128)(2,1)}, bf16[1024,3072]{1,0:T(8,128)(2,1)}, bf16[1024,3072]{1,0:T(8,128)(2,1)}, f32[1024,768]{...) custom-call(f32[768,1024]{1,0:T(8,128)} %copy-done.1, bf16[1024,768]{1,0:T(8,128)(2,1)} %bitcast.356, ...), custom_call_target="tpu_custom_call" | custom-call | flops 28000000000 | bytes 1000000 | tf_op jit(solution)/shard_map/ffn/pallas_call | solution.py:371
  226.7 41.7 %collective-permute-done.16 = bf16[512,768]{1,0:T(8,128)(2,1)S(1)} collective-permute-done((bf16[512,768]{1,0:T(8,128)(2,1)S(1)}, bf16[512,768]{1,0:T(8,128)(2,1)S(1)}, u32[]{:S(2)}, u32[]{:S(2)}) %collective-permute-start.16) | collective-permute-done | bytes 786464 | tf_op jit(solution)/shard_map/ppermute | solution.py:632
  279.5 13.2 %project.3 = (bf16[1024,768]{1,0:T(8,128)(2,1)S(1)}, bf16[768,1024]{1,0:T(8,128)(2,1)S(1)}, bf16[2048,768]{1,0:T(8,128)(2,1)S(1)}, bf16[768,2048]{1,0:T(8,128)(2...) custom-call(bf16[2048,768]{1,0:T(8,128)(2,1)} %copy-done.11, bf16[768,3200]{1,0:T(8,128)(2,1)} %bitcast.350, ...), custom_call_target="tpu_custom_call" | custom-call | flops 14000000000 | bytes 1000000 | tf_op jit(solution)/shard_map/project/pallas_call | solution.py:534
  300.4 11.3 %attend.3 = (f32[768,1024]{1,0:T(8,128)S(1)}, f32[8,8,256]{2,1,0:T(8,128)S(1)}) custom-call(s32[64]{0:T(128)S(1)} %bitcast.347, s32[8,15]{1,0:T(8,128)S(1)} %get-tuple-element.385.keep, s32[1]{0:T(128)} %bitcast.2.pos, f32[64,6,256]{2,1,0:T(8,128)S(1)} %get-tuple-element.363.factor, bf16[768,1024]{1,0:T(8,128)(2,1)S(1)} %get-tuple-element.225.q_t, ...), custom_call_target="tpu_custom_call" | custom-call | flops 12999999488 | bytes 1000000 | tf_op jit(solution)/shard_map/attend/pallas_call | solution.py:165
  315.2 28.2 %ffn.3 = (f32[1024,768]{1,0:T(8,128)}, bf16[1024,768]{1,0:T(8,128)(2,1)}, bf16[1024,3072]{1,0:T(8,128)(2,1)}, bf16[1024,3072]{1,0:T(8,128)(2,1)}, f32[1024,768]{...) custom-call(f32[768,1024]{1,0:T(8,128)} %copy-done.4, f32[1024,768]{1,0:T(8,128)} %get-tuple-element.229.hidden, ...), custom_call_target="tpu_custom_call" | custom-call | flops 28000000000 | bytes 1000000 | tf_op jit(solution)/shard_map/ffn/pallas_call | solution.py:371
  343.4 23.1 %ffn_back.2 = (bf16[1024,768]{1,0:T(8,128)(2,1)}, bf16[1024,3072]{1,0:T(8,128)(2,1)}, f32[1024,768]{1,0:T(8,128)}, bf16[1024,768]{1,0:T(8,128)(2,1)}, bf16[1024,...) custom-call(bf16[1024,768]{1,0:T(8,128)(2,1)} %bitcast.361, ...), custom_call_target="tpu_custom_call" | custom-call | flops 3000000000 | bytes 1000000 | tf_op jit(solution)/shard_map/ffn_back/pallas_call | solution.py:421
  366.4 20.4 %ffn_grads.2 = bf16[768,7040]{1,0:T(8,128)(2,1)} custom-call(bf16[1024,768]{1,0:T(8,128)(2,1)} %get-tuple-element.243.normed, bf16[1024,3072]{1,0:T(8,128)(2,1)} %get-tuple-element.244.dinner, bf16[1024,3072]{1,0:T(8,128)(2,1)} %get-tuple-element.245.active, bf16[1024,768]{1,0:T(8,128)(2,1)} %get-tuple-element.246.douter, f32[768,1024]{1,0:T(8,128)} %copy-done.4, ...), custom_call_target="tpu_custom_call" | custom-call | flops 3000000000 | bytes 1000000 | tf_op jit(solution)/shard_map/ffn_grads/pallas_call | solution.py:491
  386.9 32.6 %attend_back.2 = (bf16[768,1024]{1,0:T(8,128)(2,1)}, bf16[2048,768]{1,0:T(8,128)(2,1)}, bf16[2048,768]{1,0:T(8,128)(2,1)}, f32[64,8,128]{2,1,0:T(8,128)}) custom-call(s32[64]{0:T(128)} %bitcast.344, s32[8,15]{1,0:T(8,128)} %copy-done.30, s32[1]{0:T(128)} %bitcast.2.pos, f32[64,6,256]{2,1,0:T(8,128)} %copy_multiply_fusion.log_factor, ...), custom_call_target="tpu_custom_call" | custom-call | flops 5000000000 | bytes 1000000 | tf_op jit(solution)/shard_map/attend_back/pallas_call | solution.py:301
  425.4 11.6 %input_back.2 = (f32[1024,768]{1,0:T(8,128)S(1)}, bf16[1024,768]{1,0:T(8,128)(2,1)S(1)}) custom-call(bf16[2048,768]{1,0:T(8,128)(2,1)S(1)} %copy-done.5, bf16[2048,768]{1,0:T(8,128)(2,1)S(1)} %copy-done.6, bf16[768,1024]{1,0:T(8,128)(2,1)S(1)} %copy-done.9, f32[1024,768]{1,0:T(8,128)} %get-tuple-element.257.dfirst, bf16[768,3200]{1,0:T(8,128)(2,1)} %bitcast.353), custom_call_target="tpu_custom_call" | custom-call | flops 3000000000 | bytes 1000000 | tf_op jit(solution)/shard_map/input_back/pallas_call | solution.py:617
  447.1 11.8 %att_grads.2.rest_0_.rest_1_ = bf16[768,2432]{1,0:T(8,128)(2,1)} custom-call(bf16[2048,768]{1,0:T(8,128)(2,1)S(1)} %copy-done.12, bf16[768,1024]{1,0:T(8,128)(2,1)S(1)} %copy-done.10, bf16[2048,768]{1,0:T(8,128)(2,1)} %get-tuple-element.254.dk, bf16[2048,768]{1,0:T(8,128)(2,1)} %get-tuple-element.255.dv, f32[64,8,128]{2,1,0:T(8,128)S(1)} %copy-done.25, ...), custom_call_target="tpu_custom_call" | custom-call | flops 3000000000 | bytes 1000000 | tf_op jit(solution)/shard_map/att_grads/pallas_call | solution.py:581
  460.3 21.5 %collective-permute-done.19 = bf16[512,768]{1,0:T(8,128)(2,1)S(1)} collective-permute-done((bf16[512,768]{1,0:T(8,128)(2,1)}, bf16[512,768]{1,0:T(8,128)(2,1)S(1)}, u32[]{:S(2)}, u32[]{:S(2)}) %collective-permute-start.19) | collective-permute-done | bytes 786464 | tf_op jit(solution)/shard_map/ppermute | solution.py:633
  483.9 23.3 %ffn_back.3 = (bf16[1024,768]{1,0:T(8,128)(2,1)}, bf16[1024,3072]{1,0:T(8,128)(2,1)}, f32[1024,768]{1,0:T(8,128)}, bf16[1024,768]{1,0:T(8,128)(2,1)}, bf16[1024,...) custom-call(f32[1024,768]{1,0:T(8,128)} %copy-done, ...), custom_call_target="tpu_custom_call" | custom-call | flops 3000000000 | bytes 1000000 | tf_op jit(solution)/shard_map/ffn_back/pallas_call | solution.py:421
  507.1 24.6 %ffn_grads.3 = bf16[768,9472]{1,0:T(8,128)(2,1)} custom-call(bf16[1024,768]{1,0:T(8,128)(2,1)} %get-tuple-element.265.normed, bf16[1024,3072]{1,0:T(8,128)(2,1)} %get-tuple-element.266.dinner, bf16[1024,3072]{1,0:T(8,128)(2,1)} %get-tuple-element.267.active, bf16[1024,768]{1,0:T(8,128)(2,1)} %get-tuple-element.268.douter, f32[768,1024]{1,0:T(8,128)} %copy-done.1, ...), custom_call_target="tpu_custom_call" | custom-call | flops 3000000000 | bytes 1000000 | tf_op jit(solution)/shard_map/ffn_grads/pallas_call | solution.py:491
  537.9 11.5 %collective-permute-done.20 = bf16[4,4,24,9472]{3,2,1,0:T(8,128)(2,1)S(1)} collective-permute-done((bf16[4,4,24,9472]{3,2,1,0:T(8,128)(2,1)S(1)}, bf16[4,4,24,9472]{3,2,1,0:T(8,128)(2,1)S(1)}, u32[]{:S(2)}, u32[]{:S(2)}) %collective-permute-start.20) | collective-permute-done | bytes 7274528 | tf_op jit(solution)/shard_map/ppermute | solution.py:653
  554.0 13.8 %collective-permute-start.21 = (bf16[4,24,9472]{2,1,0:T(8,128)(2,1)}, bf16[4,24,9472]{2,1,0:T(8,128)(2,1)S(1)}, u32[]{:S(2)}, u32[]{:S(2)}) collective-permute-start(bf16[4,24,9472]{2,1,0:T(8,128)(2,1)} %get-tuple-element.291), channel_id=1, source_target_pairs={{0,2},{1,3},{2,0},{3,1},{4,6},{5,7},{6,4},{7,5},{8,10},{9,11},{10,... | collective-permute-start | bytes 5455880 | tf_op jit(solution)/shard_map/ppermute | solution.py:653
  579.0 29.5 %attend_back.3 = (bf16[768,1024]{1,0:T(8,128)(2,1)}, bf16[2048,768]{1,0:T(8,128)(2,1)}, bf16[2048,768]{1,0:T(8,128)(2,1)}, f32[64,8,128]{2,1,0:T(8,128)}) custom-call(s32[64]{0:T(128)} %bitcast.345, s32[8,15]{1,0:T(8,128)} %copy-done.29, s32[1]{0:T(128)} %bitcast.2.pos, f32[64,6,256]{2,1,0:T(8,128)} %copy_multiply_fusion.1.log_factor, ...), custom_call_target="tpu_custom_call" | custom-call | flops 5000000000 | bytes 1000000 | tf_op jit(solution)/shard_map/attend_back/pallas_call | solution.py:301
  610.9 11.7 %att_grads.3 = bf16[768,2432]{1,0:T(8,128)(2,1)} custom-call(bf16[2048,768]{1,0:T(8,128)(2,1)S(1)} %copy-done.14, bf16[768,1024]{1,0:T(8,128)(2,1)S(1)} %copy-done.7, bf16[2048,768]{1,0:T(8,128)(2,1)} %get-tuple-element.294.dk, bf16[2048,768]{1,0:T(8,128)(2,1)} %get-tuple-element.284.dv, f32[64,8,128]{2,1,0:T(8,128)S(1)} %copy-done.26, ...), custom_call_target="tpu_custom_call" | custom-call | flops 3000000000 | bytes 1000000 | tf_op jit(solution)/shard_map/att_grads/pallas_call | solution.py:581
  627.8 27.9 %collective-permute-done.22 = bf16[4,24,9472]{2,1,0:T(8,128)(2,1)} collective-permute-done((bf16[4,24,9472]{2,1,0:T(8,128)(2,1)}, bf16[4,24,9472]{2,1,0:T(8,128)(2,1)}, u32[]{:S(2)}, u32[]{:S(2)}) %collective-permute-start.22) | collective-permute-done | bytes 1818656 | tf_op jit(solution)/shard_map/ppermute | solution.py:653
  669.3 11.5 %input_back.3 = (f32[1024,768]{1,0:T(8,128)S(1)}, bf16[1024,768]{1,0:T(8,128)(2,1)S(1)}) custom-call(bf16[2048,768]{1,0:T(8,128)(2,1)S(1)} %copy-done.2, bf16[2048,768]{1,0:T(8,128)(2,1)S(1)} %copy-done.3, bf16[768,1024]{1,0:T(8,128)(2,1)S(1)} %copy-done.8, f32[1024,768]{1,0:T(8,128)} %get-tuple-element.295.dfirst, bf16[768,2432]{1,0:T(8,128)(2,1)} %bitcast.37.w), custom_call_target="tpu_custom_call" | custom-call | flops 3000000000 | bytes 1000000 | tf_op jit(solution)/shard_map/input_back/pallas_call | solution.py:617
  688.4 10.3 %collective-permute-done.34 = bf16[24,9472]{1,0:T(8,128)(2,1)S(1)} collective-permute-done((bf16[24,9472]{1,0:T(8,128)(2,1)S(1)}, bf16[24,9472]{1,0:T(8,128)(2,1)S(1)}, u32[]{:S(2)}, u32[]{:S(2)}) %collective-permute-start.34) | collective-permute-done | bytes 454688 | tf_op jit(solution)/shard_map/ppermute | solution.py:653
  (381 shorter events, 266.1 us)
Async XLA Ops:
  7.2 174.6 %all-gather.3.cloned.1.call-start = ((), (), s32[]{:S(2)}) async-start(), calls=%async_computation.1 | async-start | bytes 10948608 | tf_op jit(solution)/shard_map/all_gather | solution.py:638
  63.6 251.5 %all-gather.5.cloned.1.call-start = ((), (), s32[]{:S(2)}) async-start(), calls=%async_computation.2 | async-start | bytes 9732096 | tf_op jit(solution)/shard_map/all_gather | solution.py:638
  69.1 44.9 %collective-permute-start.7 = (bf16[512,768]{1,0:T(8,128)(2,1)S(1)}, bf16[512,768]{1,0:T(8,128)(2,1)S(1)}, u32[]{:S(2)}, u32[]{:S(2)}) collective-permute-start(bf16[512,768]{1,0:T(8,128)(2,1)S(1)} %get-tuple-element.352), channel_id=1, source_target_pairs={{0,4},{4,8},{8,12},{12,16},{16,20},{20,24},{24,28},{1,5},{5,9},{9,... | collective-permute-start | bytes 2359304 | tf_op jit(solution)/shard_map/ppermute | solution.py:632
  72.7 41.5 %collective-permute-start.8 = (bf16[512,768]{1,0:T(8,128)(2,1)S(1)}, bf16[512,768]{1,0:T(8,128)(2,1)S(1)}, u32[]{:S(2)}, u32[]{:S(2)}) collective-permute-start(bf16[512,768]{1,0:T(8,128)(2,1)S(1)} %get-tuple-element.351), channel_id=1, source_target_pairs={{4,0},{8,4},{12,8},{16,12},{20,16},{24,20},{28,24},{5,1},{9,5},{13... | collective-permute-start | bytes 2359304 | tf_op jit(solution)/shard_map/ppermute | solution.py:633
  183.6 443.1 %reduce-scatter.4.cloned.1.call-start = ((), (), s32[]{:S(2)}) async-start(), calls=%async_computation.3 | async-start | bytes 11151360
  185.7 33.4 %collective-permute-start.12 = (bf16[4,24,3200]{2,1,0:T(8,128)(2,1)S(1)}, bf16[4,24,3200]{2,1,0:T(8,128)(2,1)S(1)}, u32[]{:S(2)}, u32[]{:S(2)}) collective-permute-start(bf16[4,24,3200]{2,1,0:T(8,128)(2,1)S(1)} %bitcast_dynamic-update-slice_fusion.12), channel_id=1, source_target_pairs={{0,2},{1,3},{2,0},{3,1},{4,6},{5,7},{6,4},{7,5},{8,10},{9,11},{10,... | collective-permute-start | bytes 1843208 | tf_op jit(solution)/shard_map/ppermute | solution.py:653
  188.4 30.8 %collective-permute-start.13 = (bf16[4,24,3200]{2,1,0:T(8,128)(2,1)S(1)}, bf16[4,24,3200]{2,1,0:T(8,128)(2,1)S(1)}, u32[]{:S(2)}, u32[]{:S(2)}) collective-permute-start(bf16[4,24,3200]{2,1,0:T(8,128)(2,1)S(1)} %bitcast_dynamic-update-slice_fusion.12), channel_id=1, source_target_pairs={{0,4},{1,5},{2,6},{3,7},{4,0},{5,1},{6,2},{7,3},{8,12},{9,13},{10,... | collective-permute-start | bytes 1843208 | tf_op jit(solution)/shard_map/ppermute | solution.py:653
  190.6 28.7 %collective-permute-start.14 = (bf16[4,24,3200]{2,1,0:T(8,128)(2,1)S(1)}, bf16[4,24,3200]{2,1,0:T(8,128)(2,1)S(1)}, u32[]{:S(2)}, u32[]{:S(2)}) collective-permute-start(bf16[4,24,3200]{2,1,0:T(8,128)(2,1)S(1)} %bitcast_dynamic-update-slice_fusion.12), channel_id=1, source_target_pairs={{0,6},{1,7},{2,4},{3,5},{4,2},{5,3},{6,0},{7,1},{8,14},{9,15},{10,... | collective-permute-start | bytes 1843208 | tf_op jit(solution)/shard_map/ppermute | solution.py:653
  219.3 49.3 %collective-permute-start.15 = (bf16[4,4,24,3200]{3,2,0,1:T(8,128)(2,1)S(1)}, bf16[4,4,24,3200]{3,2,0,1:T(8,128)(2,1)}, u32[]{:S(2)}, u32[]{:S(2)}) collective-permute-start(bf16[4,4,24,3200]{3,2,0,1:T(8,128)(2,1)S(1)} %bitcast_dynamic-update-slice_fusion.7), channel_id=1, source_target_pairs={{0,1},{1,0},{2,3},{3,2},{4,5},{5,4},{6,7},{7,6},{8,9},{9,8},{10,11... | collective-permute-start | bytes 7372808 | tf_op jit(solution)/shard_map/ppermute | solution.py:653
  221.2 47.2 %collective-permute-start.16 = (bf16[512,768]{1,0:T(8,128)(2,1)S(1)}, bf16[512,768]{1,0:T(8,128)(2,1)S(1)}, u32[]{:S(2)}, u32[]{:S(2)}) collective-permute-start(bf16[512,768]{1,0:T(8,128)(2,1)S(1)} %get-tuple-element.350), channel_id=1, source_target_pairs={{0,4},{4,8},{8,12},{12,16},{16,20},{20,24},{24,28},{1,5},{5,9},{9,... | collective-permute-start | bytes 2359304 | tf_op jit(solution)/shard_map/ppermute | solution.py:632
  224.6 44.0 %collective-permute-start.17 = (bf16[512,768]{1,0:T(8,128)(2,1)S(1)}, bf16[512,768]{1,0:T(8,128)(2,1)S(1)}, u32[]{:S(2)}, u32[]{:S(2)}) collective-permute-start(bf16[512,768]{1,0:T(8,128)(2,1)S(1)} %get-tuple-element.349), channel_id=1, source_target_pairs={{4,0},{8,4},{12,8},{16,12},{20,16},{24,20},{28,24},{5,1},{9,5},{13... | collective-permute-start | bytes 2359304 | tf_op jit(solution)/shard_map/ppermute | solution.py:633
  442.2 39.7 %collective-permute-start.19 = (bf16[512,768]{1,0:T(8,128)(2,1)}, bf16[512,768]{1,0:T(8,128)(2,1)S(1)}, u32[]{:S(2)}, u32[]{:S(2)}) collective-permute-start(bf16[512,768]{1,0:T(8,128)(2,1)} %get-tuple-element.347), channel_id=1, source_target_pairs={{4,0},{8,4},{12,8},{16,12},{20,16},{24,20},{28,24},{5,1},{9,5},{13... | collective-permute-start | bytes 2359304 | tf_op jit(solution)/shard_map/ppermute | solution.py:633
  554.0 73.8 %collective-permute-start.21 = (bf16[4,24,9472]{2,1,0:T(8,128)(2,1)}, bf16[4,24,9472]{2,1,0:T(8,128)(2,1)S(1)}, u32[]{:S(2)}, u32[]{:S(2)}) collective-permute-start(bf16[4,24,9472]{2,1,0:T(8,128)(2,1)} %get-tuple-element.291), channel_id=1, source_target_pairs={{0,2},{1,3},{2,0},{3,1},{4,6},{5,7},{6,4},{7,5},{8,10},{9,11},{10,... | collective-permute-start | bytes 5455880 | tf_op jit(solution)/shard_map/ppermute | solution.py:653
  567.8 87.9 %collective-permute-start.22 = (bf16[4,24,9472]{2,1,0:T(8,128)(2,1)}, bf16[4,24,9472]{2,1,0:T(8,128)(2,1)}, u32[]{:S(2)}, u32[]{:S(2)}) collective-permute-start(bf16[4,24,9472]{2,1,0:T(8,128)(2,1)} %get-tuple-element.292), channel_id=1, source_target_pairs={{0,4},{1,5},{2,6},{3,7},{4,0},{5,1},{6,2},{7,3},{8,12},{9,13},{10,... | collective-permute-start | bytes 5455880 | tf_op jit(solution)/shard_map/ppermute | solution.py:653
  576.7 79.0 %collective-permute-start.23 = (bf16[4,24,9472]{2,1,0:T(8,128)(2,1)}, bf16[4,24,9472]{2,1,0:T(8,128)(2,1)}, u32[]{:S(2)}, u32[]{:S(2)}) collective-permute-start(bf16[4,24,9472]{2,1,0:T(8,128)(2,1)} %get-tuple-element.293), channel_id=1, source_target_pairs={{0,6},{1,7},{2,4},{3,5},{4,2},{5,3},{6,0},{7,1},{8,14},{9,15},{10,... | collective-permute-start | bytes 5455880 | tf_op jit(solution)/shard_map/ppermute | solution.py:653
  626.7 54.1 %collective-permute-start.24 = (bf16[4,4,24,2432]{3,2,1,0:T(8,128)(2,1)}, bf16[4,4,24,2432]{3,2,1,0:T(8,128)(2,1)}, u32[]{:S(2)}, u32[]{:S(2)}) collective-permute-start(bf16[4,4,24,2432]{3,2,1,0:T(8,128)(2,1)} %get-tuple-element.299), channel_id=1, source_target_pairs={{0,1},{1,0},{2,3},{3,2},{4,5},{5,4},{6,7},{7,6},{8,9},{9,8},{10,11... | collective-permute-start | bytes 5603336 | tf_op jit(solution)/shard_map/ppermute | solution.py:653
  659.2 27.5 %collective-permute-start.33 = (bf16[24,9472]{1,0:T(8,128)(2,1)S(1)}, bf16[24,9472]{1,0:T(8,128)(2,1)S(1)}, u32[]{:S(2)}, u32[]{:S(2)}) collective-permute-start(bf16[24,9472]{1,0:T(8,128)(2,1)S(1)} %get-tuple-element.311), channel_id=1, source_target_pairs={{0,8},{1,9},{2,10},{3,11},{4,12},{5,13},{6,14},{7,15},{8,0},{9,1},... | collective-permute-start | bytes 1363976 | tf_op jit(solution)/shard_map/ppermute | solution.py:653
  660.3 38.4 %collective-permute-start.34 = (bf16[24,9472]{1,0:T(8,128)(2,1)S(1)}, bf16[24,9472]{1,0:T(8,128)(2,1)S(1)}, u32[]{:S(2)}, u32[]{:S(2)}) collective-permute-start(bf16[24,9472]{1,0:T(8,128)(2,1)S(1)} %get-tuple-element.312), channel_id=1, source_target_pairs={{0,16},{1,17},{2,18},{3,19},{4,20},{5,21},{6,22},{7,23},{8,24},{9,... | collective-permute-start | bytes 1363976 | tf_op jit(solution)/shard_map/ppermute | solution.py:653
  667.9 33.9 %collective-permute-start.35 = (bf16[24,9472]{1,0:T(8,128)(2,1)S(1)}, bf16[24,9472]{1,0:T(8,128)(2,1)S(1)}, u32[]{:S(2)}, u32[]{:S(2)}) collective-permute-start(bf16[24,9472]{1,0:T(8,128)(2,1)S(1)} %get-tuple-element.313), channel_id=1, source_target_pairs={{0,24},{1,25},{2,26},{3,27},{4,28},{5,29},{6,30},{7,31},{8,16},{9,... | collective-permute-start | bytes 1363976 | tf_op jit(solution)/shard_map/ppermute | solution.py:653
  683.6 44.5 %collective-permute-start.25 = (bf16[4,24,2432]{2,1,0:T(8,128)(2,1)}, bf16[4,24,2432]{2,1,0:T(8,128)(2,1)}, u32[]{:S(2)}, u32[]{:S(2)}) collective-permute-start(bf16[4,24,2432]{2,1,0:T(8,128)(2,1)} %get-tuple-element.303), channel_id=1, source_target_pairs={{0,2},{1,3},{2,0},{3,1},{4,6},{5,7},{6,4},{7,5},{8,10},{9,11},{10,... | collective-permute-start | bytes 1400840 | tf_op jit(solution)/shard_map/ppermute | solution.py:653
  683.9 44.2 %collective-permute-start.26 = (bf16[4,24,2432]{2,1,0:T(8,128)(2,1)}, bf16[4,24,2432]{2,1,0:T(8,128)(2,1)}, u32[]{:S(2)}, u32[]{:S(2)}) collective-permute-start(bf16[4,24,2432]{2,1,0:T(8,128)(2,1)} %get-tuple-element.304), channel_id=1, source_target_pairs={{0,4},{1,5},{2,6},{3,7},{4,0},{5,1},{6,2},{7,3},{8,12},{9,13},{10,... | collective-permute-start | bytes 1400840 | tf_op jit(solution)/shard_map/ppermute | solution.py:653
  686.6 41.5 %collective-permute-start.27 = (bf16[4,24,2432]{2,1,0:T(8,128)(2,1)}, bf16[4,24,2432]{2,1,0:T(8,128)(2,1)}, u32[]{:S(2)}, u32[]{:S(2)}) collective-permute-start(bf16[4,24,2432]{2,1,0:T(8,128)(2,1)} %get-tuple-element.305), channel_id=1, source_target_pairs={{0,6},{1,7},{2,4},{3,5},{4,2},{5,3},{6,0},{7,1},{8,14},{9,15},{10,... | collective-permute-start | bytes 1400840 | tf_op jit(solution)/shard_map/ppermute | solution.py:653
  698.7 53.0 %collective-permute-start.28 = (bf16[512,768]{1,0:T(8,128)(2,1)}, bf16[512,768]{1,0:T(8,128)(2,1)}, u32[]{:S(2)}, u32[]{:S(2)}) collective-permute-start(bf16[512,768]{1,0:T(8,128)(2,1)} %get-tuple-element.346), channel_id=1, source_target_pairs={{0,4},{4,8},{8,12},{12,16},{16,20},{20,24},{24,28},{1,5},{5,9},{9,... | collective-permute-start | bytes 2359304 | tf_op jit(solution)/shard_map/ppermute | solution.py:632
  701.7 51.7 %collective-permute-start.29 = (bf16[512,768]{1,0:T(8,128)(2,1)}, bf16[512,768]{1,0:T(8,128)(2,1)}, u32[]{:S(2)}, u32[]{:S(2)}) collective-permute-start(bf16[512,768]{1,0:T(8,128)(2,1)} %get-tuple-element.345), channel_id=1, source_target_pairs={{4,0},{8,4},{12,8},{16,12},{20,16},{24,20},{28,24},{5,1},{9,5},{13... | collective-permute-start | bytes 2359304 | tf_op jit(solution)/shard_map/ppermute | solution.py:633
  (92 other events, 1458.0 us)
Sparse Core Ops, SparseCore 0:
  63.8 97.4 all-gather.2
  183.7 111.4 all-gather.4
  387.0 178.4 reduce-scatter.3

commit v3 on v2

--- a/solution.py
+++ b/solution.py
@@ -157,6 +157,29 @@
 
 def vmem():
     return pl.BlockSpec(memory_space=pltpu.VMEM)
+
+
+def unwiden_kernel(a, b, out):
+    share = a.shape[0]
+    for n, ref in enumerate((a, b)):
+        for d in range(D // share):
+            pieces = [ref[:, j * D + share * d : j * D + share * (d + 1)] for j in range(FF // D)]
+            for j, piece in enumerate(pieces):
+                at = FF // D * share * d + share * j
+                out[n, :, at : at + share] = piece
+
+
+def unwiden(a, b):
+    share = a.shape[0]
+    return pl.pallas_call(
+        unwiden_kernel,
+        grid=(1,),
+        in_specs=[pl.BlockSpec((share, FF), lambda i: (0, 0))] * 2,
+        out_specs=pl.BlockSpec((2, share, FF), lambda i: (0, 0, 0)),
+        out_shape=jax.ShapeDtypeStruct((2, share, FF), F32),
+        cost_estimate=cost(2),
+        name="unwiden",
+    )(a, b)
 
 
 def attend(flags, keep, pos, factor, q_t, k, v_t):
@@ -322,7 +345,7 @@
             pltpu.SMEM((ext,), jnp.int32),
         ],
         compiler_params=pltpu.CompilerParams(vmem_limit_bytes=56 * 2**20),
-        cost_estimate=cost(5),
+        cost_estimate=cost(1),
         name="attend_back",
     )(flags, keep, pos, log_factor, inv_factor, q_t, q, dc_t, dc, ctx_t, lse, k, k_t, v)
 
@@ -427,7 +450,7 @@
                    jax.ShapeDtypeStruct((n, D), BF16), jax.ShapeDtypeStruct((n, D), BF16), jax.ShapeDtypeStruct((D, n), BF16),
                    jax.ShapeDtypeStruct((8, D), F32), jax.ShapeDtypeStruct((1, FF), F32)],
         compiler_params=pltpu.CompilerParams(vmem_limit_bytes=56 * 2**20),
-        cost_estimate=cost(3),
+        cost_estimate=cost(1),
         name="ffn_back",
     )(grad, second, first, slope, w12, w12, wo, gains)
 
@@ -496,7 +519,7 @@
         out_shape=jax.ShapeDtypeStruct((D, width), BF16),
         scratch_shapes=[pltpu.VMEM((D, n), BF16)],
         compiler_params=pltpu.CompilerParams(vmem_limit_bytes=56 * 2**20),
-        cost_estimate=cost(3),
+        cost_estimate=cost(1),
         name="ffn_grads",
     )(*args)
 
@@ -586,7 +609,7 @@
         out_shape=jax.ShapeDtypeStruct((D, 3 * D + 128), BF16),
         scratch_shapes=[pltpu.VMEM((D, n), BF16)],
         compiler_params=pltpu.CompilerParams(vmem_limit_bytes=48 * 2**20),
-        cost_estimate=cost(3),
+        cost_estimate=cost(1),
         name="att_grads",
     )(low_ext, dq_t, dk, dv, dr, rate)
 
@@ -621,7 +644,7 @@
         out_specs=[orow, rrow],
         out_shape=[jax.ShapeDtypeStruct((own, D), F32), jax.ShapeDtypeStruct((n - own, D), BF16)],
         compiler_params=pltpu.CompilerParams(vmem_limit_bytes=40 * 2**20),
-        cost_estimate=cost(3),
+        cost_estimate=cost(1),
         name="input_back",
     )(dk, dv, dq_t, dfirst, w)
 
@@ -757,11 +780,12 @@
     return jnp.repeat(rows, BLK, axis=2)
 
 
-def layer_forward(hidden, low_ext, head, vec, flags, keep, temper, pos, between):
+def layer_forward(hidden, low_ext, head, vec, flags, keep, temper, pos, before, between):
     z = (vec["logits"] + vec["jitter"]).reshape(HEADS, SPAN, SPAN) / temper[:, None, None]
     relaxed = jax.nn.sigmoid(z)
     factor = table_rows(relaxed)
     q, q_t, k, k_t, v, v_t = project(low_ext, head, vec["qb"][None], vec["vb"][None])
+    q_t = before(q_t)
     log_factor, inv_factor = jnp.log2(factor), 1.0 / factor
     ctx_t, lse = attend(flags, keep, pos, factor, q_t, k, v_t)
     ctx_t, wo, wo_at, w12 = between(ctx_t)
@@ -847,10 +871,6 @@
         lead = part.shape[:-1]
         return jnp.swapaxes(part.reshape(lead + (devices, 4, share)), -3, -2).reshape(lead + (FF,))
 
-    def unwidened(part):
-        lead = part.shape[:-1]
-        return jnp.swapaxes(part.reshape(lead + (4, devices, share)), -3, -2).reshape(lead + (FF,))
-
     def own_parts(tier):
         narrow = w2[tier].reshape(4, share, D)
         vectors = jnp.stack(
@@ -873,19 +893,19 @@
     symbols = embedded[0]
     first, wide, out, vectors = own_parts(0)
     gather = SteppedGather(jnp.concatenate(first + vectors, 1))
-    for _ in range(3):
-        symbols = gather.advance(symbols)
+    symbols = gather.advance(symbols)
+    symbols, rest = lax.optimization_barrier((symbols, jnp.concatenate(wide + out, 1)))
+    symbols = gather.advance(gather.advance(symbols))
     lower, upper = neighbours(symbols[symbols.shape[0] - rim :], symbols[:rim])
     low_ext = jnp.concatenate([lower, symbols, upper], 0)
     head_zero = gather.result(symbols)
-    head_zero, *rest = lax.optimization_barrier((head_zero, *wide, *out))
-    tail_zero = gathered(jnp.concatenate(rest, 1))
+    head_zero, rest = lax.optimization_barrier((head_zero, rest))
+    tail_zero = gathered(rest)
     first, wide, out, vectors = own_parts(1)
     later = SteppedGather(jnp.concatenate(first + out + vectors, 1))
     tails = []
 
     def between_zero(ctx_t):
-        ctx_t = later.advance(ctx_t)
         ctx_t = later.advance(ctx_t)
         _, _, *rest = lax.optimization_barrier((ctx_t, tail_zero, *wide))
         tails.append(gathered(jnp.concatenate(rest, 1)))
@@ -903,6 +923,7 @@
         selector[0, 0],
         warmth[0],
         pos,
+        later.advance,
         between_zero,
     )
     records = [record]
@@ -919,6 +940,7 @@
         selector[1, 0],
         warmth[1],
         pos,
+        lambda q_t: q_t,
         between_one,
     )
     records.append(record)
@@ -936,7 +958,7 @@
     av = jnp.stack([last[:, 3 * D :], both[:, ends[1] + BLK :]])
     ffn_sums = jnp.stack([both[:, : ends[0]], ffn_one[:, : ends[0]]])
     att = jnp.stack([last[:, : 3 * D], both[:, ends[0] : ends[1]]])
-    w1_grad = unwidened(ffn_sums[:, :, :FF])
+    w1_grad = unwiden(both, ffn_one)
     w2_grad = jnp.concatenate([ffn_sums[:, :, FF + j * D : FF + (j + 1) * D] for j in range(4)], 1)
     wo_grad = ffn_sums[:, :, 2 * FF :]
     b1_grad = jnp.concatenate([fv[:, :, 8 + j] for j in range(4)], 1)

time: 765 us -> 752 us (0.983)
  waiting for transfers between devices: 196 us -> 174 us
  starting transfers between devices: 92.6 us -> 111 us
  Pallas kernels: 306 us -> 298 us
    ppermute x4, starting transfers between devices: 12.8 us -> 41 us  [neighbours(): lax.ppermute(tail, 'dp', [(i, i + 1) for i in range(count - 1)])]
    ppermute x4, waiting for transfers between devices: 21.5 us -> 0.01 us  [neighbours(): lax.ppermute(head, 'dp', [(i + 1, i) for i in range(count - 1)])]
    all_gather x2, waiting for transfers between devices: 0.02 us -> 20.1 us  [gathered(): return lax.all_gather(part, AXES, axis=0, tiled=True)]
    ppermute x28, waiting for transfers between devices: 93 us -> 75 us  [swap(): return lax.ppermute(block, AXES, [(i, i ^ mask) for i in range(count)])]
    unnamed x176 -> x167, local copies, waits for them, and re-layouts: 43.3 us -> 54.5 us
    ppermute x28, starting transfers between devices: 73.7 us -> 63.3 us  [swap(): return lax.ppermute(block, AXES, [(i, i ^ mask) for i in range(count)])]
    reshape x2 -> x0, local copies, waits for them, and re-layouts: 10.2 us -> none  [the longest x1 5.73 us: unwidened(): jnp.swapaxes(part.reshape(lead + (4, devices, share)), -3, -2)]
  transfers between devices with their start and end apart: 39 -> 39, of which waited for: 14 -> 15; matrix products, arithmetic and copies ran while one was open for 13% -> 13% of each run, Pallas kernels for 31% -> 30%
where the time goes in v3:
time: 752 us; the launch traced here: 750 us
  Pallas kernels  298 us (40%)
  waiting for transfers between devices  174 us (23%)
  starting transfers between devices  111 us (15%)
  local copies, waits for them, and re-layouts  110 us (15%)
  other arithmetic  41.3 us (5%)
  between operations  15.6 us (2%)
    ppermute x4, waiting for transfers between devices, neighbours(): lax.ppermute(tail, 'dp', [(i, i + 1) for i in range(count - 1)])  78.8 us
    ppermute x28, waiting for transfers between devices, swap(): return lax.ppermute(block, AXES, [(i, i ^ mask) for i in range(count)])  75 us
    ppermute x28, starting transfers between devices, swap(): return lax.ppermute(block, AXES, [(i, i ^ mask) for i in range(count)])  63.3 us
    pallas_call x2, Pallas kernels, attend_back(): pl.pallas_call(backward_kernel, out_shape=(jax.ShapeDtypeStruct(q_t.shape...  56.9 us
    pallas_call x2, Pallas kernels, ffn(): pl.pallas_call(ffn_kernel, grid=(n // ROWS,), in_specs=[pl.BlockSpec((D,...  56.6 us
    unnamed x167, local copies, waits for them, and re-layouts  54.5 us
    pallas_call x2, Pallas kernels, ffn_back(): pl.pallas_call(ffn_back_kernel, grid=(n // ROWS,), in_specs=[row(D), row(...  46.6 us
    pallas_call x2, Pallas kernels, ffn_grads(): pl.pallas_call(functools.partial(ffn_grads_kernel, extra), grid=(2 * bloc...  45.6 us
  transfers between devices with their start and end apart: 39, of which 15 were waited for; matrix products, arithmetic and copies ran while one was open for 13% of the time, Pallas kernels for 30%

profile of v3, /device:TPU:0, one launch (start us, length us, event | category | flops | bytes accessed | tf_op | source)
XLA Modules:
  0.0 749.6 jit_solution(3221557876255682288)
XLA Ops:
  33.5 10.0 %collective-permute-done.3 = bf16[4,24,2432]{2,1,0:T(8,128)(2,1)S(1)} collective-permute-done((bf16[4,24,2432]{2,1,0:T(8,128)(2,1)S(1)}, bf16[4,24,2432]{2,1,0:T(8,128)(2,1)S(1)}, u32[]{:S(2)}, u32[]{:S(2)}) %collective-permute-start.3) | collective-permute-done | bytes 466976 | tf_op jit(solution)/shard_map/ppermute | solution.py:676
  43.5 9.4 %collective-permute-done.4 = bf16[4,24,2432]{2,1,0:T(8,128)(2,1)S(1)} collective-permute-done((bf16[4,24,2432]{2,1,0:T(8,128)(2,1)S(1)}, bf16[4,24,2432]{2,1,0:T(8,128)(2,1)S(1)}, u32[]{:S(2)}, u32[]{:S(2)}) %collective-permute-start.4) | collective-permute-done | bytes 466976 | tf_op jit(solution)/shard_map/ppermute | solution.py:676
  73.5 28.1 %collective-permute-done.7 = bf16[512,768]{1,0:T(8,128)(2,1)} collective-permute-done((bf16[512,768]{1,0:T(8,128)(2,1)}, bf16[512,768]{1,0:T(8,128)(2,1)}, u32[]{:S(2)}, u32[]{:S(2)}) %collective-permute-start.7) | collective-permute-done | bytes 786464 | tf_op jit(solution)/shard_map/ppermute | solution.py:655
  110.5 13.2 %project.2 = (bf16[1024,768]{1,0:T(8,128)(2,1)S(1)}, bf16[768,1024]{1,0:T(8,128)(2,1)S(1)}, bf16[2048,768]{1,0:T(8,128)(2,1)S(1)}, bf16[768,2048]{1,0:T(8,128)(2...) custom-call(bf16[2048,768]{1,0:T(8,128)(2,1)} %copy-done.13, bf16[768,2432]{1,0:T(8,128)(2,1)} %bitcast.43.w, ...), custom_call_target="tpu_custom_call" | custom-call | flops 14000000000 | bytes 1000000 | tf_op jit(solution)/shard_map/project/pallas_call | solution.py:557
  155.3 20.1 %all-gather.3.cloned.1.call-done.wo.w1.w2 = bf16[768,6912]{1,0:T(8,128)(2,1)} async-done(((bf16[24,6912]{1,0:T(8,128)(2,1)}), bf16[768,6912]{1,0:T(8,128)(2,1)}) %all-gather.3.cloned.1.call-update) | async-done | bytes 10616848 | tf_op jit(solution)/shard_map/all_gather | solution.py:661
  182.1 28.3 %ffn.2 = (f32[1024,768]{1,0:T(8,128)}, bf16[1024,768]{1,0:T(8,128)(2,1)}, bf16[1024,3072]{1,0:T(8,128)(2,1)}, bf16[1024,3072]{1,0:T(8,128)(2,1)}, f32[1024,768]{...) custom-call(f32[768,1024]{1,0:T(8,128)} %copy-done.1, bf16[1024,768]{1,0:T(8,128)(2,1)} %bitcast.363, ...), custom_call_target="tpu_custom_call" | custom-call | flops 28000000000 | bytes 1000000 | tf_op jit(solution)/shard_map/ffn/pallas_call | solution.py:394
  220.3 45.5 %collective-permute-done.16 = bf16[512,768]{1,0:T(8,128)(2,1)S(1)} collective-permute-done((bf16[512,768]{1,0:T(8,128)(2,1)S(1)}, bf16[512,768]{1,0:T(8,128)(2,1)S(1)}, u32[]{:S(2)}, u32[]{:S(2)}) %collective-permute-start.16) | collective-permute-done | bytes 786464 | tf_op jit(solution)/shard_map/ppermute | solution.py:655
  276.2 13.5 %project.3 = (bf16[1024,768]{1,0:T(8,128)(2,1)S(1)}, bf16[768,1024]{1,0:T(8,128)(2,1)S(1)}, bf16[2048,768]{1,0:T(8,128)(2,1)S(1)}, bf16[768,2048]{1,0:T(8,128)(2...) custom-call(bf16[2048,768]{1,0:T(8,128)(2,1)} %copy-done.11, bf16[768,3200]{1,0:T(8,128)(2,1)} %bitcast.357, ...), custom_call_target="tpu_custom_call" | custom-call | flops 14000000000 | bytes 1000000 | tf_op jit(solution)/shard_map/project/pallas_call | solution.py:557
  308.9 28.3 %ffn.3 = (f32[1024,768]{1,0:T(8,128)}, bf16[1024,768]{1,0:T(8,128)(2,1)}, bf16[1024,3072]{1,0:T(8,128)(2,1)}, bf16[1024,3072]{1,0:T(8,128)(2,1)}, f32[1024,768]{...) custom-call(f32[768,1024]{1,0:T(8,128)} %copy-done.4, f32[1024,768]{1,0:T(8,128)} %get-tuple-element.223.hidden, ...), custom_call_target="tpu_custom_call" | custom-call | flops 28000000000 | bytes 1000000 | tf_op jit(solution)/shard_map/ffn/pallas_call | solution.py:394
  337.1 23.1 %ffn_back.2 = (bf16[1024,768]{1,0:T(8,128)(2,1)}, bf16[1024,3072]{1,0:T(8,128)(2,1)}, f32[1024,768]{1,0:T(8,128)}, bf16[1024,768]{1,0:T(8,128)(2,1)}, bf16[1024,...) custom-call(bf16[1024,768]{1,0:T(8,128)(2,1)} %bitcast.367, ...), custom_call_target="tpu_custom_call" | custom-call | flops 1000000000 | bytes 1000000 | tf_op jit(solution)/shard_map/ffn_back/pallas_call | solution.py:444
  360.2 20.7 %ffn_grads.2 = bf16[768,7040]{1,0:T(8,128)(2,1)} custom-call(bf16[1024,768]{1,0:T(8,128)(2,1)} %get-tuple-element.237.normed, bf16[1024,3072]{1,0:T(8,128)(2,1)} %get-tuple-element.238.dinner, bf16[1024,3072]{1,0:T(8,128)(2,1)} %get-tuple-element.239.active, bf16[1024,768]{1,0:T(8,128)(2,1)} %get-tuple-element.240.douter, f32[768,1024]{1,0:T(8,128)} %copy-done.4, ...), custom_call_target="tpu_custom_call" | custom-call | flops 1000000000 | bytes 1000000 | tf_op jit(solution)/shard_map/ffn_grads/pallas_call | solution.py:514
  382.1 27.6 %attend_back.2 = (bf16[768,1024]{1,0:T(8,128)(2,1)}, bf16[2048,768]{1,0:T(8,128)(2,1)}, bf16[2048,768]{1,0:T(8,128)(2,1)}, f32[64,8,128]{2,1,0:T(8,128)}) custom-call(s32[64]{0:T(128)} %bitcast.351, s32[8,15]{1,0:T(8,128)} %copy-done.32, s32[1]{0:T(128)} %bitcast.2.pos, f32[64,6,256]{2,1,0:T(8,128)} %copy_multiply_fusion.log_factor, ...), custom_call_target="tpu_custom_call" | custom-call | flops 1000000000 | bytes 1000000 | tf_op jit(solution)/shard_map/attend_back/pallas_call | solution.py:324
  415.2 11.6 %input_back.2 = (f32[1024,768]{1,0:T(8,128)S(1)}, bf16[1024,768]{1,0:T(8,128)(2,1)S(1)}) custom-call(bf16[2048,768]{1,0:T(8,128)(2,1)S(1)} %copy-done.5, bf16[2048,768]{1,0:T(8,128)(2,1)S(1)} %copy-done.6, bf16[768,1024]{1,0:T(8,128)(2,1)S(1)} %copy-done.9, f32[1024,768]{1,0:T(8,128)} %get-tuple-element.251.dfirst, bf16[768,3200]{1,0:T(8,128)(2,1)} %bitcast.360), custom_call_target="tpu_custom_call" | custom-call | flops 1000000000 | bytes 1000000 | tf_op jit(solution)/shard_map/input_back/pallas_call | solution.py:640
  428.1 29.0 %collective-permute-start.18 = (bf16[512,768]{1,0:T(8,128)(2,1)}, bf16[512,768]{1,0:T(8,128)(2,1)}, u32[]{:S(2)}, u32[]{:S(2)}) collective-permute-start(bf16[512,768]{1,0:T(8,128)(2,1)} %get-tuple-element.342), channel_id=1, source_target_pairs={{0,4},{4,8},{8,12},{12,16},{16,20},{20,24},{24,28},{1,5},{5,9},{9,... | collective-permute-start | bytes 2359304 | tf_op jit(solution)/shard_map/ppermute | solution.py:655
  464.2 11.6 %att_grads.2.rest_0_.rest_1_ = bf16[768,2432]{1,0:T(8,128)(2,1)} custom-call(bf16[2048,768]{1,0:T(8,128)(2,1)S(1)} %copy-done.12, bf16[768,1024]{1,0:T(8,128)(2,1)S(1)} %copy-done.10, bf16[2048,768]{1,0:T(8,128)(2,1)} %get-tuple-element.248.dk, bf16[2048,768]{1,0:T(8,128)(2,1)} %get-tuple-element.249.dv, f32[64,8,128]{2,1,0:T(8,128)S(1)} %copy-done.27, ...), custom_call_target="tpu_custom_call" | custom-call | flops 1000000000 | bytes 1000000 | tf_op jit(solution)/shard_map/att_grads/pallas_call | solution.py:604
  485.8 23.6 %ffn_back.3 = (bf16[1024,768]{1,0:T(8,128)(2,1)}, bf16[1024,3072]{1,0:T(8,128)(2,1)}, f32[1024,768]{1,0:T(8,128)}, bf16[1024,768]{1,0:T(8,128)(2,1)}, bf16[1024,...) custom-call(f32[1024,768]{1,0:T(8,128)} %copy-done, ...), custom_call_target="tpu_custom_call" | custom-call | flops 1000000000 | bytes 1000000 | tf_op jit(solution)/shard_map/ffn_back/pallas_call | solution.py:444
  509.4 24.8 %ffn_grads.3 = bf16[768,9472]{1,0:T(8,128)(2,1)} custom-call(bf16[1024,768]{1,0:T(8,128)(2,1)} %get-tuple-element.259.normed, bf16[1024,3072]{1,0:T(8,128)(2,1)} %get-tuple-element.260.dinner, bf16[1024,3072]{1,0:T(8,128)(2,1)} %get-tuple-element.261.active, bf16[1024,768]{1,0:T(8,128)(2,1)} %get-tuple-element.262.douter, f32[768,1024]{1,0:T(8,128)} %copy-done.1, ...), custom_call_target="tpu_custom_call" | custom-call | flops 1000000000 | bytes 1000000 | tf_op jit(solution)/shard_map/ffn_grads/pallas_call | solution.py:514
  540.3 11.6 %collective-permute-done.20 = bf16[4,4,24,9472]{3,2,1,0:T(8,128)(2,1)} collective-permute-done((bf16[4,4,24,9472]{3,2,1,0:T(8,128)(2,1)S(1)}, bf16[4,4,24,9472]{3,2,1,0:T(8,128)(2,1)}, u32[]{:S(2)}, u32[]{:S(2)}) %collective-permute-start.20) | collective-permute-done | bytes 7274528 | tf_op jit(solution)/shard_map/ppermute | solution.py:676
  557.7 20.5 %collective-permute-start.21 = (bf16[4,24,9472]{2,1,0:T(8,128)(2,1)}, bf16[4,24,9472]{2,1,0:T(8,128)(2,1)S(1)}, u32[]{:S(2)}, u32[]{:S(2)}) collective-permute-start(bf16[4,24,9472]{2,1,0:T(8,128)(2,1)} %get-tuple-element.285), channel_id=1, source_target_pairs={{0,2},{1,3},{2,0},{3,1},{4,6},{5,7},{6,4},{7,5},{8,10},{9,11},{10,... | collective-permute-start | bytes 5455880 | tf_op jit(solution)/shard_map/ppermute | solution.py:676
  583.2 29.3 %attend_back.3 = (bf16[768,1024]{1,0:T(8,128)(2,1)}, bf16[2048,768]{1,0:T(8,128)(2,1)}, bf16[2048,768]{1,0:T(8,128)(2,1)}, f32[64,8,128]{2,1,0:T(8,128)}) custom-call(s32[64]{0:T(128)} %bitcast.352, s32[8,15]{1,0:T(8,128)} %copy-done.31, s32[1]{0:T(128)} %bitcast.2.pos, f32[64,6,256]{2,1,0:T(8,128)} %copy_multiply_fusion.1.log_factor, ...), custom_call_target="tpu_custom_call" | custom-call | flops 1000000000 | bytes 1000000 | tf_op jit(solution)/shard_map/attend_back/pallas_call | solution.py:324
  614.9 11.7 %att_grads.3 = bf16[768,2432]{1,0:T(8,128)(2,1)} custom-call(bf16[2048,768]{1,0:T(8,128)(2,1)S(1)} %copy-done.14, bf16[768,1024]{1,0:T(8,128)(2,1)S(1)} %copy-done.7, bf16[2048,768]{1,0:T(8,128)(2,1)} %get-tuple-element.288.dk, bf16[2048,768]{1,0:T(8,128)(2,1)} %get-tuple-element.278.dv, f32[64,8,128]{2,1,0:T(8,128)S(1)} %copy-done.28, ...), custom_call_target="tpu_custom_call" | custom-call | flops 1000000000 | bytes 1000000 | tf_op jit(solution)/shard_map/att_grads/pallas_call | solution.py:604
  636.5 23.4 %collective-permute-done.22 = bf16[4,24,9472]{2,1,0:T(8,128)(2,1)} collective-permute-done((bf16[4,24,9472]{2,1,0:T(8,128)(2,1)}, bf16[4,24,9472]{2,1,0:T(8,128)(2,1)}, u32[]{:S(2)}, u32[]{:S(2)}) %collective-permute-start.22) | collective-permute-done | bytes 1818656 | tf_op jit(solution)/shard_map/ppermute | solution.py:676
  667.8 11.5 %input_back.3 = (f32[1024,768]{1,0:T(8,128)S(1)}, bf16[1024,768]{1,0:T(8,128)(2,1)S(1)}) custom-call(bf16[2048,768]{1,0:T(8,128)(2,1)S(1)} %copy-done.2, bf16[2048,768]{1,0:T(8,128)(2,1)S(1)} %copy-done.3, bf16[768,1024]{1,0:T(8,128)(2,1)S(1)} %copy-done.8, f32[1024,768]{1,0:T(8,128)} %get-tuple-element.289.dfirst, bf16[768,2432]{1,0:T(8,128)(2,1)} %bitcast.43.w), custom_call_target="tpu_custom_call" | custom-call | flops 1000000000 | bytes 1000000 | tf_op jit(solution)/shard_map/input_back/pallas_call | solution.py:640
  687.5 9.5 %collective-permute-done.34 = bf16[24,9472]{1,0:T(8,128)(2,1)S(1)} collective-permute-done((bf16[24,9472]{1,0:T(8,128)(2,1)S(1)}, bf16[24,9472]{1,0:T(8,128)(2,1)S(1)}, u32[]{:S(2)}, u32[]{:S(2)}) %collective-permute-start.34) | collective-permute-done | bytes 454688 | tf_op jit(solution)/shard_map/ppermute | solution.py:676
  (368 shorter events, 248.3 us)
Async XLA Ops:
  7.2 168.2 %all-gather.3.cloned.1.call-start = ((), (), s32[]{:S(2)}) async-start(), calls=%async_computation.1 | async-start | bytes 10948608 | tf_op jit(solution)/shard_map/all_gather | solution.py:661
  60.1 248.8 %all-gather.5.cloned.1.call-start = ((), (), s32[]{:S(2)}) async-start(), calls=%async_computation.2 | async-start | bytes 9732096 | tf_op jit(solution)/shard_map/all_gather | solution.py:661
  61.6 40.0 %collective-permute-start.7 = (bf16[512,768]{1,0:T(8,128)(2,1)}, bf16[512,768]{1,0:T(8,128)(2,1)}, u32[]{:S(2)}, u32[]{:S(2)}) collective-permute-start(bf16[512,768]{1,0:T(8,128)(2,1)} %get-tuple-element.346), channel_id=1, source_target_pairs={{0,4},{4,8},{8,12},{12,16},{16,20},{20,24},{24,28},{1,5},{5,9},{9,... | collective-permute-start | bytes 2359304 | tf_op jit(solution)/shard_map/ppermute | solution.py:655
  66.9 37.3 %collective-permute-start.8 = (bf16[512,768]{1,0:T(8,128)(2,1)}, bf16[512,768]{1,0:T(8,128)(2,1)}, u32[]{:S(2)}, u32[]{:S(2)}) collective-permute-start(bf16[512,768]{1,0:T(8,128)(2,1)} %get-tuple-element.345), channel_id=1, source_target_pairs={{4,0},{8,4},{12,8},{16,12},{20,16},{24,20},{28,24},{5,1},{9,5},{13... | collective-permute-start | bytes 2359304 | tf_op jit(solution)/shard_map/ppermute | solution.py:656
  176.3 459.1 %reduce-scatter.4.cloned.1.call-start = ((), (), s32[]{:S(2)}) async-start(), calls=%async_computation.3 | async-start | bytes 11151360
  178.6 32.1 %collective-permute-start.12 = (bf16[4,24,3200]{2,1,0:T(8,128)(2,1)S(1)}, bf16[4,24,3200]{2,1,0:T(8,128)(2,1)S(1)}, u32[]{:S(2)}, u32[]{:S(2)}) collective-permute-start(bf16[4,24,3200]{2,1,0:T(8,128)(2,1)S(1)} %bitcast_dynamic-update-slice_fusion.12), channel_id=1, source_target_pairs={{0,2},{1,3},{2,0},{3,1},{4,6},{5,7},{6,4},{7,5},{8,10},{9,11},{10,... | collective-permute-start | bytes 1843208 | tf_op jit(solution)/shard_map/ppermute | solution.py:676
  180.0 31.7 %collective-permute-start.13 = (bf16[4,24,3200]{2,1,0:T(8,128)(2,1)S(1)}, bf16[4,24,3200]{2,1,0:T(8,128)(2,1)S(1)}, u32[]{:S(2)}, u32[]{:S(2)}) collective-permute-start(bf16[4,24,3200]{2,1,0:T(8,128)(2,1)S(1)} %bitcast_dynamic-update-slice_fusion.12), channel_id=1, source_target_pairs={{0,4},{1,5},{2,6},{3,7},{4,0},{5,1},{6,2},{7,3},{8,12},{9,13},{10,... | collective-permute-start | bytes 1843208 | tf_op jit(solution)/shard_map/ppermute | solution.py:676
  181.5 31.8 %collective-permute-start.14 = (bf16[4,24,3200]{2,1,0:T(8,128)(2,1)S(1)}, bf16[4,24,3200]{2,1,0:T(8,128)(2,1)S(1)}, u32[]{:S(2)}, u32[]{:S(2)}) collective-permute-start(bf16[4,24,3200]{2,1,0:T(8,128)(2,1)S(1)} %bitcast_dynamic-update-slice_fusion.12), channel_id=1, source_target_pairs={{0,6},{1,7},{2,4},{3,5},{4,2},{5,3},{6,0},{7,1},{8,14},{9,15},{10,... | collective-permute-start | bytes 1843208 | tf_op jit(solution)/shard_map/ppermute | solution.py:676
  213.4 52.6 %collective-permute-start.15 = (bf16[4,4,24,3200]{3,2,0,1:T(8,128)(2,1)S(1)}, bf16[4,4,24,3200]{3,2,0,1:T(8,128)(2,1)}, u32[]{:S(2)}, u32[]{:S(2)}) collective-permute-start(bf16[4,4,24,3200]{3,2,0,1:T(8,128)(2,1)S(1)} %bitcast_dynamic-update-slice_fusion.7), channel_id=1, source_target_pairs={{0,1},{1,0},{2,3},{3,2},{4,5},{5,4},{6,7},{7,6},{8,9},{9,8},{10,11... | collective-permute-start | bytes 7372808 | tf_op jit(solution)/shard_map/ppermute | solution.py:676
  215.1 50.7 %collective-permute-start.16 = (bf16[512,768]{1,0:T(8,128)(2,1)S(1)}, bf16[512,768]{1,0:T(8,128)(2,1)S(1)}, u32[]{:S(2)}, u32[]{:S(2)}) collective-permute-start(bf16[512,768]{1,0:T(8,128)(2,1)S(1)} %get-tuple-element.344), channel_id=1, source_target_pairs={{0,4},{4,8},{8,12},{12,16},{16,20},{20,24},{24,28},{1,5},{5,9},{9,... | collective-permute-start | bytes 2359304 | tf_op jit(solution)/shard_map/ppermute | solution.py:655
  218.3 47.6 %collective-permute-start.17 = (bf16[512,768]{1,0:T(8,128)(2,1)S(1)}, bf16[512,768]{1,0:T(8,128)(2,1)S(1)}, u32[]{:S(2)}, u32[]{:S(2)}) collective-permute-start(bf16[512,768]{1,0:T(8,128)(2,1)S(1)} %get-tuple-element.343), channel_id=1, source_target_pairs={{4,0},{8,4},{12,8},{16,12},{20,16},{24,20},{28,24},{5,1},{9,5},{13... | collective-permute-start | bytes 2359304 | tf_op jit(solution)/shard_map/ppermute | solution.py:656
  428.1 53.1 %collective-permute-start.18 = (bf16[512,768]{1,0:T(8,128)(2,1)}, bf16[512,768]{1,0:T(8,128)(2,1)}, u32[]{:S(2)}, u32[]{:S(2)}) collective-permute-start(bf16[512,768]{1,0:T(8,128)(2,1)} %get-tuple-element.342), channel_id=1, source_target_pairs={{0,4},{4,8},{8,12},{12,16},{16,20},{20,24},{24,28},{1,5},{5,9},{9,... | collective-permute-start | bytes 2359304 | tf_op jit(solution)/shard_map/ppermute | solution.py:655
  457.1 25.5 %collective-permute-start.19 = (bf16[512,768]{1,0:T(8,128)(2,1)}, bf16[512,768]{1,0:T(8,128)(2,1)}, u32[]{:S(2)}, u32[]{:S(2)}) collective-permute-start(bf16[512,768]{1,0:T(8,128)(2,1)} %get-tuple-element.341), channel_id=1, source_target_pairs={{4,0},{8,4},{12,8},{16,12},{20,16},{24,20},{28,24},{5,1},{9,5},{13... | collective-permute-start | bytes 2359304 | tf_op jit(solution)/shard_map/ppermute | solution.py:656
  557.7 78.8 %collective-permute-start.21 = (bf16[4,24,9472]{2,1,0:T(8,128)(2,1)}, bf16[4,24,9472]{2,1,0:T(8,128)(2,1)S(1)}, u32[]{:S(2)}, u32[]{:S(2)}) collective-permute-start(bf16[4,24,9472]{2,1,0:T(8,128)(2,1)} %get-tuple-element.285), channel_id=1, source_target_pairs={{0,2},{1,3},{2,0},{3,1},{4,6},{5,7},{6,4},{7,5},{8,10},{9,11},{10,... | collective-permute-start | bytes 5455880 | tf_op jit(solution)/shard_map/ppermute | solution.py:676
  578.2 81.7 %collective-permute-start.22 = (bf16[4,24,9472]{2,1,0:T(8,128)(2,1)}, bf16[4,24,9472]{2,1,0:T(8,128)(2,1)}, u32[]{:S(2)}, u32[]{:S(2)}) collective-permute-start(bf16[4,24,9472]{2,1,0:T(8,128)(2,1)} %get-tuple-element.286), channel_id=1, source_target_pairs={{0,4},{1,5},{2,6},{3,7},{4,0},{5,1},{6,2},{7,3},{8,12},{9,13},{10,... | collective-permute-start | bytes 5455880 | tf_op jit(solution)/shard_map/ppermute | solution.py:676
  580.9 79.0 %collective-permute-start.23 = (bf16[4,24,9472]{2,1,0:T(8,128)(2,1)}, bf16[4,24,9472]{2,1,0:T(8,128)(2,1)}, u32[]{:S(2)}, u32[]{:S(2)}) collective-permute-start(bf16[4,24,9472]{2,1,0:T(8,128)(2,1)} %get-tuple-element.287), channel_id=1, source_target_pairs={{0,6},{1,7},{2,4},{3,5},{4,2},{5,3},{6,0},{7,1},{8,14},{9,15},{10,... | collective-permute-start | bytes 5455880 | tf_op jit(solution)/shard_map/ppermute | solution.py:676
  630.7 49.5 %collective-permute-start.24 = (bf16[4,4,24,2432]{3,2,1,0:T(8,128)(2,1)}, bf16[4,4,24,2432]{3,2,1,0:T(8,128)(2,1)}, u32[]{:S(2)}, u32[]{:S(2)}) collective-permute-start(bf16[4,4,24,2432]{3,2,1,0:T(8,128)(2,1)} %get-tuple-element.293), channel_id=1, source_target_pairs={{0,1},{1,0},{2,3},{3,2},{4,5},{5,4},{6,7},{7,6},{8,9},{9,8},{10,11... | collective-permute-start | bytes 5603336 | tf_op jit(solution)/shard_map/ppermute | solution.py:676
  663.4 33.6 %collective-permute-start.34 = (bf16[24,9472]{1,0:T(8,128)(2,1)S(1)}, bf16[24,9472]{1,0:T(8,128)(2,1)S(1)}, u32[]{:S(2)}, u32[]{:S(2)}) collective-permute-start(bf16[24,9472]{1,0:T(8,128)(2,1)S(1)} %get-tuple-element.306), channel_id=1, source_target_pairs={{0,16},{1,17},{2,18},{3,19},{4,20},{5,21},{6,22},{7,23},{8,24},{9,... | collective-permute-start | bytes 1363976 | tf_op jit(solution)/shard_map/ppermute | solution.py:676
  663.5 37.9 %collective-permute-start.35 = (bf16[24,9472]{1,0:T(8,128)(2,1)S(1)}, bf16[24,9472]{1,0:T(8,128)(2,1)S(1)}, u32[]{:S(2)}, u32[]{:S(2)}) collective-permute-start(bf16[24,9472]{1,0:T(8,128)(2,1)S(1)} %get-tuple-element.307), channel_id=1, source_target_pairs={{0,24},{1,25},{2,26},{3,27},{4,28},{5,29},{6,30},{7,31},{8,16},{9,... | collective-permute-start | bytes 1363976 | tf_op jit(solution)/shard_map/ppermute | solution.py:676
  682.8 31.4 %collective-permute-start.25 = (bf16[4,24,2432]{2,1,0:T(8,128)(2,1)}, bf16[4,24,2432]{2,1,0:T(8,128)(2,1)}, u32[]{:S(2)}, u32[]{:S(2)}) collective-permute-start(bf16[4,24,2432]{2,1,0:T(8,128)(2,1)} %get-tuple-element.297), channel_id=1, source_target_pairs={{0,2},{1,3},{2,0},{3,1},{4,6},{5,7},{6,4},{7,5},{8,10},{9,11},{10,... | collective-permute-start | bytes 1400840 | tf_op jit(solution)/shard_map/ppermute | solution.py:676
  684.2 29.9 %collective-permute-start.26 = (bf16[4,24,2432]{2,1,0:T(8,128)(2,1)}, bf16[4,24,2432]{2,1,0:T(8,128)(2,1)}, u32[]{:S(2)}, u32[]{:S(2)}) collective-permute-start(bf16[4,24,2432]{2,1,0:T(8,128)(2,1)} %get-tuple-element.298), channel_id=1, source_target_pairs={{0,4},{1,5},{2,6},{3,7},{4,0},{5,1},{6,2},{7,3},{8,12},{9,13},{10,... | collective-permute-start | bytes 1400840 | tf_op jit(solution)/shard_map/ppermute | solution.py:676
  686.1 28.1 %collective-permute-start.27 = (bf16[4,24,2432]{2,1,0:T(8,128)(2,1)}, bf16[4,24,2432]{2,1,0:T(8,128)(2,1)}, u32[]{:S(2)}, u32[]{:S(2)}) collective-permute-start(bf16[4,24,2432]{2,1,0:T(8,128)(2,1)} %get-tuple-element.299), channel_id=1, source_target_pairs={{0,6},{1,7},{2,4},{3,5},{4,2},{5,3},{6,0},{7,1},{8,14},{9,15},{10,... | collective-permute-start | bytes 1400840 | tf_op jit(solution)/shard_map/ppermute | solution.py:676
  697.0 40.9 %collective-permute-start.28 = (bf16[512,768]{1,0:T(8,128)(2,1)}, bf16[512,768]{1,0:T(8,128)(2,1)}, u32[]{:S(2)}, u32[]{:S(2)}) collective-permute-start(bf16[512,768]{1,0:T(8,128)(2,1)} %get-tuple-element.340), channel_id=1, source_target_pairs={{0,4},{4,8},{8,12},{12,16},{16,20},{20,24},{24,28},{1,5},{5,9},{9,... | collective-permute-start | bytes 2359304 | tf_op jit(solution)/shard_map/ppermute | solution.py:655
  701.4 38.2 %collective-permute-start.29 = (bf16[512,768]{1,0:T(8,128)(2,1)}, bf16[512,768]{1,0:T(8,128)(2,1)}, u32[]{:S(2)}, u32[]{:S(2)}) collective-permute-start(bf16[512,768]{1,0:T(8,128)(2,1)} %get-tuple-element.339), channel_id=1, source_target_pairs={{4,0},{8,4},{12,8},{16,12},{20,16},{24,20},{28,24},{5,1},{9,5},{13... | collective-permute-start | bytes 2359304 | tf_op jit(solution)/shard_map/ppermute | solution.py:656
  (88 other events, 1552.7 us)
Sparse Core Ops, SparseCore 0:
  60.2 115.1 all-gather.2
  178.3 105.0 all-gather.4
  381.1 175.6 reduce-scatter.3

commit v4 on v3

--- a/solution.py
+++ b/solution.py
@@ -524,46 +524,50 @@
     )(*args)
 
 
-def project_kernel(low, w, qb, vb, q, q_t, k, k_t, v, v_t):
-    i = pl.program_id(0)
-    n = pl.num_programs(0)
+def project_kernel(own, low, w, qb, vb, *refs):
+    outs = refs if own else refs[4:]
     x = low[...]
+    k, k_t, v, v_t = outs[-4:]
     kk = dot(x, w[:, D : 2 * D]).astype(BF16)
     k[...] = kk
     k_t[...] = kk.T
     vv = (dot(x, w[:, 2 * D : 3 * D]) + vb[...]).astype(BF16)
     v[...] = vv
     v_t[...] = vv.T
-    skip = RIM * BLK // ROWS
-
-    @pl.when(jnp.logical_and(i >= skip, i < n - skip))
-    def _():
+    if own:
         qq = (dot(x, w[:, :D]) + qb[...]).astype(BF16)
-        q[...] = qq
-        q_t[...] = qq.T
-
-def project(low_ext, w, qb, vb):
-    n = low_ext.shape[0]
+        outs[0][...] = qq
+        outs[1][...] = qq.T
+
+
+def project(rows, w, qb, vb, begun=()):
+    own = not begun
     rim = RIM * BLK
     skip = rim // ROWS
-    own = n - 2 * rim
-    last = own // ROWS - 1
-    row = pl.BlockSpec((ROWS, D), lambda i: (i, 0))
-    col = pl.BlockSpec((D, ROWS), lambda i: (0, i))
-    qrow = pl.BlockSpec((ROWS, D), lambda i: (jnp.clip(i - skip, 0, last), 0))
-    qcol = pl.BlockSpec((D, ROWS), lambda i: (0, jnp.clip(i - skip, 0, last)))
-    tall = jax.ShapeDtypeStruct((n, D), BF16)
-    wide = jax.ShapeDtypeStruct((D, n), BF16)
+    count = rows.shape[0]
+    total = count + 2 * rim if own else begun[0].shape[0]
+    middle = (total - 2 * rim) // ROWS
+    at = (lambda i: i + skip) if own else (lambda i: jnp.where(i < skip, i, i + middle))
+    row = pl.BlockSpec((ROWS, D), lambda i: (at(i), 0))
+    col = pl.BlockSpec((D, ROWS), lambda i: (0, at(i)))
+    plain = pl.BlockSpec((ROWS, D), lambda i: (i, 0))
+    turned = pl.BlockSpec((D, ROWS), lambda i: (0, i))
+    tall = jax.ShapeDtypeStruct((total, D), BF16)
+    wide = jax.ShapeDtypeStruct((D, total), BF16)
+    short = [jax.ShapeDtypeStruct((count, D), BF16), jax.ShapeDtypeStruct((D, count), BF16)]
     return pl.pallas_call(
-        project_kernel,
-        grid=(n // ROWS,),
-        in_specs=[row, once((D, 3 * D)), once((1, D)), once((1, D))],
-        out_specs=[qrow, qcol, row, col, row, col],
-        out_shape=[jax.ShapeDtypeStruct((own, D), BF16), jax.ShapeDtypeStruct((D, own), BF16), tall, wide, tall, wide],
+        functools.partial(project_kernel, own),
+        grid=(count // ROWS,),
+        in_specs=[plain, once((D, 3 * D)), once((1, D)), once((1, D))]
+        + [pl.BlockSpec(memory_space=pl.ANY)] * len(begun),
+        out_specs=([plain, turned] if own else []) + [row, col, row, col],
+        out_shape=(short if own else []) + [tall, wide, tall, wide],
+        input_output_aliases={4 + j: j for j in range(len(begun))},
         compiler_params=pltpu.CompilerParams(vmem_limit_bytes=40 * 2**20),
-        cost_estimate=cost(14),
+        cost_estimate=cost(8),
         name="project",
-    )(low_ext, w, qb, vb)
+    )(rows, w, qb, vb, *begun)
+
 
 def att_grads_kernel(low, dq_t, dk, dv, dr, rate, out, turned):
     n = pl.program_id(0)
@@ -780,11 +784,17 @@
     return jnp.repeat(rows, BLK, axis=2)
 
 
-def layer_forward(hidden, low_ext, head, vec, flags, keep, temper, pos, before, between):
+def layer_forward(hidden, low_parts, head, vec, flags, keep, temper, pos, before, between):
     z = (vec["logits"] + vec["jitter"]).reshape(HEADS, SPAN, SPAN) / temper[:, None, None]
     relaxed = jax.nn.sigmoid(z)
     factor = table_rows(relaxed)
-    q, q_t, k, k_t, v, v_t = project(low_ext, head, vec["qb"][None], vec["vb"][None])
+    biases = (vec["qb"][None], vec["vb"][None])
+    lower, own, upper = low_parts
+    low_ext = jnp.concatenate(low_parts, 0)
+    q, q_t, *begun = project(own, head, *biases)
+    q_t, lower = lax.optimization_barrier((q_t, lower))
+    rims = jnp.concatenate([lower, upper], 0)
+    k, k_t, v, v_t = project(rims, head, *biases, begun)
     q_t = before(q_t)
     log_factor, inv_factor = jnp.log2(factor), 1.0 / factor
     ctx_t, lse = attend(flags, keep, pos, factor, q_t, k, v_t)
@@ -897,7 +907,7 @@
     symbols, rest = lax.optimization_barrier((symbols, jnp.concatenate(wide + out, 1)))
     symbols = gather.advance(gather.advance(symbols))
     lower, upper = neighbours(symbols[symbols.shape[0] - rim :], symbols[:rim])
-    low_ext = jnp.concatenate([lower, symbols, upper], 0)
+    low_ext = (lower, symbols, upper)
     head_zero = gather.result(symbols)
     head_zero, rest = lax.optimization_barrier((head_zero, rest))
     tail_zero = gathered(rest)
@@ -929,7 +939,7 @@
     records = [record]
     low = later.advance(low)
     lower, upper = neighbours(low[low.shape[0] - rim :], low[:rim])
-    low_ext = jnp.concatenate([lower, low, upper], 0)
+    low_ext = (lower, low, upper)
     head_one = later.result(low)
     hidden, _, record = layer_forward(
         hidden,

time: 752 us -> 728 us (0.968); the launches traced: 750 us -> 717 us
  waiting for transfers between devices: 174 us -> 121 us
  starting transfers between devices: 111 us -> 72.6 us
  Pallas kernels: 298 us -> 328 us
  local copies, waits for them, and re-layouts: 110 us -> 133 us
    ppermute x4, waiting for transfers between devices: 78.8 us -> 52.8 us  [neighbours(): lax.ppermute(tail, 'dp', [(i, i + 1) for i in range(count - 1)])]
    ppermute x28, starting transfers between devices: 63.3 us -> 44.1 us  [swap(): return lax.ppermute(block, AXES, [(i, i ^ mask) for i in range(count)])]
    ppermute x4, starting transfers between devices: 41 us -> 22.5 us  [neighbours(): lax.ppermute(tail, 'dp', [(i, i + 1) for i in range(count - 1)])]
    pallas_call x2, Pallas kernels: 56.9 us -> 75.2 us  [attend_back(): pl.pallas_call(backward_kernel, out_shape=(jax.ShapeDtypeStruct(q_t.shape...]
    all_gather x2, waiting for transfers between devices: 20.1 us -> 3.87 us  [gathered(): return lax.all_gather(part, AXES, axis=0, tiled=True)]
    pallas_call x2, Pallas kernels: 16.5 us -> 28.4 us  [attend(): pl.pallas_call(forward_kernel, out_shape=(jax.ShapeDtypeStruct(q_t.shape,...]
    ppermute x28, waiting for transfers between devices: 75 us -> 63.9 us  [swap(): return lax.ppermute(block, AXES, [(i, i ^ mask) for i in range(count)])]
    unnamed x167 -> x187, local copies, waits for them, and re-layouts: 54.5 us -> 59.1 us
  transfers between devices with their start and end apart: 39 -> 39, of which waited for: 15 -> 11; matrix products, arithmetic and copies ran while one was open for 13% -> 16% of each run, Pallas kernels for 30% -> 36%
where the time goes in v4:
time: 728 us; the launch traced here: 717 us
  Pallas kernels  328 us (45%)
  local copies, waits for them, and re-layouts  133 us (18%)
  waiting for transfers between devices  121 us (17%)
  starting transfers between devices  72.6 us (10%)
  other arithmetic  47 us (6%)
  between operations  15.5 us (2%)
    pallas_call x2, Pallas kernels, attend_back(): pl.pallas_call(backward_kernel, out_shape=(jax.ShapeDtypeStruct(q_t.shape...  75.2 us
    ppermute x28, waiting for transfers between devices, swap(): return lax.ppermute(block, AXES, [(i, i ^ mask) for i in range(count)])  63.9 us
    unnamed x187, local copies, waits for them, and re-layouts  59.1 us
    pallas_call x2, Pallas kernels, ffn(): pl.pallas_call(ffn_kernel, grid=(n // ROWS,), in_specs=[pl.BlockSpec((D,...  56.5 us
    ppermute x4, waiting for transfers between devices, neighbours(): lax.ppermute(tail, 'dp', [(i, i + 1) for i in range(count - 1)])  52.8 us
    pallas_call x2, Pallas kernels, ffn_back(): pl.pallas_call(ffn_back_kernel, grid=(n // ROWS,), in_specs=[row(D), row(...  47 us
    pallas_call x2, Pallas kernels, ffn_grads(): pl.pallas_call(functools.partial(ffn_grads_kernel, extra), grid=(2 * bloc...  44.5 us
    ppermute x28, starting transfers between devices, swap(): return lax.ppermute(block, AXES, [(i, i ^ mask) for i in range(count)])  44.1 us
  transfers between devices with their start and end apart: 39, of which 11 were waited for; matrix products, arithmetic and copies ran while one was open for 16% of the time, Pallas kernels for 36%

profile of v4, /device:TPU:0, one launch (start us, length us, event | category | flops | bytes accessed | tf_op | source)
XLA Modules:
  0.0 716.7 jit_solution(11791066350158916823)
XLA Ops:
  33.6 10.0 %collective-permute-done.3 = bf16[4,24,2432]{2,1,0:T(8,128)(2,1)S(1)} collective-permute-done((bf16[4,24,2432]{2,1,0:T(8,128)(2,1)S(1)}, bf16[4,24,2432]{2,1,0:T(8,128)(2,1)S(1)}, u32[]{:S(2)}, u32[]{:S(2)}) %collective-permute-start.3) | collective-permute-done | bytes 466976 | tf_op jit(solution)/shard_map/ppermute | solution.py:680
  43.6 9.4 %collective-permute-done.4 = bf16[4,24,2432]{2,1,0:T(8,128)(2,1)S(1)} collective-permute-done((bf16[4,24,2432]{2,1,0:T(8,128)(2,1)S(1)}, bf16[4,24,2432]{2,1,0:T(8,128)(2,1)S(1)}, u32[]{:S(2)}, u32[]{:S(2)}) %collective-permute-start.4) | collective-permute-done | bytes 466976 | tf_op jit(solution)/shard_map/ppermute | solution.py:680
  92.0 18.8 %collective-permute-done.7 = bf16[512,768]{1,0:T(8,128)(2,1)} collective-permute-done((bf16[512,768]{1,0:T(8,128)(2,1)}, bf16[512,768]{1,0:T(8,128)(2,1)}, u32[]{:S(2)}, u32[]{:S(2)}) %collective-permute-start.7) | collective-permute-done | bytes 786464 | tf_op jit(solution)/shard_map/ppermute | solution.py:659
  134.5 15.3 %attend.2 = (f32[768,1024]{1,0:T(8,128)S(1)}, f32[8,8,256]{2,1,0:T(8,128)S(1)}) custom-call(s32[64]{0:T(128)S(1)} %bitcast.357, s32[8,15]{1,0:T(8,128)S(1)} %get-tuple-element.396.keep, s32[1]{0:T(128)} %bitcast.2.pos, f32[64,6,256]{2,1,0:T(8,128)S(1)} %get-tuple-element.379.factor, bf16[768,1024]{1,0:T(8,128)(2,1)S(1)} %copy-done.34, ...), custom_call_target="tpu_custom_call" | custom-call | flops 12999999488 | bytes 1000000 | tf_op jit(solution)/shard_map/attend/pallas_call | solution.py:188
  167.7 28.3 %ffn.2 = (f32[1024,768]{1,0:T(8,128)}, bf16[1024,768]{1,0:T(8,128)(2,1)}, bf16[1024,3072]{1,0:T(8,128)(2,1)}, bf16[1024,3072]{1,0:T(8,128)(2,1)}, f32[1024,768]{...) custom-call(f32[768,1024]{1,0:T(8,128)} %copy-done.1, bf16[1024,768]{1,0:T(8,128)(2,1)} %bitcast.351, ...), custom_call_target="tpu_custom_call" | custom-call | flops 28000000000 | bytes 1000000 | tf_op jit(solution)/shard_map/ffn/pallas_call | solution.py:394
  237.1 17.7 %collective-permute-done.16 = bf16[512,768]{1,0:T(8,128)(2,1)S(1)} collective-permute-done((bf16[512,768]{1,0:T(8,128)(2,1)}, bf16[512,768]{1,0:T(8,128)(2,1)S(1)}, u32[]{:S(2)}, u32[]{:S(2)}) %collective-permute-start.16) | collective-permute-done | bytes 786464 | tf_op jit(solution)/shard_map/ppermute | solution.py:659
  278.4 13.1 %attend.3 = (f32[768,1024]{1,0:T(8,128)S(1)}, f32[8,8,256]{2,1,0:T(8,128)S(1)}) custom-call(s32[64]{0:T(128)S(1)} %bitcast.358, s32[8,15]{1,0:T(8,128)S(1)} %get-tuple-element.397.keep, s32[1]{0:T(128)} %bitcast.2.pos, f32[64,6,256]{2,1,0:T(8,128)S(1)} %get-tuple-element.377.factor, bf16[768,1024]{1,0:T(8,128)(2,1)S(1)} %copy-done.37, ...), custom_call_target="tpu_custom_call" | custom-call | flops 12999999488 | bytes 1000000 | tf_op jit(solution)/shard_map/attend/pallas_call | solution.py:188
  293.9 28.2 %ffn.3 = (f32[1024,768]{1,0:T(8,128)}, bf16[1024,768]{1,0:T(8,128)(2,1)}, bf16[1024,3072]{1,0:T(8,128)(2,1)}, bf16[1024,3072]{1,0:T(8,128)(2,1)}, f32[1024,768]{...) custom-call(f32[768,1024]{1,0:T(8,128)} %copy-done.4, f32[1024,768]{1,0:T(8,128)} %get-tuple-element.247.hidden, ...), custom_call_target="tpu_custom_call" | custom-call | flops 28000000000 | bytes 1000000 | tf_op jit(solution)/shard_map/ffn/pallas_call | solution.py:394
  322.1 23.5 %ffn_back.2 = (bf16[1024,768]{1,0:T(8,128)(2,1)}, bf16[1024,3072]{1,0:T(8,128)(2,1)}, f32[1024,768]{1,0:T(8,128)}, bf16[1024,768]{1,0:T(8,128)(2,1)}, bf16[1024,...) custom-call(bf16[1024,768]{1,0:T(8,128)(2,1)} %bitcast.369, ...), custom_call_target="tpu_custom_call" | custom-call | flops 1000000000 | bytes 1000000 | tf_op jit(solution)/shard_map/ffn_back/pallas_call | solution.py:444
  345.6 20.2 %ffn_grads.2 = bf16[768,7040]{1,0:T(8,128)(2,1)} custom-call(bf16[1024,768]{1,0:T(8,128)(2,1)} %get-tuple-element.261.normed, bf16[1024,3072]{1,0:T(8,128)(2,1)} %get-tuple-element.262.dinner, bf16[1024,3072]{1,0:T(8,128)(2,1)} %get-tuple-element.263.active, bf16[1024,768]{1,0:T(8,128)(2,1)} %get-tuple-element.264.douter, f32[768,1024]{1,0:T(8,128)} %copy-done.4, ...), custom_call_target="tpu_custom_call" | custom-call | flops 1000000000 | bytes 1000000 | tf_op jit(solution)/shard_map/ffn_grads/pallas_call | solution.py:514
  367.9 36.0 %attend_back.2 = (bf16[768,1024]{1,0:T(8,128)(2,1)}, bf16[2048,768]{1,0:T(8,128)(2,1)}, bf16[2048,768]{1,0:T(8,128)(2,1)}, f32[64,8,128]{2,1,0:T(8,128)}) custom-call(s32[64]{0:T(128)} %bitcast.355, s32[8,15]{1,0:T(8,128)} %copy-done.43, s32[1]{0:T(128)} %bitcast.2.pos, f32[64,6,256]{2,1,0:T(8,128)} %copy_multiply_fusion.log_factor, ...), custom_call_target="tpu_custom_call" | custom-call | flops 1000000000 | bytes 1000000 | tf_op jit(solution)/shard_map/attend_back/pallas_call | solution.py:324
  409.5 11.6 %input_back.2 = (f32[1024,768]{1,0:T(8,128)S(1)}, bf16[1024,768]{1,0:T(8,128)(2,1)S(1)}) custom-call(bf16[2048,768]{1,0:T(8,128)(2,1)S(1)} %copy-done.5, bf16[2048,768]{1,0:T(8,128)(2,1)S(1)} %copy-done.6, bf16[768,1024]{1,0:T(8,128)(2,1)S(1)} %copy-done.12, f32[1024,768]{1,0:T(8,128)} %get-tuple-element.275.dfirst, bf16[768,3200]{1,0:T(8,128)(2,1)} %bitcast.365), custom_call_target="tpu_custom_call" | custom-call | flops 1000000000 | bytes 1000000 | tf_op jit(solution)/shard_map/input_back/pallas_call | solution.py:644
  422.4 9.8 %collective-permute-start.18 = (bf16[512,768]{1,0:T(8,128)(2,1)}, bf16[512,768]{1,0:T(8,128)(2,1)}, u32[]{:S(2)}, u32[]{:S(2)}) collective-permute-start(bf16[512,768]{1,0:T(8,128)(2,1)} %get-tuple-element.366), channel_id=1, source_target_pairs={{0,4},{4,8},{8,12},{12,16},{16,20},{20,24},{24,28},{1,5},{5,9},{9,... | collective-permute-start | bytes 2359304 | tf_op jit(solution)/shard_map/ppermute | solution.py:659
  437.6 11.6 %att_grads.2.rest_0_.rest_1_ = bf16[768,2432]{1,0:T(8,128)(2,1)} custom-call(bf16[2048,768]{1,0:T(8,128)(2,1)S(1)} %pad_maximum_fusion.low, bf16[768,1024]{1,0:T(8,128)(2,1)S(1)} %copy-done.13, bf16[2048,768]{1,0:T(8,128)(2,1)} %get-tuple-element.272.dk, bf16[2048,768]{1,0:T(8,128)(2,1)} %get-tuple-element.273.dv, f32[64,8,128]{2,1,0:T(8,128)S(1)} %copy-done.38, ...), custom_call_target="tpu_custom_call" | custom-call | flops 1000000000 | bytes 1000000 | tf_op jit(solution)/shard_map/att_grads/pallas_call | solution.py:608
  449.2 16.3 %collective-permute-done.18 = bf16[512,768]{1,0:T(8,128)(2,1)} collective-permute-done((bf16[512,768]{1,0:T(8,128)(2,1)}, bf16[512,768]{1,0:T(8,128)(2,1)}, u32[]{:S(2)}, u32[]{:S(2)}) %collective-permute-start.18) | collective-permute-done | bytes 786464 | tf_op jit(solution)/shard_map/ppermute | solution.py:659
  469.1 23.5 %ffn_back.3 = (bf16[1024,768]{1,0:T(8,128)(2,1)}, bf16[1024,3072]{1,0:T(8,128)(2,1)}, f32[1024,768]{1,0:T(8,128)}, bf16[1024,768]{1,0:T(8,128)(2,1)}, bf16[1024,...) custom-call(f32[1024,768]{1,0:T(8,128)} %copy-done, ...), custom_call_target="tpu_custom_call" | custom-call | flops 1000000000 | bytes 1000000 | tf_op jit(solution)/shard_map/ffn_back/pallas_call | solution.py:444
  492.6 24.3 %ffn_grads.3 = bf16[768,9472]{1,0:T(8,128)(2,1)} custom-call(bf16[1024,768]{1,0:T(8,128)(2,1)} %get-tuple-element.283.normed, bf16[1024,3072]{1,0:T(8,128)(2,1)} %get-tuple-element.284.dinner, bf16[1024,3072]{1,0:T(8,128)(2,1)} %get-tuple-element.285.active, bf16[1024,768]{1,0:T(8,128)(2,1)} %get-tuple-element.286.douter, f32[768,1024]{1,0:T(8,128)} %copy-done.1, ...), custom_call_target="tpu_custom_call" | custom-call | flops 1000000000 | bytes 1000000 | tf_op jit(solution)/shard_map/ffn_grads/pallas_call | solution.py:514
  522.9 11.6 %collective-permute-done.20 = bf16[4,4,24,9472]{3,2,1,0:T(8,128)(2,1)} collective-permute-done((bf16[4,4,24,9472]{3,2,1,0:T(8,128)(2,1)S(1)}, bf16[4,4,24,9472]{3,2,1,0:T(8,128)(2,1)}, u32[]{:S(2)}, u32[]{:S(2)}) %collective-permute-start.20) | collective-permute-done | bytes 7274528 | tf_op jit(solution)/shard_map/ppermute | solution.py:680
  552.4 39.2 %attend_back.3 = (bf16[768,1024]{1,0:T(8,128)(2,1)}, bf16[2048,768]{1,0:T(8,128)(2,1)}, bf16[2048,768]{1,0:T(8,128)(2,1)}, f32[64,8,128]{2,1,0:T(8,128)}) custom-call(s32[64]{0:T(128)} %bitcast.356, s32[8,15]{1,0:T(8,128)} %copy-done.42, s32[1]{0:T(128)} %bitcast.2.pos, f32[64,6,256]{2,1,0:T(8,128)} %copy_multiply_fusion.1.log_factor, ...), custom_call_target="tpu_custom_call" | custom-call | flops 1000000000 | bytes 1000000 | tf_op jit(solution)/shard_map/attend_back/pallas_call | solution.py:324
  594.0 11.7 %att_grads.3 = bf16[768,2432]{1,0:T(8,128)(2,1)} custom-call(bf16[2048,768]{1,0:T(8,128)(2,1)S(1)} %pad_maximum_fusion.1.low, bf16[768,1024]{1,0:T(8,128)(2,1)S(1)} %copy-done.7, bf16[2048,768]{1,0:T(8,128)(2,1)} %get-tuple-element.312.dk, bf16[2048,768]{1,0:T(8,128)(2,1)} %get-tuple-element.302.dv, f32[64,8,128]{2,1,0:T(8,128)S(1)} %copy-done.39, ...), custom_call_target="tpu_custom_call" | custom-call | flops 1000000000 | bytes 1000000 | tf_op jit(solution)/shard_map/att_grads/pallas_call | solution.py:608
  611.0 15.9 %collective-permute-done.22 = bf16[4,24,9472]{2,1,0:T(8,128)(2,1)} collective-permute-done((bf16[4,24,9472]{2,1,0:T(8,128)(2,1)}, bf16[4,24,9472]{2,1,0:T(8,128)(2,1)}, u32[]{:S(2)}, u32[]{:S(2)}) %collective-permute-start.22) | collective-permute-done | bytes 1818656 | tf_op jit(solution)/shard_map/ppermute | solution.py:680
  634.9 11.5 %input_back.3 = (f32[1024,768]{1,0:T(8,128)S(1)}, bf16[1024,768]{1,0:T(8,128)(2,1)S(1)}) custom-call(bf16[2048,768]{1,0:T(8,128)(2,1)S(1)} %copy-done.2, bf16[2048,768]{1,0:T(8,128)(2,1)S(1)} %copy-done.3, bf16[768,1024]{1,0:T(8,128)(2,1)S(1)} %copy-done.8, f32[1024,768]{1,0:T(8,128)} %get-tuple-element.313.dfirst, bf16[768,2432]{1,0:T(8,128)(2,1)} %bitcast.43.w), custom_call_target="tpu_custom_call" | custom-call | flops 1000000000 | bytes 1000000 | tf_op jit(solution)/shard_map/input_back/pallas_call | solution.py:644
  654.6 10.1 %collective-permute-done.34 = bf16[24,9472]{1,0:T(8,128)(2,1)S(1)} collective-permute-done((bf16[24,9472]{1,0:T(8,128)(2,1)S(1)}, bf16[24,9472]{1,0:T(8,128)(2,1)S(1)}, u32[]{:S(2)}, u32[]{:S(2)}) %collective-permute-start.34) | collective-permute-done | bytes 454688 | tf_op jit(solution)/shard_map/ppermute | solution.py:680
  683.4 8.7 %collective-permute-start.30 = (bf16[24,2432]{1,0:T(8,128)(2,1)S(1)}, bf16[24,2432]{1,0:T(8,128)(2,1)S(1)}, u32[]{:S(2)}, u32[]{:S(2)}) collective-permute-start(bf16[24,2432]{1,0:T(8,128)(2,1)S(1)} %get-tuple-element.326), channel_id=1, source_target_pairs={{0,8},{1,9},{2,10},{3,11},{4,12},{5,13},{6,14},{7,15},{8,0},{9,1},... | collective-permute-start | bytes 350216 | tf_op jit(solution)/shard_map/ppermute | solution.py:680
  (392 shorter events, 274.9 us)
Async XLA Ops:
  7.2 152.6 %all-gather.3.cloned.1.call-start = ((), (), s32[]{:S(2)}) async-start(), calls=%async_computation.1 | async-start | bytes 10948608 | tf_op jit(solution)/shard_map/all_gather | solution.py:665
  60.2 233.6 %all-gather.5.cloned.1.call-start = ((), (), s32[]{:S(2)}) async-start(), calls=%async_computation.2 | async-start | bytes 9732096 | tf_op jit(solution)/shard_map/all_gather | solution.py:665
  68.3 42.4 %collective-permute-start.7 = (bf16[512,768]{1,0:T(8,128)(2,1)}, bf16[512,768]{1,0:T(8,128)(2,1)}, u32[]{:S(2)}, u32[]{:S(2)}) collective-permute-start(bf16[512,768]{1,0:T(8,128)(2,1)} %get-tuple-element.370), channel_id=1, source_target_pairs={{0,4},{4,8},{8,12},{12,16},{16,20},{20,24},{24,28},{1,5},{5,9},{9,... | collective-permute-start | bytes 2359304 | tf_op jit(solution)/shard_map/ppermute | solution.py:659
  72.7 45.3 %collective-permute-start.8 = (bf16[512,768]{1,0:T(8,128)(2,1)}, bf16[512,768]{1,0:T(8,128)(2,1)}, u32[]{:S(2)}, u32[]{:S(2)}) collective-permute-start(bf16[512,768]{1,0:T(8,128)(2,1)} %get-tuple-element.369), channel_id=1, source_target_pairs={{4,0},{8,4},{12,8},{16,12},{20,16},{24,20},{28,24},{5,1},{9,5},{13... | collective-permute-start | bytes 2359304 | tf_op jit(solution)/shard_map/ppermute | solution.py:660
  110.8 42.4 %collective-permute-start.9 = (bf16[24,3200]{1,0:T(8,128)(2,1)}, bf16[24,3200]{1,0:T(8,128)(2,1)}, u32[]{:S(2)}, u32[]{:S(2)}) collective-permute-start(bf16[24,3200]{1,0:T(8,128)(2,1)} %constant_dynamic-update-slice_fusion.1), channel_id=1, source_target_pairs={{0,8},{1,9},{2,10},{3,11},{4,12},{5,13},{6,14},{7,15},{8,0},{9,1},... | collective-permute-start | bytes 460808 | tf_op jit(solution)/shard_map/ppermute | solution.py:680
  112.5 41.7 %collective-permute-start.10 = (bf16[24,3200]{1,0:T(8,128)(2,1)}, bf16[24,3200]{1,0:T(8,128)(2,1)}, u32[]{:S(2)}, u32[]{:S(2)}) collective-permute-start(bf16[24,3200]{1,0:T(8,128)(2,1)} %constant_dynamic-update-slice_fusion.1), channel_id=1, source_target_pairs={{0,16},{1,17},{2,18},{3,19},{4,20},{5,21},{6,22},{7,23},{8,24},{9,... | collective-permute-start | bytes 460808 | tf_op jit(solution)/shard_map/ppermute | solution.py:680
  113.4 41.7 %collective-permute-start.11 = (bf16[24,3200]{1,0:T(8,128)(2,1)}, bf16[24,3200]{1,0:T(8,128)(2,1)}, u32[]{:S(2)}, u32[]{:S(2)}) collective-permute-start(bf16[24,3200]{1,0:T(8,128)(2,1)} %constant_dynamic-update-slice_fusion.1), channel_id=1, source_target_pairs={{0,24},{1,25},{2,26},{3,27},{4,28},{5,29},{6,30},{7,31},{8,16},{9,... | collective-permute-start | bytes 460808 | tf_op jit(solution)/shard_map/ppermute | solution.py:680
  160.7 449.2 %reduce-scatter.4.cloned.1.call-start = ((), (), s32[]{:S(2)}) async-start(), calls=%async_computation.3 | async-start | bytes 11151360
  163.9 34.6 %collective-permute-start.12 = (bf16[4,24,3200]{2,1,0:T(8,128)(2,1)S(1)}, bf16[4,24,3200]{2,1,0:T(8,128)(2,1)S(1)}, u32[]{:S(2)}, u32[]{:S(2)}) collective-permute-start(bf16[4,24,3200]{2,1,0:T(8,128)(2,1)S(1)} %bitcast_dynamic-update-slice_fusion.12), channel_id=1, source_target_pairs={{0,2},{1,3},{2,0},{3,1},{4,6},{5,7},{6,4},{7,5},{8,10},{9,11},{10,... | collective-permute-start | bytes 1843208 | tf_op jit(solution)/shard_map/ppermute | solution.py:680
  165.4 34.0 %collective-permute-start.13 = (bf16[4,24,3200]{2,1,0:T(8,128)(2,1)S(1)}, bf16[4,24,3200]{2,1,0:T(8,128)(2,1)S(1)}, u32[]{:S(2)}, u32[]{:S(2)}) collective-permute-start(bf16[4,24,3200]{2,1,0:T(8,128)(2,1)S(1)} %bitcast_dynamic-update-slice_fusion.12), channel_id=1, source_target_pairs={{0,4},{1,5},{2,6},{3,7},{4,0},{5,1},{6,2},{7,3},{8,12},{9,13},{10,... | collective-permute-start | bytes 1843208 | tf_op jit(solution)/shard_map/ppermute | solution.py:680
  167.7 32.6 %collective-permute-start.14 = (bf16[4,24,3200]{2,1,0:T(8,128)(2,1)S(1)}, bf16[4,24,3200]{2,1,0:T(8,128)(2,1)S(1)}, u32[]{:S(2)}, u32[]{:S(2)}) collective-permute-start(bf16[4,24,3200]{2,1,0:T(8,128)(2,1)S(1)} %bitcast_dynamic-update-slice_fusion.12), channel_id=1, source_target_pairs={{0,6},{1,7},{2,4},{3,5},{4,2},{5,3},{6,0},{7,1},{8,14},{9,15},{10,... | collective-permute-start | bytes 1843208 | tf_op jit(solution)/shard_map/ppermute | solution.py:680
  202.4 52.4 %collective-permute-start.16 = (bf16[512,768]{1,0:T(8,128)(2,1)}, bf16[512,768]{1,0:T(8,128)(2,1)S(1)}, u32[]{:S(2)}, u32[]{:S(2)}) collective-permute-start(bf16[512,768]{1,0:T(8,128)(2,1)} %get-tuple-element.368), channel_id=1, source_target_pairs={{0,4},{4,8},{8,12},{12,16},{16,20},{20,24},{24,28},{1,5},{5,9},{9,... | collective-permute-start | bytes 2359304 | tf_op jit(solution)/shard_map/ppermute | solution.py:659
  206.5 55.0 %collective-permute-start.17 = (bf16[512,768]{1,0:T(8,128)(2,1)}, bf16[512,768]{1,0:T(8,128)(2,1)}, u32[]{:S(2)}, u32[]{:S(2)}) collective-permute-start(bf16[512,768]{1,0:T(8,128)(2,1)} %get-tuple-element.367), channel_id=1, source_target_pairs={{4,0},{8,4},{12,8},{16,12},{20,16},{24,20},{28,24},{5,1},{9,5},{13... | collective-permute-start | bytes 2359304 | tf_op jit(solution)/shard_map/ppermute | solution.py:660
  422.4 43.2 %collective-permute-start.18 = (bf16[512,768]{1,0:T(8,128)(2,1)}, bf16[512,768]{1,0:T(8,128)(2,1)}, u32[]{:S(2)}, u32[]{:S(2)}) collective-permute-start(bf16[512,768]{1,0:T(8,128)(2,1)} %get-tuple-element.366), channel_id=1, source_target_pairs={{0,4},{4,8},{8,12},{12,16},{16,20},{20,24},{24,28},{1,5},{5,9},{9,... | collective-permute-start | bytes 2359304 | tf_op jit(solution)/shard_map/ppermute | solution.py:659
  433.9 33.2 %collective-permute-start.19 = (bf16[512,768]{1,0:T(8,128)(2,1)}, bf16[512,768]{1,0:T(8,128)(2,1)S(1)}, u32[]{:S(2)}, u32[]{:S(2)}) collective-permute-start(bf16[512,768]{1,0:T(8,128)(2,1)} %get-tuple-element.365), channel_id=1, source_target_pairs={{4,0},{8,4},{12,8},{16,12},{20,16},{24,20},{28,24},{5,1},{9,5},{13... | collective-permute-start | bytes 2359304 | tf_op jit(solution)/shard_map/ppermute | solution.py:660
  540.4 70.6 %collective-permute-start.21 = (bf16[4,24,9472]{2,1,0:T(8,128)(2,1)}, bf16[4,24,9472]{2,1,0:T(8,128)(2,1)S(1)}, u32[]{:S(2)}, u32[]{:S(2)}) collective-permute-start(bf16[4,24,9472]{2,1,0:T(8,128)(2,1)} %get-tuple-element.309), channel_id=1, source_target_pairs={{0,2},{1,3},{2,0},{3,1},{4,6},{5,7},{6,4},{7,5},{8,10},{9,11},{10,... | collective-permute-start | bytes 5455880 | tf_op jit(solution)/shard_map/ppermute | solution.py:680
  540.4 86.6 %collective-permute-start.22 = (bf16[4,24,9472]{2,1,0:T(8,128)(2,1)}, bf16[4,24,9472]{2,1,0:T(8,128)(2,1)}, u32[]{:S(2)}, u32[]{:S(2)}) collective-permute-start(bf16[4,24,9472]{2,1,0:T(8,128)(2,1)} %get-tuple-element.310), channel_id=1, source_target_pairs={{0,4},{1,5},{2,6},{3,7},{4,0},{5,1},{6,2},{7,3},{8,12},{9,13},{10,... | collective-permute-start | bytes 5455880 | tf_op jit(solution)/shard_map/ppermute | solution.py:680
  547.8 79.2 %collective-permute-start.23 = (bf16[4,24,9472]{2,1,0:T(8,128)(2,1)}, bf16[4,24,9472]{2,1,0:T(8,128)(2,1)}, u32[]{:S(2)}, u32[]{:S(2)}) collective-permute-start(bf16[4,24,9472]{2,1,0:T(8,128)(2,1)} %get-tuple-element.311), channel_id=1, source_target_pairs={{0,6},{1,7},{2,4},{3,5},{4,2},{5,3},{6,0},{7,1},{8,14},{9,15},{10,... | collective-permute-start | bytes 5455880 | tf_op jit(solution)/shard_map/ppermute | solution.py:680
  609.9 37.3 %collective-permute-start.24 = (bf16[4,4,24,2432]{3,2,1,0:T(8,128)(2,1)}, bf16[4,4,24,2432]{3,2,1,0:T(8,128)(2,1)}, u32[]{:S(2)}, u32[]{:S(2)}) collective-permute-start(bf16[4,4,24,2432]{3,2,1,0:T(8,128)(2,1)} %get-tuple-element.317), channel_id=1, source_target_pairs={{0,1},{1,0},{2,3},{3,2},{4,5},{5,4},{6,7},{7,6},{8,9},{9,8},{10,11... | collective-permute-start | bytes 5603336 | tf_op jit(solution)/shard_map/ppermute | solution.py:680
  630.9 33.8 %collective-permute-start.34 = (bf16[24,9472]{1,0:T(8,128)(2,1)S(1)}, bf16[24,9472]{1,0:T(8,128)(2,1)S(1)}, u32[]{:S(2)}, u32[]{:S(2)}) collective-permute-start(bf16[24,9472]{1,0:T(8,128)(2,1)S(1)} %get-tuple-element.330), channel_id=1, source_target_pairs={{0,16},{1,17},{2,18},{3,19},{4,20},{5,21},{6,22},{7,23},{8,24},{9,... | collective-permute-start | bytes 1363976 | tf_op jit(solution)/shard_map/ppermute | solution.py:680
  633.7 35.2 %collective-permute-start.35 = (bf16[24,9472]{1,0:T(8,128)(2,1)S(1)}, bf16[24,9472]{1,0:T(8,128)(2,1)S(1)}, u32[]{:S(2)}, u32[]{:S(2)}) collective-permute-start(bf16[24,9472]{1,0:T(8,128)(2,1)S(1)} %get-tuple-element.331), channel_id=1, source_target_pairs={{0,24},{1,25},{2,26},{3,27},{4,28},{5,29},{6,30},{7,31},{8,16},{9,... | collective-permute-start | bytes 1363976 | tf_op jit(solution)/shard_map/ppermute | solution.py:680
  649.8 31.8 %collective-permute-start.25 = (bf16[4,24,2432]{2,1,0:T(8,128)(2,1)}, bf16[4,24,2432]{2,1,0:T(8,128)(2,1)}, u32[]{:S(2)}, u32[]{:S(2)}) collective-permute-start(bf16[4,24,2432]{2,1,0:T(8,128)(2,1)} %get-tuple-element.321), channel_id=1, source_target_pairs={{0,2},{1,3},{2,0},{3,1},{4,6},{5,7},{6,4},{7,5},{8,10},{9,11},{10,... | collective-permute-start | bytes 1400840 | tf_op jit(solution)/shard_map/ppermute | solution.py:680
  664.7 40.4 %collective-permute-start.28 = (bf16[512,768]{1,0:T(8,128)(2,1)}, bf16[512,768]{1,0:T(8,128)(2,1)}, u32[]{:S(2)}, u32[]{:S(2)}) collective-permute-start(bf16[512,768]{1,0:T(8,128)(2,1)} %get-tuple-element.364), channel_id=1, source_target_pairs={{0,4},{4,8},{8,12},{12,16},{16,20},{20,24},{24,28},{1,5},{5,9},{9,... | collective-permute-start | bytes 2359304 | tf_op jit(solution)/shard_map/ppermute | solution.py:659
  668.9 37.9 %collective-permute-start.29 = (bf16[512,768]{1,0:T(8,128)(2,1)}, bf16[512,768]{1,0:T(8,128)(2,1)}, u32[]{:S(2)}, u32[]{:S(2)}) collective-permute-start(bf16[512,768]{1,0:T(8,128)(2,1)} %get-tuple-element.363), channel_id=1, source_target_pairs={{4,0},{8,4},{12,8},{16,12},{20,16},{24,20},{28,24},{5,1},{9,5},{13... | collective-permute-start | bytes 2359304 | tf_op jit(solution)/shard_map/ppermute | solution.py:660
  (100 other events, 1273.4 us)
Sparse Core Ops, SparseCore 0:
  60.3 99.4 all-gather.2
  162.8 112.1 all-gather.4
  365.9 166.0 reduce-scatter.3
